TPU v7x, 256 devices: a whole 4x4x8 slice. The times are simulated.
256 devices in a mesh: rows: 64 (over z, y, core), cols: 4 (over x).
Axes of the slice: x: 4, y: 4, z: 8, core: 2. Of those that a mesh axis runs over, the one named last changes fastest.
Arguments:
- stiffness: bfloat16 [1024, 16, 192, 192], P('rows', 'cols'), may hold values from -0.4375 to 0.4375
- neighbors: int32 [1024, 16], P('rows', 'cols'), may hold values from 0 to 1023, as said below
- live_counts: int32 [1024], P('rows'), may hold values from 8 to 16, as said below
- prolong: bfloat16 [1024, 192, 192], P('rows', 'cols'), may hold values from -0.59765625 to 0.59765625
- prolong_aggs: int32 [1024, 32], replicated, may hold values from 0 to 1023, as said below
Outputs:
- coarse_rows: float32 [6144, 672], P('rows', 'cols')
Inputs may be any that keep to these rules, and one draw needn't show every extreme that they name: `neighbors`: each slot's column lies within 16 blocks of its row block; on every index of rows some slot reaches the first block of the index below and some the last block of the index above, clipped to the slab. `live_counts`: the first row block of every index of rows has all 16 slots live. `prolong_aggs`: the 32 aggregates of a row block are distinct, include the row block itself, and lie in the blocks of its own index of rows and of the indices just below and above.
All inputs are finite; a program needn't handle non-finite values.
Results may differ from a plain program's by a relative error of at most 0.0029.
Values may be sent and summed in bfloat16 or wider, within the bound.
No kernel may reach another device: no remote copies, remote signals or barrier semaphores. Data moves between devices by JAX's collectives and lax.ppermute only.
A program may use at most 64 MiB of HBM per device.

v0:
```python
import jax
import jax.numpy as jnp
from jax import lax
from jax.sharding import PartitionSpec as P

MODES = 6


def from_behind(x, axis, by):
    length = lax.axis_size(axis)
    pairs = [(i, i + by) for i in range(length) if 0 <= i + by < length]
    return lax.ppermute(x, axis, pairs)


def place_rows(piece, before, blocks):
    widened = jnp.pad(piece, ((0, 0), (0, 0), (0, 0), (before, 2 * blocks - before)))
    return widened.reshape(blocks * MODES, MODES * 7 * blocks)


def on_device(stiffness, neighbors, live_counts, prolong, prolong_aggs):
    row_pos = lax.axis_index("rows")
    col_pos = lax.axis_index("cols")
    blocks = stiffness.shape[0]
    slots = stiffness.shape[1]
    dofs = stiffness.shape[2]
    groups = prolong_aggs.shape[1]
    reach = 5 * blocks
    full = lax.all_gather(prolong, "cols", axis=1, tiled=True)
    below = from_behind(full, "rows", 1)
    above = from_behind(full, "rows", -1)
    window = jnp.concatenate([below, full, above], axis=0)
    coarse = window.shape[1]
    own_blocks = window[blocks : 2 * blocks]
    first_block = (row_pos - 1) * blocks
    positions = (neighbors - first_block).reshape(-1)
    picked = jnp.take(window, positions, axis=0).reshape(blocks, slots, coarse, dofs)
    image = jnp.einsum("ikbf,ikcf->ikbc", stiffness, picked, preferred_element_type=jnp.float32)
    image = image.astype(jnp.bfloat16)
    padded_table = jnp.pad(prolong_aggs, ((blocks, blocks), (0, 0)))
    window_table = lax.dynamic_slice_in_dim(padded_table, row_pos * blocks, 3 * blocks, 0)
    own_table = window_table[blocks : 2 * blocks]
    far_table = jnp.take(window_table, positions, axis=0).reshape(blocks, slots, groups)
    column_pos = far_table - (row_pos - 2) * blocks
    slot_global = col_pos * slots + jnp.arange(slots, dtype=jnp.int32)
    live = slot_global[None, :] < live_counts[:, None]
    targets = jnp.arange(reach, dtype=jnp.int32)
    placement = ((column_pos[:, :, :, None] == targets) & live[:, :, None, None]).astype(
        jnp.bfloat16
    )
    spread = image.reshape(blocks, slots, dofs, groups, MODES)
    assembled = jnp.einsum(
        "ikfam,ikaw->ifmw", spread, placement, preferred_element_type=jnp.float32
    )
    projected = jnp.einsum(
        "icf,ifx->icx",
        own_blocks.astype(jnp.float32),
        assembled.reshape(blocks, dofs, MODES * reach),
        precision=lax.Precision.HIGHEST,
    )
    row_ids = (own_table - first_block).reshape(-1)
    summed_rows = jax.ops.segment_sum(
        projected.reshape(blocks * groups, MODES, MODES * reach), row_ids, num_segments=3 * blocks
    )
    window_sum = summed_rows.reshape(3 * blocks, MODES, MODES, reach)
    lower = place_rows(window_sum[:blocks], 2 * blocks, blocks)
    middle = place_rows(window_sum[blocks : 2 * blocks], blocks, blocks)
    upper = place_rows(window_sum[2 * blocks :], 0, blocks)
    from_above = from_behind(lower, "rows", -1)
    from_below = from_behind(upper, "rows", 1)
    return lax.psum_scatter(
        middle + from_above + from_below, "cols", scatter_dimension=1, tiled=True
    )


def solution(mesh):
    in_specs = (
        P("rows", "cols", None, None),
        P("rows", "cols"),
        P("rows"),
        P("rows", "cols", None),
        P(),
    )
    out_specs = P("rows", "cols")
    return jax.shard_map(
        on_device, mesh=mesh, in_specs=in_specs, out_specs=out_specs, check_vma=False
    )
```

profile of v0, /device:TPU:134, one launch (start us, length us, event | category | flops | bytes accessed | tf_op | source)
XLA Modules:
  0.0 229.3 jit_solution(7401663898812715538)
XLA Ops:
  6.5 0.7 all-gather.2.cloned.1.call-update
  7.3 31.3 %all-gather.2.cloned.1.call-done = bf16[16,192,192]{2,1,0:T(8,128)(2,1)} async-done(((bf16[16,48,192]{2,1,0:T(8,128)(2,1)}), bf16[16,192,192]{2,1,0:T(8,128)(2,1)}) %all-gather.2.cloned.1.call-update) | async-done | bytes 1179664 | tf_op jit(solution)/shard_map/all_gather | solution.py:28
  38.6 1.9 collective-permute-start
  40.6 7.0 %collective-permute-start.1 = (bf16[16,192,192]{2,1,0:T(8,128)(2,1)}, bf16[16,192,192]{2,1,0:T(8,128)(2,1)}, u32[]{:S(2)}, u32[]{:S(2)}) collective-permute-start(bf16[16,192,192]{2,1,0:T(8,128)(2,1)} %all-gather.2.cloned.1.call-done), channel_id=1, source_target_pairs={{4,0},{8,4},{12,8},{16,12},{20,16},{24,20},{28,24},{32,28},{36,32}... | collective-permute-start | bytes 3538952 | tf_op jit(solution)/shard_map/ppermute | solution.py:12
  48.2 1.1 copy.34
  50.3 0.7 broadcast_compare_fusion
  51.2 12.7 %collective-permute-done = bf16[16,192,192]{2,1,0:T(8,128)(2,1)S(1)} collective-permute-done((bf16[16,192,192]{2,1,0:T(8,128)(2,1)}, bf16[16,192,192]{2,1,0:T(8,128)(2,1)S(1)}, u32[]{:S(2)}, u32[]{:S(2)}) %collective-permute-start) | collective-permute-done | bytes 1179680 | tf_op jit(solution)/shard_map/ppermute | solution.py:12
  63.9 1.9 collective-permute-done.1
  65.8 4.1 %pad_maximum_fusion = bf16[48,192,192]{2,1,0:T(8,128)(2,1)} fusion(bf16[16,192,192]{2,1,0:T(8,128)(2,1)} %collective-permute-done.1, bf16[16,192,192]{2,1,0:T(8,128)(2,1)} %all-gather.2.cloned.1.call-done, bf16[16,192,192]{2,1,0:T(8,128)(2,1)S(1)} %collective-permute-done), kind=kLoop, calls=%fused_computation.9 | loop fusion | flops 3538944 | bytes 7077888 | tf_op jit(solution)/shard_map/concatenate | solution.py:31
  69.8 6.0 %gather_fusion = bf16[64,192,192]{2,1,0:T(8,128)(2,1)} fusion(bf16[48,192,192]{2,1,0:T(8,128)(2,1)} %pad_maximum_fusion, s32[1024]{0:T(1024)S(1)} %pad_clamp_fusion), kind=kCustom, calls=%fused_computation | custom fusion | bytes 9437440 | tf_op jit(solution)/shard_map/jit(_take)/gather | solution.py:36
  75.8 8.1 %convert_bitcast_fusion = bf16[16,4,192,192]{2,3,1,0:T(8,128)(2,1)S(1)} fusion(bf16[16,4,192,192]{3,2,1,0:T(8,128)(2,1)} %param.5, bf16[16,4,192,192]{3,2,1,0:T(8,128)(2,1)} %bitcast.26, pred[16,4]{1,0:T(8,128)(4,1)S(1)} %copy.35), kind=kOutput, calls=%fused_computation.5 | convolution fusion | flops 910688256 | bytes 14155840 | tf_op jit(solution)/shard_map/ikbf,ikcf->ikbc/dot_general | solution.py:37
  83.9 3.7 %copy.37 = bf16[16,4,192,192]{2,0,3,1:T(8,128)(2,1)S(1)} copy(bf16[16,4,192,192]{2,3,1,0:T(8,128)(2,1)S(1)} %convert_bitcast_fusion) | data formatting | bytes 9437184 | tf_op jit(solution)/shard_map/convert_element_type | solution.py:38
  87.6 8.7 %fusion = f32[16,192,6,80,1]{1,3,4,2,0:T(8,128)S(1)} fusion(bf16[16,4,192,32,6]{2,0,4,3,1:T(8,128)(2,1)S(1)} %bitcast.25, s32[16,4,32]{2,1,0:T(4,128)S(1)} %select_subtract_fusion, pred[16,4]{1,0:T(8,128)(4,1)S(1)} %broadcast_compare_fusion), kind=kOutput, calls=%fused_computation.3 | convolution fusion | flops 377815040 | bytes 10625088 | tf_op jit(solution)/shard_map/ikfam,ikaw->ifmw/dot_general | solution.py:51
  96.3 6.5 %convolution_bitcast_fusion = f32[16,192,480]{2,1,0:T(8,128)} fusion(f32[16,192,480]{1,2,0:T(8,128)S(1)} %bitcast.24, bf16[16,192,192]{2,1,0:T(8,128)(2,1)S(1)} %copy-done), kind=kOutput, calls=%fused_computation.11 | convolution fusion | flops 3397386240 | bytes 12976128 | tf_op jit(solution)/shard_map/icf,ifx->icx/dot_general | solution.py:54
  102.9 8.3 %reshape.134 = f32[512,6,480]{2,1,0:T(8,128)} reshape(f32[16,192,480]{2,1,0:T(8,128)} %convolution_bitcast_fusion) | data formatting | bytes 11796480 | tf_op jit(solution)/shard_map/reshape | solution.py:62
  111.3 44.5 %scatter_fusion = f32[48,6,480]{2,1,0:T(8,128)S(1)} fusion(f32[48,6,480]{2,1,0:T(8,128)S(1)} %broadcast_in_dim.28, s32[512]{0:T(512)S(1)} %reshape.132, f32[512,6,480]{2,1,0:T(8,128)} %reshape.134), kind=kCustom, calls=%fused_computation.2 | custom fusion | flops 1474560 | bytes 17696768 | tf_op jit(solution)/shard_map/scatter-add | solution.py:61
  156.3 7.1 %collective-permute-start.2 = (f32[96,672]{1,0:T(8,128)S(1)}, f32[96,672]{1,0:T(8,128)S(1)}, u32[]{:S(2)}, u32[]{:S(2)}) collective-permute-start(f32[96,672]{1,0:T(8,128)S(1)} %reshape.112), channel_id=1, source_target_pairs={{4,0},{8,4},{12,8},{16,12},{20,16},{24,20},{28,24},{32,28},{36,32}... | collective-permute-start | bytes 774152 | tf_op jit(solution)/shard_map/ppermute | solution.py:12
  163.8 1.9 collective-permute-start.3
  166.2 1.5 collective-permute-done.2
  167.7 7.5 %collective-permute-done.3 = f32[96,672]{1,0:T(8,128)S(1)} collective-permute-done((f32[96,672]{1,0:T(8,128)S(1)}, f32[96,672]{1,0:T(8,128)S(1)}, u32[]{:S(2)}, u32[]{:S(2)}) %collective-permute-start.3) | collective-permute-done | bytes 258080 | tf_op jit(solution)/shard_map/ppermute | solution.py:12
  175.2 0.8 add_add_fusion
  177.2 43.5 %all-reduce.7.cloned.1.call-done = f32[96,672]{1,0:T(8,128)} async-done(((f32[96,672]{1,0:T(8,128)}), f32[96,672]{1,0:T(8,128)}) %all-reduce.7.cloned.1.call-update) | async-done | bytes 258064
  220.7 1.0 constant_dynamic-slice_fusion
  221.7 0.7 copy.47
  (31 shorter events, 3.8 us)
Async XLA Ops:
  6.5 32.1 %all-gather.2.cloned.1.call-start = ((), (), s32[]{:S(2)}) async-start(), calls=%async_computation | async-start | bytes 1966080 | tf_op jit(solution)/shard_map/all_gather | solution.py:28
  7.3 213.5 %all-reduce.7.cloned.1.call-start = ((), (), s32[]{:S(2)}) async-start(), calls=%async_computation.1 | async-start | bytes 589824
  38.6 25.3 %collective-permute-start = (bf16[16,192,192]{2,1,0:T(8,128)(2,1)}, bf16[16,192,192]{2,1,0:T(8,128)(2,1)S(1)}, u32[]{:S(2)}, u32[]{:S(2)}) collective-permute-start(bf16[16,192,192]{2,1,0:T(8,128)(2,1)} %all-gather.2.cloned.1.call-done), channel_id=1, source_target_pairs={{0,4},{4,8},{8,12},{12,16},{16,20},{20,24},{24,28},{28,32},{32,36}... | collective-permute-start | bytes 3538952 | tf_op jit(solution)/shard_map/ppermute | solution.py:12
  40.6 25.2 %collective-permute-start.1 = (bf16[16,192,192]{2,1,0:T(8,128)(2,1)}, bf16[16,192,192]{2,1,0:T(8,128)(2,1)}, u32[]{:S(2)}, u32[]{:S(2)}) collective-permute-start(bf16[16,192,192]{2,1,0:T(8,128)(2,1)} %all-gather.2.cloned.1.call-done), channel_id=1, source_target_pairs={{4,0},{8,4},{12,8},{16,12},{20,16},{24,20},{28,24},{32,28},{36,32}... | collective-permute-start | bytes 3538952 | tf_op jit(solution)/shard_map/ppermute | solution.py:12
  87.6 8.7 %copy-start = (bf16[16,192,192]{2,1,0:T(8,128)(2,1)S(1)}, bf16[16,192,192]{2,1,0:T(8,128)(2,1)}, u32[]{:S(2)}) copy-start(bf16[16,192,192]{2,1,0:T(8,128)(2,1)} %all-gather.2.cloned.1.call-done) | copy-start | bytes 3538948
  155.8 20.2 %copy-start.1 = (u32[256]{0:T(256)S(1)}, u32[256]{0:T(256)}, u32[]{:S(2)}) copy-start(u32[256]{0:T(256)} %constant.68) | copy-start | bytes 3076
  156.3 11.4 %collective-permute-start.2 = (f32[96,672]{1,0:T(8,128)S(1)}, f32[96,672]{1,0:T(8,128)S(1)}, u32[]{:S(2)}, u32[]{:S(2)}) collective-permute-start(f32[96,672]{1,0:T(8,128)S(1)} %reshape.112), channel_id=1, source_target_pairs={{4,0},{8,4},{12,8},{16,12},{20,16},{24,20},{28,24},{32,28},{36,32}... | collective-permute-start | bytes 774152 | tf_op jit(solution)/shard_map/ppermute | solution.py:12
  163.8 11.4 %collective-permute-start.3 = (f32[96,672]{1,0:T(8,128)S(1)}, f32[96,672]{1,0:T(8,128)S(1)}, u32[]{:S(2)}, u32[]{:S(2)}) collective-permute-start(f32[96,672]{1,0:T(8,128)S(1)} %reshape.113), channel_id=1, source_target_pairs={{0,4},{4,8},{8,12},{12,16},{16,20},{20,24},{24,28},{28,32},{32,36}... | collective-permute-start | bytes 774152 | tf_op jit(solution)/shard_map/ppermute | solution.py:12
Sparse Core Ops, SparseCore 0:
  9.2 29.4 all-gather.1
  176.1 44.5 all-reduce.6
where the time goes:
time: 233 us; the launch traced here: 229 us
  waiting for transfers between devices  99.1 us (43%)
  other arithmetic  50.8 us (22%)
  local copies, waits for them, and re-layouts  23.8 us (10%)
  matrix products  23.4 us (10%)
  starting transfers between devices  18 us (8%)
  between operations  14.3 us (6%)
    scatter-add x1, other arithmetic, on_device(): jax.ops.segment_sum(projected.reshape(blocks * groups, MODES, MODES * rea...  44.5 us
    unnamed x3, waiting for transfers between devices  44.2 us
    all_gather x1, waiting for transfers between devices, on_device(): full = lax.all_gather(prolong, 'cols', axis=1, tiled=True)  31.3 us
    ppermute x4, waiting for transfers between devices, from_behind(): return lax.ppermute(x, axis, pairs)  23.5 us
    ppermute x4, starting transfers between devices, from_behind(): return lax.ppermute(x, axis, pairs)  17.9 us
    dot_general x1, matrix products, on_device(): jnp.einsum('ikfam,ikaw->ifmw', spread, placement, preferred_element_type=...  8.71 us
    reshape x1, local copies, waits for them, and re-layouts, on_device(): projected.reshape(blocks * groups, MODES, MODES * reach)  8.32 us
    dot_general x1, matrix products, on_device(): jnp.einsum('ikbf,ikcf->ikbc', stiffness, picked, preferred_element_type=j...  8.1 us
  transfers between devices with their start and end apart: 6, of which 6 were waited for; matrix products, arithmetic and copies ran while one was open for 2% of the time, Pallas kernels for 0%

commit v1 on v0

v1 whole, which is shorter than its diff:
```python
import jax
import jax.numpy as jnp
from jax import lax
from jax.experimental import pallas as pl
from jax.experimental.pallas import tpu as pltpu
from jax.sharding import PartitionSpec as P

MODES = 6
LANES = 128
BF = jnp.bfloat16
F32 = jnp.float32


def from_behind(x, axis, by):
    length = lax.axis_size(axis)
    pairs = [(i, i + by) for i in range(length) if 0 <= i + by < length]
    return lax.ppermute(x, axis, pairs)


def around(x, axis, by):
    length = lax.axis_size(axis)
    return lax.ppermute(x, axis, [(i, (i + by) % length) for i in range(length)])


def pack_kernel(q_ref, out_ref):
    blocks, rows, _ = q_ref.shape
    half = blocks // 2
    groups = rows // MODES
    r = lax.broadcasted_iota(jnp.int32, (rows, rows), 0)
    c = lax.broadcasted_iota(jnp.int32, (rows, rows), 1)
    perm = jnp.where((r % groups) * MODES + r // groups == c, 1.0, 0.0).astype(BF)
    for j in range(half):
        a = jnp.dot(perm, q_ref[j], preferred_element_type=F32)
        b = jnp.dot(perm, q_ref[j + half], preferred_element_type=F32)
        out_ref[j * rows : (j + 1) * rows, :] = a[:, :LANES].astype(BF)
        out_ref[(j + half) * rows : (j + half + 1) * rows, :] = b[:, :LANES].astype(BF)
        mixed = jnp.concatenate([a[:, LANES:], b[:, LANES:]], axis=1)
        out_ref[(blocks + j) * rows : (blocks + j + 1) * rows, :] = mixed.astype(BF)


def main_kernel(
    pos_ref, aggr_ref, aggl_ref, s_hbm, w00, w01, w02, w03, below0, below, above0, above,
    low_ref, mid_ref, up_ref, wbuf, sbuf, acc, wsem, ssem
):
    blocks, slots, dofs, _ = sbuf.shape
    half = blocks // 2
    quarter = w00.shape[0]
    rows = quarter // (blocks + half)
    groups = rows // MODES
    parts = 4
    reach = 5 * blocks

    def window_copies():
        copies = []

        def add(src, place, count):
            copies.append(
                pltpu.make_async_copy(
                    src, wbuf.at[pl.ds(place * quarter, count * quarter)], wsem.at[len(copies)]
                )
            )

        add(below0, 0, 1)
        add(below, 1, 3)
        for d, own in enumerate((w00, w01, w02, w03)):
            add(own, parts + d, 1)
        add(above0, 2 * parts, 1)
        add(above, 2 * parts + 1, 3)
        return copies

    def stiff_copy(i):
        return pltpu.make_async_copy(s_hbm.at[i], sbuf.at[i], ssem.at[i])

    for cp in window_copies():
        cp.start()
    for n in range(half):
        stiff_copy(n).start()
        stiff_copy(n + half).start()
    acc[...] = jnp.zeros_like(acc)
    for cp in window_copies():
        cp.wait()

    def block_of(place, j):
        first = [
            wbuf[pl.ds(pl.multiple_of((place + d) * quarter + j * rows, 16), rows), :]
            for d in range(parts)
        ]
        jh = jnp.where(j >= half, j - half, j)
        second = [
            wbuf[pl.ds(pl.multiple_of((place + d) * quarter + (blocks + jh) * rows, 16), rows), :]
            for d in range(parts)
        ]
        return jnp.concatenate(
            [jnp.concatenate(first, axis=0), jnp.concatenate(second, axis=0)], axis=1
        )

    zeros = jnp.zeros((dofs, 2 * LANES - dofs), BF)

    def one(i, upper):
        images = []
        for k in range(slots):
            j = pos_ref[i * slots + k]
            w = j // blocks
            jl = j - w * blocks
            pj = block_of(w * parts, jl)
            s = sbuf[i, k]
            tail = s[:, LANES:]
            tail = jnp.where(
                jl < half,
                jnp.concatenate([tail, zeros], axis=1),
                jnp.concatenate([zeros, tail], axis=1),
            )
            sp = jnp.concatenate([s[:, :LANES], tail], axis=1)
            images.append(
                lax.dot_general(pj, sp, (((1,), (1,)), ((), ())), preferred_element_type=F32)
            )
        place_t = (
            lax.broadcasted_iota(jnp.int32, (reach, slots * parts * groups), 0)
            == aggr_ref[pl.ds(i, 1), :]
        )
        place_t = jnp.where(place_t, 1.0, 0.0).astype(BF)
        assembled = []
        for m in range(MODES):
            rhs = jnp.concatenate(
                [
                    img[d * rows + m * groups : d * rows + (m + 1) * groups]
                    for img in images
                    for d in range(parts)
                ],
                axis=0,
            ).astype(BF)
            assembled.append(jnp.dot(place_t, rhs, preferred_element_type=F32).astype(BF))
        assembled = jnp.concatenate(assembled, axis=0)
        hot = (
            lax.broadcasted_iota(jnp.int32, (3 * LANES, parts * rows), 0)
            == aggl_ref[pl.ds(i, 1), :]
        )
        hot = jnp.where(hot, 1.0, 0.0).astype(BF)
        left = jnp.dot(hot, block_of(parts, i), preferred_element_type=F32)
        if upper:
            left = jnp.concatenate([left[:, :LANES], left[:, dofs:]], axis=1)
        else:
            left = left[:, :dofs]
        return lax.dot_general(
            assembled, left.astype(BF), (((1,), (1,)), ((), ())), preferred_element_type=F32
        )

    def step(n, carry):
        stiff_copy(n).wait()
        stiff_copy(n + half).wait()
        acc[...] += one(n, False) + one(n + half, True)
        return carry

    lax.fori_loop(0, half, step, 0)
    width = low_ref.shape[1]
    low_ref[...] = acc[:, :width]
    mid_ref[...] = acc[:, LANES : LANES + width]
    up_ref[...] = acc[:, 2 * LANES : 2 * LANES + width]


def share_kernel(col_ref, mid_ref, above_ref, below_ref, o0, o1, o2, o3, tot):
    reach = mid_ref.shape[0] // MODES
    band = tot.shape[0] // MODES
    blocks = band // 7
    piece = o0.shape[0]
    tot[...] = jnp.zeros_like(tot)
    for m in range(MODES):
        src = slice(m * reach, (m + 1) * reach)
        tot[m * band + blocks : m * band + blocks + reach] += mid_ref[src]
        tot[m * band + 2 * blocks : m * band + 2 * blocks + reach] += above_ref[src]
        tot[m * band : m * band + reach] += below_ref[src]
    for d, o in enumerate((o0, o1, o2, o3)):
        c = col_ref[0] + d
        c = jnp.where(c >= 4, c - 4, c)
        o[...] = tot[pl.ds(pl.multiple_of(c * piece, 8), piece), :]


def final_kernel(a, b, c, d, out_ref):
    out_ref[...] = ((a[...] + b[...]) + (c[...] + d[...])).T


def on_device(stiffness, neighbors, live_counts, prolong, prolong_aggs):
    row_pos = lax.axis_index("rows")
    col_pos = lax.axis_index("cols")
    blocks, slots, dofs, _ = stiffness.shape
    rows = prolong.shape[1]
    groups = rows // MODES
    nagg = prolong_aggs.shape[1]
    parts = nagg // groups
    quarter = (blocks + blocks // 2) * rows
    vmem = pl.BlockSpec(memory_space=pltpu.VMEM)
    smem = pl.BlockSpec(memory_space=pltpu.SMEM)
    any_ = pl.BlockSpec(memory_space=pl.ANY)

    w0 = pl.pallas_call(
        pack_kernel,
        out_shape=jax.ShapeDtypeStruct((quarter, LANES), BF),
        in_specs=[vmem],
        out_specs=vmem,
    )(prolong)
    w1 = around(w0, "cols", -1)
    w3 = around(w0, "cols", 1)
    w2 = around(w0, "cols", 2)
    below0 = from_behind(w0, "rows", 1)
    above0 = from_behind(w0, "rows", -1)

    first_block = (row_pos - 1) * blocks
    pos = (neighbors - first_block).reshape(-1)
    cols_order = (col_pos + jnp.arange(parts, dtype=jnp.int32)) % parts
    rolled = jnp.take(prolong_aggs.reshape(-1, parts, groups), cols_order, axis=1)
    slot_global = col_pos * slots + jnp.arange(slots, dtype=jnp.int32)
    live = slot_global[None, :] < live_counts[:, None]
    far = jnp.take(rolled, neighbors.reshape(-1), axis=0).reshape(blocks, slots, parts * groups)
    aggr = jnp.where(live[:, :, None], far - (row_pos - 2) * blocks, -1)
    aggr = aggr.reshape(blocks, slots * nagg)
    own = lax.dynamic_slice_in_dim(rolled, row_pos * blocks, blocks, 0) - first_block
    own = (own // blocks) * LANES + (own % blocks) * MODES
    aggl = own[:, :, None, :] + jnp.arange(MODES, dtype=jnp.int32)[:, None]
    aggl = aggl.reshape(blocks, parts * rows)

    rest = jnp.concatenate([w1, w2, w3], axis=0)
    below = from_behind(rest, "rows", 1)
    above = from_behind(rest, "rows", -1)

    reach = 5 * blocks
    out = jax.ShapeDtypeStruct((MODES * reach, blocks * MODES), F32)
    low, mid, up = pl.pallas_call(
        main_kernel,
        out_shape=[out, out, out],
        in_specs=[smem, vmem, vmem] + [any_] * 9,
        out_specs=[vmem] * 3,
        scratch_shapes=[
            pltpu.VMEM((3 * parts * quarter, LANES), BF),
            pltpu.VMEM(stiffness.shape, BF),
            pltpu.VMEM((MODES * reach, 3 * LANES), F32),
            pltpu.SemaphoreType.DMA((8,)),
            pltpu.SemaphoreType.DMA((blocks,)),
        ],
        compiler_params=pltpu.CompilerParams(vmem_limit_bytes=40 * 2**20),
    )(pos, aggr, aggl, stiffness, w0, w1, w2, w3, below0, below, above0, above)
    from_above = from_behind(low, "rows", -1)
    from_below = from_behind(up, "rows", 1)
    piece = MODES * 7 * blocks // parts
    sh = jax.ShapeDtypeStruct((piece, blocks * MODES), F32)
    s0, s1, s2, s3 = pl.pallas_call(
        share_kernel,
        out_shape=[sh] * 4,
        in_specs=[smem] + [vmem] * 3,
        out_specs=[vmem] * 4,
        scratch_shapes=[pltpu.VMEM((MODES * 7 * blocks, blocks * MODES), F32)],
    )(col_pos.reshape(1), mid, from_above, from_below)
    t1 = around(s1, "cols", 1)
    t3 = around(s3, "cols", -1)
    t2 = around(s2, "cols", 2)
    return pl.pallas_call(
        final_kernel,
        out_shape=jax.ShapeDtypeStruct((blocks * MODES, piece), F32),
        in_specs=[vmem] * 4,
        out_specs=vmem,
    )(s0, t1, t2, t3)


def solution(mesh):
    in_specs = (
        P("rows", "cols", None, None),
        P("rows", "cols"),
        P("rows"),
        P("rows", "cols", None),
        P(),
    )
    out_specs = P("rows", "cols")
    return jax.shard_map(
        on_device, mesh=mesh, in_specs=in_specs, out_specs=out_specs, check_vma=False
    )
```

time: 233 us -> 95.7 us (0.41)
  the two profiles are of different devices: /device:TPU:134 before, /device:TPU:128 now
where the time goes in v1:
time: 95.7 us; the launch traced here: 95.2 us
  starting transfers between devices  34.2 us (36%)
  Pallas kernels  22.2 us (23%)
  waiting for transfers between devices  19.6 us (20%)
  local copies, waits for them, and re-layouts  17.3 us (18%)
  other arithmetic  1.74 us (2%)
    ppermute x6, starting transfers between devices, from_behind(): return lax.ppermute(x, axis, pairs)  26.7 us
    pallas_call x1, Pallas kernels, on_device(): pl.pallas_call(main_kernel, out_shape=[out, out, out], in_specs=[smem, vm...  16.4 us
    ppermute x6, waiting for transfers between devices, from_behind(): return lax.ppermute(x, axis, pairs)  12.2 us
    ppermute x6, starting transfers between devices, around(): lax.ppermute(x, axis, [(i, (i + by) % length) for i in range(length)])  7.5 us
    ppermute x6, waiting for transfers between devices, around(): lax.ppermute(x, axis, [(i, (i + by) % length) for i in range(length)])  7.33 us
    unnamed x25, local copies, waits for them, and re-layouts  7.06 us
    gather x2, local copies, waits for them, and re-layouts, on_device(): jnp.take(rolled, neighbors.reshape(-1), axis=0)  3.94 us
    select_n x1, local copies, waits for them, and re-layouts, on_device(): jnp.take(prolong_aggs.reshape(-1, parts, groups), cols_order, axis=1)  2.52 us
  transfers between devices with their start and end apart: 12, of which 7 were waited for; matrix products, arithmetic and copies ran while one was open for 13% of the time, Pallas kernels for 0%

profile of v1, /device:TPU:128, one launch (start us, length us, event | category | flops | bytes accessed | tf_op | source)
XLA Modules:
  0.0 95.2 jit_solution(17802282616326475120)
XLA Ops:
  0.0 2.1 %shard_map.55.w00 = bf16[1152,128]{1,0:T(8,128)(2,1)} custom-call(bf16[16,48,192]{2,1,0:T(8,128)(2,1)} %q_ref.1), custom_call_target="tpu_custom_call" | custom-call | tf_op jit(solution)/shard_map/pallas_call | solution.py:195
  2.1 2.8 %collective-permute-start = (bf16[1152,128]{1,0:T(8,128)(2,1)}, bf16[1152,128]{1,0:T(8,128)(2,1)S(1)}, u32[]{:S(2)}, u32[]{:S(2)}) collective-permute-start(bf16[1152,128]{1,0:T(8,128)(2,1)} %shard_map.55.w00), channel_id=1, source_target_pairs={{0,3},{1,0},{2,1},{3,2},{4,7},{5,4},{6,5},{7,6},{8,11},{9,8},{10,9... | collective-permute-start | bytes 884744 | tf_op jit(solution)/shard_map/ppermute | solution.py:22
  6.5 1.9 %collective-permute-start.3 = (bf16[1152,128]{1,0:T(8,128)(2,1)}, bf16[1152,128]{1,0:T(8,128)(2,1)S(1)}, u32[]{:S(2)}, u32[]{:S(2)}) collective-permute-start(bf16[1152,128]{1,0:T(8,128)(2,1)} %shard_map.55.w00), channel_id=1, source_target_pairs={{0,4},{4,8},{8,12},{12,16},{16,20},{20,24},{24,28},{28,32},{32,36}... | collective-permute-start | bytes 884744 | tf_op jit(solution)/shard_map/ppermute | solution.py:17
  8.4 7.0 %collective-permute-start.5 = (bf16[1152,128]{1,0:T(8,128)(2,1)}, bf16[1152,128]{1,0:T(8,128)(2,1)}, u32[]{:S(2)}, u32[]{:S(2)}) collective-permute-start(bf16[1152,128]{1,0:T(8,128)(2,1)} %shard_map.55.w00), channel_id=1, source_target_pairs={{4,0},{8,4},{12,8},{16,12},{20,16},{24,20},{28,24},{32,28},{36,32}... | collective-permute-start | bytes 884744 | tf_op jit(solution)/shard_map/ppermute | solution.py:17
  19.9 1.4 %collective-permute-done.2.w03 = bf16[1152,128]{1,0:T(8,128)(2,1)S(1)} collective-permute-done((bf16[1152,128]{1,0:T(8,128)(2,1)}, bf16[1152,128]{1,0:T(8,128)(2,1)S(1)}, u32[]{:S(2)}, u32[]{:S(2)}) %collective-permute-start.2) | collective-permute-done | bytes 294944 | tf_op jit(solution)/shard_map/ppermute | solution.py:22
  22.1 1.9 %collective-permute-start.4 = (bf16[3456,128]{1,0:T(8,128)(2,1)}, bf16[3456,128]{1,0:T(8,128)(2,1)S(1)}, u32[]{:S(2)}, u32[]{:S(2)}) collective-permute-start(bf16[3456,128]{1,0:T(8,128)(2,1)} %constant_dynamic-update-slice_fusion), channel_id=1, source_target_pairs={{0,4},{4,8},{8,12},{12,16},{16,20},{20,24},{24,28},{28,32},{32,36}... | collective-permute-start | bytes 2654216 | tf_op jit(solution)/shard_map/ppermute | solution.py:17
  24.0 7.0 %collective-permute-start.6 = (bf16[3456,128]{1,0:T(8,128)(2,1)}, bf16[3456,128]{1,0:T(8,128)(2,1)S(1)}, u32[]{:S(2)}, u32[]{:S(2)}) collective-permute-start(bf16[3456,128]{1,0:T(8,128)(2,1)} %constant_dynamic-update-slice_fusion), channel_id=1, source_target_pairs={{4,0},{8,4},{12,8},{16,12},{20,16},{24,20},{28,24},{32,28},{36,32}... | collective-permute-start | bytes 2654216 | tf_op jit(solution)/shard_map/ppermute | solution.py:17
  31.0 2.5 %copy.20 = s32[1024,4,8]{2,1,0:T(4,128)} copy(s32[1024,4,8]{0,2,1:T(8,128)} %fusion.12) | data formatting | bytes 262144 | tf_op jit(solution)/shard_map/jit(_take)/select_n | solution.py:210
  33.5 2.9 %gather_fusion.1 = s32[64,4,8]{2,1,0:T(4,128)} fusion(s32[1024,4,8]{2,1,0:T(4,128)} %copy.20, s32[1024]{0:T(1024)S(1)} %get-tuple-element.19), kind=kCustom, calls=%fused_computation.1 | custom fusion | bytes 16640 | tf_op jit(solution)/shard_map/jit(_take)/gather | solution.py:213
  36.4 1.0 %gather.12 = s32[16,128]{1,0:T(8,128)S(1)} reshape(s32[64,4,8]{2,1,0:T(4,128)} %gather_fusion.1) | data formatting | bytes 16384 | tf_op jit(solution)/shard_map/jit(_take)/gather | solution.py:213
  38.5 1.5 %collective-permute-done.4.below = bf16[3456,128]{1,0:T(8,128)(2,1)S(1)} collective-permute-done((bf16[3456,128]{1,0:T(8,128)(2,1)}, bf16[3456,128]{1,0:T(8,128)(2,1)S(1)}, u32[]{:S(2)}, u32[]{:S(2)}) %collective-permute-start.4) | collective-permute-done | bytes 884768 | tf_op jit(solution)/shard_map/ppermute | solution.py:17
  40.0 1.9 %collective-permute-done.6.above = bf16[3456,128]{1,0:T(8,128)(2,1)S(1)} collective-permute-done((bf16[3456,128]{1,0:T(8,128)(2,1)}, bf16[3456,128]{1,0:T(8,128)(2,1)S(1)}, u32[]{:S(2)}, u32[]{:S(2)}) %collective-permute-start.6) | collective-permute-done | bytes 884768 | tf_op jit(solution)/shard_map/ppermute | solution.py:17
  41.8 2.8 %copy-done.1 = bf16[16,4,192,192]{3,2,1,0:T(8,128)(2,1)S(1)} copy-done((bf16[16,4,192,192]{3,2,1,0:T(8,128)(2,1)S(1)}, bf16[16,4,192,192]{3,2,1,0:T(8,128)(2,1)}, u32[]{:S(2)}) %copy-start.1) | copy-done | bytes 4718616
  44.6 16.4 %shard_map.56 = (f32[480,96]{1,0:T(8,128)S(1)}, f32[480,96]{1,0:T(8,128)S(1)}, f32[480,96]{1,0:T(8,128)S(1)}) custom-call(s32[64]{0:T(128)S(1)} %reshape.144.pos_ref, s32[16,128]{1,0:T(8,128)S(1)} %subtract_select_fusion.aggr_ref, s32[16,192]{1,0:T(8,128)S(1)} %broadcast_add_fusion.aggl_ref, bf16[16,4,192,192]{3,2,1,0:T(8,128)(2,1)S(1)} %copy-done.1, ...), custom_call_target="tpu_custom_call" | custom-call | tf_op jit(solution)/shard_map/pallas_call | solution.py:227
  61.7 7.0 %collective-permute-start.7 = (f32[480,96]{1,0:T(8,128)S(1)}, f32[480,96]{1,0:T(8,128)S(1)}, u32[]{:S(2)}, u32[]{:S(2)}) collective-permute-start(f32[480,96]{1,0:T(8,128)S(1)} %get-tuple-element.13), channel_id=1, source_target_pairs={{4,0},{8,4},{12,8},{16,12},{20,16},{24,20},{28,24},{32,28},{36,32}... | collective-permute-start | bytes 552968 | tf_op jit(solution)/shard_map/ppermute | solution.py:17
  68.7 1.9 %collective-permute-start.8 = (f32[480,96]{1,0:T(8,128)S(1)}, f32[480,96]{1,0:T(8,128)S(1)}, u32[]{:S(2)}, u32[]{:S(2)}) collective-permute-start(f32[480,96]{1,0:T(8,128)S(1)} %get-tuple-element.14), channel_id=1, source_target_pairs={{0,4},{4,8},{8,12},{12,16},{16,20},{20,24},{24,28},{28,32},{32,36}... | collective-permute-start | bytes 552968 | tf_op jit(solution)/shard_map/ppermute | solution.py:17
  70.6 1.8 %collective-permute-done.7.above_ref = f32[480,96]{1,0:T(8,128)S(1)} collective-permute-done((f32[480,96]{1,0:T(8,128)S(1)}, f32[480,96]{1,0:T(8,128)S(1)}, u32[]{:S(2)}, u32[]{:S(2)}) %collective-permute-start.7) | collective-permute-done | bytes 184352 | tf_op jit(solution)/shard_map/ppermute | solution.py:17
  72.4 7.1 %collective-permute-done.8.below_ref = f32[480,96]{1,0:T(8,128)S(1)} collective-permute-done((f32[480,96]{1,0:T(8,128)S(1)}, f32[480,96]{1,0:T(8,128)S(1)}, u32[]{:S(2)}, u32[]{:S(2)}) %collective-permute-start.8) | collective-permute-done | bytes 184352 | tf_op jit(solution)/shard_map/ppermute | solution.py:17
  80.2 2.0 %shard_map.57 = (f32[168,96]{1,0:T(8,128)}, f32[168,96]{1,0:T(8,128)}, f32[168,96]{1,0:T(8,128)}, f32[168,96]{1,0:T(8,128)}) custom-call(s32[1]{0:T(128)} %bitcast.col_ref, f32[480,96]{1,0:T(8,128)} %copy-done.3, f32[480,96]{1,0:T(8,128)} %copy-done.4, f32[480,96]{1,0:T(8,128)} %copy-done.5), custom_call_target="tpu_custom_call" | custom-call | tf_op jit(solution)/shard_map/pallas_call | solution.py:245
  83.0 2.3 %collective-permute-start.11 = (f32[168,96]{1,0:T(8,128)}, f32[168,96]{1,0:T(8,128)S(1)}, u32[]{:S(2)}, u32[]{:S(2)}) collective-permute-start(f32[168,96]{1,0:T(8,128)} %get-tuple-element.18), channel_id=1, source_target_pairs={{0,3},{1,0},{2,1},{3,2},{4,7},{5,4},{6,5},{7,6},{8,11},{9,8},{10,9... | collective-permute-start | bytes 193544 | tf_op jit(solution)/shard_map/ppermute | solution.py:22
  85.3 3.1 %collective-permute-done.10.c = f32[168,96]{1,0:T(8,128)S(1)} collective-permute-done((f32[168,96]{1,0:T(8,128)}, f32[168,96]{1,0:T(8,128)S(1)}, u32[]{:S(2)}, u32[]{:S(2)}) %collective-permute-start.10) | collective-permute-done | bytes 64544 | tf_op jit(solution)/shard_map/ppermute | solution.py:22
  88.5 2.7 %collective-permute-done.9.b = f32[168,96]{1,0:T(8,128)S(1)} collective-permute-done((f32[168,96]{1,0:T(8,128)}, f32[168,96]{1,0:T(8,128)S(1)}, u32[]{:S(2)}, u32[]{:S(2)}) %collective-permute-start.9) | collective-permute-done | bytes 64544 | tf_op jit(solution)/shard_map/ppermute | solution.py:22
  91.8 1.7 %shard_map.58 = f32[96,168]{1,0:T(8,128)} custom-call(f32[168,96]{1,0:T(8,128)} %get-tuple-element.15.a, f32[168,96]{1,0:T(8,128)} %copy-done.8, f32[168,96]{1,0:T(8,128)} %copy-done.6, f32[168,96]{1,0:T(8,128)} %copy-done.7), custom_call_target="tpu_custom_call" | custom-call | tf_op jit(solution)/shard_map/pallas_call | solution.py:255
  93.6 1.6 %copy.22 = f32[96,168]{0,1:T(8,128)} copy(f32[96,168]{1,0:T(8,128)} %shard_map.58) | data formatting | bytes 129024 | tf_op jit(solution)/shard_map/pallas_call | solution.py:255
  (60 shorter events, 10.7 us)
Async XLA Ops:
  0.0 17.0 %copy-start = (s32[1024,32]{0,1:T(8,128)S(1)}, s32[1024,32]{0,1:T(8,128)}, u32[]{:S(2)}) copy-start(s32[1024,32]{0,1:T(8,128)} %param.9) | copy-start | bytes 393220
  2.1 16.3 %collective-permute-start = (bf16[1152,128]{1,0:T(8,128)(2,1)}, bf16[1152,128]{1,0:T(8,128)(2,1)S(1)}, u32[]{:S(2)}, u32[]{:S(2)}) collective-permute-start(bf16[1152,128]{1,0:T(8,128)(2,1)} %shard_map.55.w00), channel_id=1, source_target_pairs={{0,3},{1,0},{2,1},{3,2},{4,7},{5,4},{6,5},{7,6},{8,11},{9,8},{10,9... | collective-permute-start | bytes 884744 | tf_op jit(solution)/shard_map/ppermute | solution.py:22
  4.8 14.3 %collective-permute-start.1 = (bf16[1152,128]{1,0:T(8,128)(2,1)}, bf16[1152,128]{1,0:T(8,128)(2,1)S(1)}, u32[]{:S(2)}, u32[]{:S(2)}) collective-permute-start(bf16[1152,128]{1,0:T(8,128)(2,1)} %shard_map.55.w00), channel_id=1, source_target_pairs={{0,2},{1,3},{2,0},{3,1},{4,6},{5,7},{6,4},{7,5},{8,10},{9,11},{10,... | collective-permute-start | bytes 884744 | tf_op jit(solution)/shard_map/ppermute | solution.py:22
  5.6 15.7 %collective-permute-start.2 = (bf16[1152,128]{1,0:T(8,128)(2,1)}, bf16[1152,128]{1,0:T(8,128)(2,1)S(1)}, u32[]{:S(2)}, u32[]{:S(2)}) collective-permute-start(bf16[1152,128]{1,0:T(8,128)(2,1)} %shard_map.55.w00), channel_id=1, source_target_pairs={{0,1},{1,2},{2,3},{3,0},{4,5},{5,6},{6,7},{7,4},{8,9},{9,10},{10,1... | collective-permute-start | bytes 884744 | tf_op jit(solution)/shard_map/ppermute | solution.py:22
  6.5 32.0 %collective-permute-start.3 = (bf16[1152,128]{1,0:T(8,128)(2,1)}, bf16[1152,128]{1,0:T(8,128)(2,1)S(1)}, u32[]{:S(2)}, u32[]{:S(2)}) collective-permute-start(bf16[1152,128]{1,0:T(8,128)(2,1)} %shard_map.55.w00), channel_id=1, source_target_pairs={{0,4},{4,8},{8,12},{12,16},{16,20},{20,24},{24,28},{28,32},{32,36}... | collective-permute-start | bytes 884744 | tf_op jit(solution)/shard_map/ppermute | solution.py:17
  8.4 30.1 %collective-permute-start.5 = (bf16[1152,128]{1,0:T(8,128)(2,1)}, bf16[1152,128]{1,0:T(8,128)(2,1)}, u32[]{:S(2)}, u32[]{:S(2)}) collective-permute-start(bf16[1152,128]{1,0:T(8,128)(2,1)} %shard_map.55.w00), channel_id=1, source_target_pairs={{4,0},{8,4},{12,8},{16,12},{20,16},{24,20},{28,24},{32,28},{36,32}... | collective-permute-start | bytes 884744 | tf_op jit(solution)/shard_map/ppermute | solution.py:17
  17.0 1.3 %copy-start.10 = (s32[16]{0:T(128)S(1)}, s32[16]{0:T(128)}, u32[]{:S(2)}) copy-start(s32[16]{0:T(128)} %param.7) | copy-start | bytes 196
  17.0 14.0 %copy-start.9 = (s32[16,4]{0,1:T(4,128)S(1)}, s32[16,4]{0,1:T(4,128)}, u32[]{:S(2)}) copy-start(s32[16,4]{0,1:T(4,128)} %param.6) | copy-start | bytes 772
  19.9 21.9 %copy-start.2 = (bf16[1152,128]{1,0:T(8,128)(2,1)S(1)}, bf16[1152,128]{1,0:T(8,128)(2,1)}, u32[]{:S(2)}) copy-start(bf16[1152,128]{1,0:T(8,128)(2,1)} %shard_map.55.w00) | copy-start | bytes 884740
  22.1 17.9 %collective-permute-start.4 = (bf16[3456,128]{1,0:T(8,128)(2,1)}, bf16[3456,128]{1,0:T(8,128)(2,1)S(1)}, u32[]{:S(2)}, u32[]{:S(2)}) collective-permute-start(bf16[3456,128]{1,0:T(8,128)(2,1)} %constant_dynamic-update-slice_fusion), channel_id=1, source_target_pairs={{0,4},{4,8},{8,12},{12,16},{16,20},{20,24},{24,28},{28,32},{32,36}... | collective-permute-start | bytes 2654216 | tf_op jit(solution)/shard_map/ppermute | solution.py:17
  24.0 17.8 %collective-permute-start.6 = (bf16[3456,128]{1,0:T(8,128)(2,1)}, bf16[3456,128]{1,0:T(8,128)(2,1)S(1)}, u32[]{:S(2)}, u32[]{:S(2)}) collective-permute-start(bf16[3456,128]{1,0:T(8,128)(2,1)} %constant_dynamic-update-slice_fusion), channel_id=1, source_target_pairs={{4,0},{8,4},{12,8},{16,12},{20,16},{24,20},{28,24},{32,28},{36,32}... | collective-permute-start | bytes 2654216 | tf_op jit(solution)/shard_map/ppermute | solution.py:17
  41.8 2.8 %copy-start.1 = (bf16[16,4,192,192]{3,2,1,0:T(8,128)(2,1)S(1)}, bf16[16,4,192,192]{3,2,1,0:T(8,128)(2,1)}, u32[]{:S(2)}) copy-start(bf16[16,4,192,192]{3,2,1,0:T(8,128)(2,1)} %s_hbm.1) | copy-start | bytes 14155780
  61.0 0.7 copy-start.3
  61.7 10.7 %collective-permute-start.7 = (f32[480,96]{1,0:T(8,128)S(1)}, f32[480,96]{1,0:T(8,128)S(1)}, u32[]{:S(2)}, u32[]{:S(2)}) collective-permute-start(f32[480,96]{1,0:T(8,128)S(1)} %get-tuple-element.13), channel_id=1, source_target_pairs={{4,0},{8,4},{12,8},{16,12},{20,16},{24,20},{28,24},{32,28},{36,32}... | collective-permute-start | bytes 552968 | tf_op jit(solution)/shard_map/ppermute | solution.py:17
  68.7 10.8 %collective-permute-start.8 = (f32[480,96]{1,0:T(8,128)S(1)}, f32[480,96]{1,0:T(8,128)S(1)}, u32[]{:S(2)}, u32[]{:S(2)}) collective-permute-start(f32[480,96]{1,0:T(8,128)S(1)} %get-tuple-element.14), channel_id=1, source_target_pairs={{0,4},{4,8},{8,12},{12,16},{16,20},{20,24},{24,28},{28,32},{32,36}... | collective-permute-start | bytes 552968 | tf_op jit(solution)/shard_map/ppermute | solution.py:17
  72.4 7.1 %copy-start.4 = (f32[480,96]{1,0:T(8,128)}, f32[480,96]{1,0:T(8,128)S(1)}, u32[]{:S(2)}) copy-start(f32[480,96]{1,0:T(8,128)S(1)} %collective-permute-done.7.above_ref) | copy-start | bytes 552964
  79.5 0.7 copy-start.5
  82.3 6.2 %collective-permute-start.10 = (f32[168,96]{1,0:T(8,128)}, f32[168,96]{1,0:T(8,128)S(1)}, u32[]{:S(2)}, u32[]{:S(2)}) collective-permute-start(f32[168,96]{1,0:T(8,128)} %get-tuple-element.17), channel_id=1, source_target_pairs={{0,2},{1,3},{2,0},{3,1},{4,6},{5,7},{6,4},{7,5},{8,10},{9,11},{10,... | collective-permute-start | bytes 193544 | tf_op jit(solution)/shard_map/ppermute | solution.py:22
  83.0 5.4 %collective-permute-start.11 = (f32[168,96]{1,0:T(8,128)}, f32[168,96]{1,0:T(8,128)S(1)}, u32[]{:S(2)}, u32[]{:S(2)}) collective-permute-start(f32[168,96]{1,0:T(8,128)} %get-tuple-element.18), channel_id=1, source_target_pairs={{0,3},{1,0},{2,1},{3,2},{4,7},{5,4},{6,5},{7,6},{8,11},{9,8},{10,9... | collective-permute-start | bytes 193544 | tf_op jit(solution)/shard_map/ppermute | solution.py:22
  85.3 5.9 %collective-permute-start.9 = (f32[168,96]{1,0:T(8,128)}, f32[168,96]{1,0:T(8,128)S(1)}, u32[]{:S(2)}, u32[]{:S(2)}) collective-permute-start(f32[168,96]{1,0:T(8,128)} %get-tuple-element.16), channel_id=1, source_target_pairs={{0,1},{1,2},{2,3},{3,0},{4,5},{5,6},{6,7},{7,4},{8,9},{9,10},{10,1... | collective-permute-start | bytes 193544 | tf_op jit(solution)/shard_map/ppermute | solution.py:22
  88.5 2.8 %copy-start.6 = (f32[168,96]{1,0:T(8,128)}, f32[168,96]{1,0:T(8,128)S(1)}, u32[]{:S(2)}) copy-start(f32[168,96]{1,0:T(8,128)S(1)} %collective-permute-done.10.c) | copy-start | bytes 193540
  88.5 2.8 %copy-start.7 = (f32[168,96]{1,0:T(8,128)}, f32[168,96]{1,0:T(8,128)S(1)}, u32[]{:S(2)}) copy-start(f32[168,96]{1,0:T(8,128)S(1)} %collective-permute-done.11.d) | copy-start | bytes 193540
  91.2 0.6 copy-start.8

commit v2 on v0

v2 whole, which is shorter than its diff:
```python
import jax
import jax.numpy as jnp
from jax import lax
from jax.experimental import pallas as pl
from jax.experimental.pallas import tpu as pltpu
from jax.sharding import PartitionSpec as P

MODES = 6
LANES = 128
PARTS = 4
BF = jnp.bfloat16
F32 = jnp.float32
I32 = jnp.int32


def around(x, by):
    length = lax.axis_size("cols")
    return lax.ppermute(x, "cols", [(i, (i + by) % length) for i in range(length)])


def swap_chip(x):
    length = lax.axis_size("rows")
    return lax.ppermute(x, "rows", [(i, i ^ 1) for i in range(length)])


def swap_cross(x):
    rows = lax.axis_size("rows")
    cols = lax.axis_size("cols")
    pairs = []
    for c in range(cols):
        for r in range(1, rows - 1, 2):
            pairs += [(r * cols + c, (r + 1) * cols + c), ((r + 1) * cols + c, r * cols + c)]
        for r in (0, rows - 1):
            pairs.append((r * cols + c, r * cols + (c ^ 1)))
    return lax.ppermute(x, ("rows", "cols"), pairs)


def dot(a, b, trans_b=False):
    return lax.dot_general(
        a, b, (((1,), (1 if trans_b else 0,)), ((), ())), preferred_element_type=F32
    )


def pack_kernel(q_ref, out_ref):
    blocks, rows, dofs = q_ref.shape
    half = blocks // 2
    groups = rows // MODES
    many = 4
    r = lax.broadcasted_iota(I32, (many * rows, many * rows), 0)
    c = lax.broadcasted_iota(I32, (many * rows, many * rows), 1)
    rl = r % rows
    perm = (r - rl) + (rl % groups) * MODES + rl // groups == c
    perm = jnp.where(perm, 1.0, 0.0).astype(BF)
    step = many * rows
    for n in range(half // many):
        a = dot(perm, q_ref[n * many : (n + 1) * many].reshape(step, dofs))
        b = dot(perm, q_ref[half + n * many : half + (n + 1) * many].reshape(step, dofs))
        lo = n * step
        out_ref[lo : lo + step, :] = a[:, :LANES].astype(BF)
        hi = half * rows + lo
        out_ref[hi : hi + step, :] = b[:, :LANES].astype(BF)
        mixed = jnp.concatenate([a[:, LANES:], b[:, LANES:]], axis=1)
        tail = blocks * rows + lo
        out_ref[tail : tail + step, :] = mixed.astype(BF)


def table_kernel(where_ref, nbr_ref, aggs_ref, s_hbm, s_out, aggr_ref, aggl_ref, rel, ssem):
    slots, blocks = nbr_ref.shape
    copies = [pltpu.make_async_copy(s_hbm.at[i], s_out.at[i], ssem.at[i]) for i in range(blocks)]
    for cp in copies:
        cp.start()
    nagg, total = aggs_ref.shape
    groups = nagg // PARTS
    row = where_ref[0]
    col = where_ref[1]
    rel[...] = (aggs_ref[...] - (row - 2) * blocks).astype(F32)
    turned = []
    for d in range(PARTS):
        q = col + d
        q = jnp.where(q >= PARTS, q - PARTS, q)
        turned.append(rel[pl.ds(pl.multiple_of(q * groups, groups), groups), :])
    turned = jnp.concatenate(turned, axis=0).astype(BF)
    wanted = nbr_ref[...].T
    lane = lax.broadcasted_iota(I32, (blocks, total), 1)
    pieces = []
    for k in range(slots):
        hot = jnp.where(lane == wanted[:, k : k + 1], 1.0, 0.0).astype(BF)
        pieces.append(dot(hot, turned, True))
    aggr_ref[...] = jnp.concatenate(pieces, axis=1).astype(I32)
    sub = lax.broadcasted_iota(I32, (blocks, total), 0) + row * blocks
    own = dot(jnp.where(lane == sub, 1.0, 0.0).astype(BF), turned, True)
    src = lax.broadcasted_iota(I32, (nagg, MODES * nagg), 0)
    dst = lax.broadcasted_iota(I32, (nagg, MODES * nagg), 1)
    rows = MODES * groups
    spread = src == (dst // rows) * groups + dst % groups
    own = dot(own.astype(BF), jnp.where(spread, 1.0, 0.0).astype(BF)).astype(I32) - blocks
    mode = (lax.broadcasted_iota(I32, own.shape, 1) % rows) // groups
    aggl_ref[...] = (own // blocks) * LANES + (own % blocks) * MODES + mode
    for cp in copies:
        cp.wait()


def left_kernel(aggl_ref, w0, w1, w2, w3, out_ref):
    blocks = out_ref.shape[0]
    half = blocks // 2
    dofs = out_ref.shape[2]
    rows = aggl_ref.shape[1] // PARTS
    for i in range(blocks):
        hot = lax.broadcasted_iota(I32, (3 * LANES, PARTS * rows), 0) == aggl_ref[i : i + 1, :]
        hot = jnp.where(hot, 1.0, 0.0).astype(BF)
        first = jnp.concatenate([w[i * rows : (i + 1) * rows] for w in (w0, w1, w2, w3)], axis=0)
        at = (blocks + i % half) * rows
        second = jnp.concatenate([w[at : at + rows] for w in (w0, w1, w2, w3)], axis=0)
        left = dot(hot, jnp.concatenate([first, second], axis=1))
        if i < half:
            left = left[:, :dofs]
        else:
            left = jnp.concatenate([left[:, :LANES], left[:, dofs:]], axis=1)
        out_ref[i] = left.astype(BF)


def main_kernel(where_ref, nbr_ref, live_ref, aggr_ref, left_ref, sbuf, *rest):
    pieces = rest[: 3 * PARTS]
    chip_ref, mid_ref, cross_ref, wbuf, acc, wsem = rest[3 * PARTS :]
    blocks, slots, dofs, _ = sbuf.shape
    half = blocks // 2
    quarter = pieces[0].shape[0]
    rows = quarter // (blocks + half)
    groups = rows // MODES
    reach = 5 * blocks
    row = where_ref[0]
    col = where_ref[1]
    copies = [
        pltpu.make_async_copy(p, wbuf.at[pl.ds(n * quarter, quarter)], wsem.at[n])
        for n, p in enumerate(pieces)
    ]
    for cp in copies:
        cp.start()

    acc[...] = jnp.zeros_like(acc)
    zeros = jnp.zeros((dofs, 2 * LANES - dofs), BF)
    for cp in copies:
        cp.wait()

    def one(i):
        images = []
        for k in range(slots):
            j = nbr_ref[k, i] - (row - 1) * blocks
            w = j // blocks
            jl = j - w * blocks
            odd = row % 2
            w = jnp.where(w == 1, 0, jnp.where((w == 2) == (odd == 0), 1, 2))
            place = w * PARTS * quarter
            jh = jnp.where(jl >= half, jl - half, jl)
            first = [
                wbuf[pl.ds(pl.multiple_of(place + d * quarter + jl * rows, 16), rows), :]
                for d in range(PARTS)
            ]
            second = [
                wbuf[pl.ds(pl.multiple_of(place + d * quarter + (blocks + jh) * rows, 16), rows), :]
                for d in range(PARTS)
            ]
            pj = jnp.concatenate(
                [jnp.concatenate(first, axis=0), jnp.concatenate(second, axis=0)], axis=1
            )
            s = sbuf[i, k]
            tail = s[:, LANES:]
            tail = jnp.where(
                jl < half,
                jnp.concatenate([tail, zeros], axis=1),
                jnp.concatenate([zeros, tail], axis=1),
            )
            images.append(dot(pj, jnp.concatenate([s[:, :LANES], tail], axis=1), True))
        lane = lax.broadcasted_iota(I32, (1, slots * PARTS * groups), 1) // (PARTS * groups)
        target = jnp.where(lane + col * slots < live_ref[i], aggr_ref[pl.ds(i, 1), :], -1)
        place_t = lax.broadcasted_iota(I32, (reach, slots * PARTS * groups), 0) == target
        place_t = jnp.where(place_t, 1.0, 0.0).astype(BF)
        assembled = []
        for m in range(MODES):
            rhs = jnp.concatenate(
                [
                    img[d * rows + m * groups : d * rows + (m + 1) * groups]
                    for img in images
                    for d in range(PARTS)
                ],
                axis=0,
            ).astype(BF)
            assembled.append(dot(place_t, rhs).astype(BF))
        return dot(jnp.concatenate(assembled, axis=0), left_ref[i], True)

    def step(n, carry):
        acc[...] += one(n) + one(n + half)
        return carry

    lax.fori_loop(0, half, step, 0)
    width = mid_ref.shape[1]
    even = row % 2 == 0
    low = acc[:, :width]
    up = acc[:, 2 * LANES : 2 * LANES + width]
    chip_ref[...] = jnp.where(even, up, low)
    mid_ref[...] = acc[:, LANES : LANES + width]
    cross_ref[...] = jnp.where(even, low, up)


def share_kernel(where_ref, mid_ref, chip_ref, cross_ref, o0, o1, o2, o3, tot):
    reach = mid_ref.shape[0] // MODES
    band = tot.shape[0] // MODES
    blocks = band // 7
    piece = o0.shape[0]
    width = tot.shape[1]

    def zeros(n):
        return jnp.zeros((n * blocks, width), F32)

    even = where_ref[0] % 2 == 0
    for m in range(MODES):
        src = slice(m * reach, (m + 1) * reach)
        above = jnp.where(even, chip_ref[src], cross_ref[src])
        below = jnp.where(even, cross_ref[src], chip_ref[src])
        tot[m * band : (m + 1) * band] = (
            jnp.concatenate([zeros(1), mid_ref[src], zeros(1)], axis=0)
            + jnp.concatenate([zeros(2), above], axis=0)
            + jnp.concatenate([below, zeros(2)], axis=0)
        )
    for d, o in enumerate((o0, o1, o2, o3)):
        c = where_ref[1] + d
        c = jnp.where(c >= PARTS, c - PARTS, c)
        o[...] = tot[pl.ds(pl.multiple_of(c * piece, 8), piece), :]


def on_device(stiffness, neighbors, live_counts, prolong, prolong_aggs):
    row_pos = lax.axis_index("rows")
    col_pos = lax.axis_index("cols")
    blocks, slots, dofs, _ = stiffness.shape
    rows = prolong.shape[1]
    nagg = prolong_aggs.shape[1]
    quarter = (blocks + blocks // 2) * rows
    vmem = pl.BlockSpec(memory_space=pltpu.VMEM)
    smem = pl.BlockSpec(memory_space=pltpu.SMEM)
    any_ = pl.BlockSpec(memory_space=pl.ANY)
    hbm = pl.BlockSpec(memory_space=pltpu.HBM)
    where = jnp.stack([row_pos, col_pos]).astype(I32)
    nbr = neighbors.T

    w0 = pl.pallas_call(
        pack_kernel,
        out_shape=jax.ShapeDtypeStruct((quarter, LANES), BF),
        in_specs=[vmem],
        out_specs=vmem,
    )(prolong)
    w1 = around(w0, -1)
    w3 = around(w0, 1)
    b0 = swap_cross(w0)
    a0 = swap_chip(w0)
    later, a0 = lax.optimization_barrier((w0, a0))
    w2 = around(later, 2)

    s_near, aggr, aggl = pl.pallas_call(
        table_kernel,
        out_shape=[
            pltpu.VMEM(stiffness.shape, BF),
            jax.ShapeDtypeStruct((blocks, slots * nagg), I32),
            jax.ShapeDtypeStruct((blocks, MODES * nagg), I32),
        ],
        in_specs=[smem, vmem, vmem, hbm],
        out_specs=[vmem] * 3,
        scratch_shapes=[
            pltpu.VMEM((nagg, prolong_aggs.shape[0]), F32),
            pltpu.SemaphoreType.DMA((blocks,)),
        ],
        compiler_params=pltpu.CompilerParams(vmem_limit_bytes=52 * 2**20),
    )(where, nbr, prolong_aggs.T, stiffness)
    w1, w3, aggl = lax.optimization_barrier((w1, w3, aggl))

    b1 = swap_cross(w1)
    b3 = swap_cross(w3)
    a1 = swap_chip(w1)
    a3 = swap_chip(w3)
    w2, w1, w3 = lax.optimization_barrier((w2, w1, w3))
    b2 = swap_cross(w2)
    a2 = swap_chip(w2)

    left = pl.pallas_call(
        left_kernel,
        out_shape=pltpu.VMEM((blocks, 3 * LANES, dofs), BF),
        in_specs=[vmem] * 5,
        out_specs=vmem,
        compiler_params=pltpu.CompilerParams(vmem_limit_bytes=16 * 2**20),
    )(aggl, w0, w1, w2, w3)

    reach = 5 * blocks
    out = jax.ShapeDtypeStruct((MODES * reach, blocks * MODES), F32)
    to_chip, mid, to_cross = pl.pallas_call(
        main_kernel,
        out_shape=[out, out, out],
        in_specs=[smem, smem, smem, vmem, vmem, vmem] + [any_] * 12,
        out_specs=[vmem] * 3,
        scratch_shapes=[
            pltpu.VMEM((3 * PARTS * quarter, LANES), BF),
            pltpu.VMEM((MODES * reach, 3 * LANES), F32),
            pltpu.SemaphoreType.DMA((3 * PARTS,)),
        ],
        compiler_params=pltpu.CompilerParams(vmem_limit_bytes=40 * 2**20),
    )(where, nbr, live_counts, aggr, left, s_near, w0, w1, w2, w3, a0, a1, a2, a3, b0, b1, b2, b3)
    from_cross = swap_cross(to_cross)
    from_chip = swap_chip(to_chip)
    piece = MODES * 7 * blocks // PARTS
    sh = jax.ShapeDtypeStruct((piece, blocks * MODES), F32)
    s0, s1, s2, s3 = pl.pallas_call(
        share_kernel,
        out_shape=[sh] * 4,
        in_specs=[smem] + [vmem] * 3,
        out_specs=[vmem] * 4,
        scratch_shapes=[pltpu.VMEM((MODES * 7 * blocks, blocks * MODES), F32)],
    )(where, mid, from_chip, from_cross)
    t1 = around(s1, 1)
    t3 = around(s3, -1)
    t2 = around(s2, 2)
    return ((s0 + t1) + (t2 + t3)).T


def solution(mesh):
    in_specs = (
        P("rows", "cols", None, None),
        P("rows", "cols"),
        P("rows"),
        P("rows", "cols", None),
        P(),
    )
    out_specs = P("rows", "cols")
    return jax.shard_map(
        on_device, mesh=mesh, in_specs=in_specs, out_specs=out_specs, check_vma=False
    )
```

time: 233 us -> 66.2 us (0.28); the launches traced: 229 us -> 65.8 us
  waiting for transfers between devices: 99.1 us -> 23 us
  other arithmetic: 50.8 us -> 2.2 us
  matrix products: 23.4 us -> 0 us
  Pallas kernels: 0 us -> 21.1 us
  local copies, waits for them, and re-layouts: 23.8 us -> 2.8 us
  between operations: 14.3 us -> 0.1 us
    scatter-add x1 -> x0, other arithmetic: 44.5 us -> none  [on_device(): jax.ops.segment_sum(projected.reshape(blocks * groups, MODES, MODES * rea...]
    unnamed x3 -> x0, waiting for transfers between devices: 44.2 us -> none
    all_gather x1 -> x0, waiting for transfers between devices: 31.3 us -> none  [on_device(): full = lax.all_gather(prolong, 'cols', axis=1, tiled=True)]
    dot_general x3 -> x0, matrix products: 23.4 us -> none  [the longest x1 8.71 us: on_device(): jnp.einsum('ikfam,ikaw->ifmw', spread, placement, preferred_element_type=...]
    pallas_call x0 -> x5, Pallas kernels: none -> 21.1 us  [the longest x1 11.4 us: on_device(): pl.pallas_call(main_kernel, out_shape=[out, out, out], in_specs=[smem, sm...]
    reshape x5 -> x0, local copies, waits for them, and re-layouts: 8.81 us -> none  [the longest x1 8.32 us: on_device(): projected.reshape(blocks * groups, MODES, MODES * reach)]
    gather x2 -> x0, local copies, waits for them, and re-layouts: 6.55 us -> none  [the longest x1 5.96 us: on_device(): jnp.take(window, positions, axis=0).reshape(blocks, slots, coarse, dofs)]
    concatenate x1 -> x0, other arithmetic: 4.05 us -> none  [on_device(): window = jnp.concatenate([below, full, above], axis=0)]
  transfers between devices with their start and end apart: 6 -> 16, of which waited for: 6 -> 8; matrix products, arithmetic and copies ran while one was open for 2% -> 1% of each run, Pallas kernels for 0% -> 8%
where the time goes in v2:
time: 66.2 us; the launch traced here: 65.8 us
  waiting for transfers between devices  23 us (35%)
  Pallas kernels  21.1 us (32%)
  starting transfers between devices  16.7 us (25%)
  local copies, waits for them, and re-layouts  2.8 us (4%)
  other arithmetic  2.2 us (3%)
    ppermute x5, waiting for transfers between devices, swap_cross(): return lax.ppermute(x, ('rows', 'cols'), pairs)  13.5 us
    pallas_call x1, Pallas kernels, on_device(): pl.pallas_call(main_kernel, out_shape=[out, out, out], in_specs=[smem, sm...  11.4 us
    ppermute x5, starting transfers between devices, swap_cross(): return lax.ppermute(x, ('rows', 'cols'), pairs)  10.3 us
    ppermute x6, waiting for transfers between devices, around(): lax.ppermute(x, 'cols', [(i, (i + by) % length) for i in range(length)])  9.42 us
    ppermute x6, starting transfers between devices, around(): lax.ppermute(x, 'cols', [(i, (i + by) % length) for i in range(length)])  6.42 us
    pallas_call x1, Pallas kernels, on_device(): pl.pallas_call(table_kernel, out_shape=[pltpu.VMEM(stiffness.shape, BF),...  4.53 us
    unnamed x18, local copies, waits for them, and re-layouts  2.8 us
    pallas_call x1, Pallas kernels, on_device(): pl.pallas_call(pack_kernel, out_shape=jax.ShapeDtypeStruct((quarter, LANE...  2.11 us
  transfers between devices with their start and end apart: 16, of which 8 were waited for; matrix products, arithmetic and copies ran while one was open for 1% of the time, Pallas kernels for 8%

profile of v2, /device:TPU:134, one launch (start us, length us, event | category | flops | bytes accessed | tf_op | source)
XLA Modules:
  0.0 65.8 jit_solution(5040685226115393170)
XLA Ops:
  0.0 2.1 %shard_map.56.w0.rest_0_ = bf16[1152,128]{1,0:T(8,128)(2,1)} custom-call(bf16[16,48,192]{2,1,0:T(8,128)(2,1)} %q_ref.1), custom_call_target="tpu_custom_call" | custom-call | tf_op jit(solution)/shard_map/pallas_call | solution.py:245
  2.6 1.5 %collective-permute-start = (bf16[1152,128]{1,0:T(8,128)(2,1)}, bf16[1152,128]{1,0:T(8,128)(2,1)S(1)}, u32[]{:S(2)}, u32[]{:S(2)}) collective-permute-start(bf16[1152,128]{1,0:T(8,128)(2,1)} %shard_map.56.w0.rest_0_), channel_id=1, source_target_pairs={{0,3},{1,0},{2,1},{3,2},{4,7},{5,4},{6,5},{7,6},{8,11},{9,8},{10,9... | collective-permute-start | bytes 884744 | tf_op jit(solution)/shard_map/ppermute | solution.py:18
  4.2 2.1 %collective-permute-start.7 = (bf16[1152,128]{1,0:T(8,128)(2,1)}, bf16[1152,128]{1,0:T(8,128)(2,1)S(1)}, u32[]{:S(2)}, u32[]{:S(2)}) collective-permute-start(bf16[1152,128]{1,0:T(8,128)(2,1)} %shard_map.56.w0.rest_0_), channel_id=1, source_target_pairs={{4,8},{8,4},{12,16},{16,12},{20,24},{24,20},{28,32},{32,28},{36,40... | collective-permute-start | bytes 884744 | tf_op jit(solution)/shard_map/ppermute | solution.py:35
  6.9 4.5 %shard_map.55 = (bf16[16,4,192,192]{3,2,1,0:T(8,128)(2,1)S(1)}, s32[16,128]{1,0:T(8,128)}, s32[16,192]{1,0:T(8,128)}) custom-call(s32[2]{0:T(128)} %pad_add_fusion.where_ref, s32[4,16]{1,0:T(4,128)} %bitcast.6, s32[32,1024]{1,0:T(8,128)} %bitcast.8, bf16[16,4,192,192]{3,2,1,0:T(8,128)(2,1)} %s_hbm.1), custom_call_target="tpu_custom_call" | custom-call | tf_op jit(solution)/shard_map/pallas_call | solution.py:258
  11.5 1.5 %collective-permute-start.3 = (bf16[1152,128]{1,0:T(8,128)(2,1)S(1)}, bf16[1152,128]{1,0:T(8,128)(2,1)S(1)}, u32[]{:S(2)}, u32[]{:S(2)}) collective-permute-start(bf16[1152,128]{1,0:T(8,128)(2,1)S(1)} %copy-done), channel_id=1, source_target_pairs={{0,2},{1,3},{2,0},{3,1},{4,6},{5,7},{6,4},{7,5},{8,10},{9,11},{10,... | collective-permute-start | bytes 884744 | tf_op jit(solution)/shard_map/ppermute | solution.py:18
  13.2 2.5 %collective-permute-start.8 = (bf16[1152,128]{1,0:T(8,128)(2,1)S(1)}, bf16[1152,128]{1,0:T(8,128)(2,1)S(1)}, u32[]{:S(2)}, u32[]{:S(2)}) collective-permute-start(bf16[1152,128]{1,0:T(8,128)(2,1)S(1)} %collective-permute-done.w1.rest_1_), channel_id=1, source_target_pairs={{4,8},{8,4},{12,16},{16,12},{20,24},{24,20},{28,32},{32,28},{36,40... | collective-permute-start | bytes 884744 | tf_op jit(solution)/shard_map/ppermute | solution.py:35
  15.7 2.6 %collective-permute-start.10 = (bf16[1152,128]{1,0:T(8,128)(2,1)S(1)}, bf16[1152,128]{1,0:T(8,128)(2,1)S(1)}, u32[]{:S(2)}, u32[]{:S(2)}) collective-permute-start(bf16[1152,128]{1,0:T(8,128)(2,1)S(1)} %collective-permute-done.1.w3.rest_3_), channel_id=1, source_target_pairs={{4,8},{8,4},{12,16},{16,12},{20,24},{24,20},{28,32},{32,28},{36,40... | collective-permute-start | bytes 884744 | tf_op jit(solution)/shard_map/ppermute | solution.py:35
  18.2 3.3 %collective-permute-done.3.w2.rest_2_ = bf16[1152,128]{1,0:T(8,128)(2,1)S(1)} collective-permute-done((bf16[1152,128]{1,0:T(8,128)(2,1)S(1)}, bf16[1152,128]{1,0:T(8,128)(2,1)S(1)}, u32[]{:S(2)}, u32[]{:S(2)}) %collective-permute-start.3) | collective-permute-done | bytes 294944 | tf_op jit(solution)/shard_map/ppermute | solution.py:18
  21.6 1.6 %collective-permute-start.9 = (bf16[1152,128]{1,0:T(8,128)(2,1)S(1)}, bf16[1152,128]{1,0:T(8,128)(2,1)S(1)}, u32[]{:S(2)}, u32[]{:S(2)}) collective-permute-start(bf16[1152,128]{1,0:T(8,128)(2,1)S(1)} %collective-permute-done.3.w2.rest_2_), channel_id=1, source_target_pairs={{4,8},{8,4},{12,16},{16,12},{20,24},{24,20},{28,32},{32,28},{36,40... | collective-permute-start | bytes 884744 | tf_op jit(solution)/shard_map/ppermute | solution.py:35
  23.1 0.7 %copy-done.2 = s32[16,192]{1,0:T(8,128)S(1)} copy-done((s32[16,192]{1,0:T(8,128)S(1)}, s32[16,192]{1,0:T(8,128)}, u32[]{:S(2)}) %copy-start.2) | copy-done | bytes 12312
  23.8 1.0 %shard_map.57.left_ref = bf16[16,384,192]{2,1,0:T(8,128)(2,1)S(1)} custom-call(s32[16,192]{1,0:T(8,128)S(1)} %copy-done.2, bf16[1152,128]{1,0:T(8,128)(2,1)S(1)} %copy-done, bf16[1152,128]{1,0:T(8,128)(2,1)S(1)} %collective-permute-done.w1.rest_1_, bf16[1152,128]{1,0:T(8,128)(2,1)S(1)} %collective-permute-done.3.w2.rest_2_, ...), custom_call_target="tpu_custom_call" | custom-call | tf_op jit(solution)/shard_map/pallas_call | solution.py:283
  24.9 0.9 %collective-permute-done.10.rest_11_ = bf16[1152,128]{1,0:T(8,128)(2,1)S(1)} collective-permute-done((bf16[1152,128]{1,0:T(8,128)(2,1)S(1)}, bf16[1152,128]{1,0:T(8,128)(2,1)S(1)}, u32[]{:S(2)}, u32[]{:S(2)}) %collective-permute-start.10) | collective-permute-done | bytes 294944 | tf_op jit(solution)/shard_map/ppermute | solution.py:35
  25.8 5.2 %collective-permute-done.9.rest_10_ = bf16[1152,128]{1,0:T(8,128)(2,1)S(1)} collective-permute-done((bf16[1152,128]{1,0:T(8,128)(2,1)S(1)}, bf16[1152,128]{1,0:T(8,128)(2,1)S(1)}, u32[]{:S(2)}, u32[]{:S(2)}) %collective-permute-start.9) | collective-permute-done | bytes 294944 | tf_op jit(solution)/shard_map/ppermute | solution.py:35
  31.1 0.7 %copy-done.3 = s32[16,128]{1,0:T(8,128)S(1)} copy-done((s32[16,128]{1,0:T(8,128)S(1)}, s32[16,128]{1,0:T(8,128)}, u32[]{:S(2)}) %copy-start.3) | copy-done | bytes 8216
  31.8 11.4 %shard_map.58 = (f32[480,96]{1,0:T(8,128)S(1)}, f32[480,96]{1,0:T(8,128)S(1)}, f32[480,96]{1,0:T(8,128)S(1)}) custom-call(s32[2]{0:T(128)S(1)} %copy-done.5, s32[4,16]{1,0:T(4,128)S(1)} %bitcast.7, s32[16]{0:T(128)S(1)} %copy-done.6, s32[16,128]{1,0:T(8,128)S(1)} %copy-done.3, bf16[16,384,192]{2,1,0:T(8,128)(2,1)S(1)} %shard_map.57.left_ref, ...), custom_call_target="tpu_custom_call" | custom-call | tf_op jit(solution)/shard_map/pallas_call | solution.py:293
  43.9 1.5 %collective-permute-start.12 = (f32[480,96]{1,0:T(8,128)S(1)}, f32[480,96]{1,0:T(8,128)S(1)}, u32[]{:S(2)}, u32[]{:S(2)}) collective-permute-start(f32[480,96]{1,0:T(8,128)S(1)} %get-tuple-element.36), channel_id=1, source_target_pairs={{4,8},{8,4},{12,16},{16,12},{20,24},{24,20},{28,32},{32,28},{36,40... | collective-permute-start | bytes 552968 | tf_op jit(solution)/shard_map/ppermute | solution.py:35
  45.4 7.4 %collective-permute-done.12.cross_ref = f32[480,96]{1,0:T(8,128)S(1)} collective-permute-done((f32[480,96]{1,0:T(8,128)S(1)}, f32[480,96]{1,0:T(8,128)S(1)}, u32[]{:S(2)}, u32[]{:S(2)}) %collective-permute-start.12) | collective-permute-done | bytes 184352 | tf_op jit(solution)/shard_map/ppermute | solution.py:35
  53.5 2.0 %shard_map.59 = (f32[168,96]{1,0:T(8,128)}, f32[168,96]{1,0:T(8,128)}, f32[168,96]{1,0:T(8,128)}, f32[168,96]{1,0:T(8,128)}) custom-call(s32[2]{0:T(128)} %pad_add_fusion.where_ref, f32[480,96]{1,0:T(8,128)} %copy-done.1, f32[480,96]{1,0:T(8,128)} %copy-done.7, f32[480,96]{1,0:T(8,128)} %copy-done.8), custom_call_target="tpu_custom_call" | custom-call | tf_op jit(solution)/shard_map/pallas_call | solution.py:309
  55.5 1.7 %collective-permute-start.13 = (f32[168,96]{1,0:T(8,128)}, f32[168,96]{1,0:T(8,128)S(1)}, u32[]{:S(2)}, u32[]{:S(2)}) collective-permute-start(f32[168,96]{1,0:T(8,128)} %get-tuple-element.38), channel_id=1, source_target_pairs={{0,1},{1,2},{2,3},{3,0},{4,5},{5,6},{6,7},{7,4},{8,9},{9,10},{10,1... | collective-permute-start | bytes 193544 | tf_op jit(solution)/shard_map/ppermute | solution.py:18
  57.2 1.2 %collective-permute-start.14 = (f32[168,96]{1,0:T(8,128)}, f32[168,96]{1,0:T(8,128)S(1)}, u32[]{:S(2)}, u32[]{:S(2)}) collective-permute-start(f32[168,96]{1,0:T(8,128)} %get-tuple-element.39), channel_id=1, source_target_pairs={{0,2},{1,3},{2,0},{3,1},{4,6},{5,7},{6,4},{7,5},{8,10},{9,11},{10,... | collective-permute-start | bytes 193544 | tf_op jit(solution)/shard_map/ppermute | solution.py:18
  58.4 1.8 %collective-permute-done.13 = f32[168,96]{1,0:T(8,128)S(1)} collective-permute-done((f32[168,96]{1,0:T(8,128)}, f32[168,96]{1,0:T(8,128)S(1)}, u32[]{:S(2)}, u32[]{:S(2)}) %collective-permute-start.13) | collective-permute-done | bytes 64544 | tf_op jit(solution)/shard_map/ppermute | solution.py:18
  60.2 3.2 %collective-permute-done.14 = f32[168,96]{1,0:T(8,128)S(1)} collective-permute-done((f32[168,96]{1,0:T(8,128)}, f32[168,96]{1,0:T(8,128)S(1)}, u32[]{:S(2)}, u32[]{:S(2)}) %collective-permute-start.14) | collective-permute-done | bytes 64544 | tf_op jit(solution)/shard_map/ppermute | solution.py:18
  63.4 0.9 %collective-permute-done.15 = f32[168,96]{1,0:T(8,128)S(1)} collective-permute-done((f32[168,96]{1,0:T(8,128)}, f32[168,96]{1,0:T(8,128)S(1)}, u32[]{:S(2)}, u32[]{:S(2)}) %collective-permute-start.15) | collective-permute-done | bytes 64544 | tf_op jit(solution)/shard_map/ppermute | solution.py:18
  64.3 1.6 %add_bitcast_fusion = f32[96,168]{0,1:T(8,128)} fusion(f32[168,96]{1,0:T(8,128)S(1)} %collective-permute-done.14, f32[168,96]{1,0:T(8,128)S(1)} %collective-permute-done.15, f32[168,96]{1,0:T(8,128)} %get-tuple-element.37, f32[168,96]{1,0:T(8,128)S(1)} %collective-permute-done.13), kind=kLoop, calls=%fused_computation | loop fusion | flops 48384 | bytes 322560 | tf_op jit(solution)/shard_map/transpose | solution.py:319
  (33 shorter events, 2.8 us)
Async XLA Ops:
  0.0 31.0 %copy-start.4 = (s32[16,4]{0,1:T(4,128)S(1)}, s32[16,4]{0,1:T(4,128)}, u32[]{:S(2)}) copy-start(s32[16,4]{0,1:T(4,128)} %param.6) | copy-start | bytes 772
  0.0 31.0 %copy-start.6 = (s32[16]{0:T(128)S(1)}, s32[16]{0:T(128)}, u32[]{:S(2)}) copy-start(s32[16]{0:T(128)} %live_ref.1) | copy-start | bytes 196
  2.1 9.3 %copy-start = (bf16[1152,128]{1,0:T(8,128)(2,1)S(1)}, bf16[1152,128]{1,0:T(8,128)(2,1)}, u32[]{:S(2)}) copy-start(bf16[1152,128]{1,0:T(8,128)(2,1)} %shard_map.56.w0.rest_0_) | copy-start | bytes 884740
  2.1 9.3 %collective-permute-start.2 = (bf16[1152,128]{1,0:T(8,128)(2,1)}, bf16[1152,128]{1,0:T(8,128)(2,1)S(1)}, u32[]{:S(2)}, u32[]{:S(2)}) collective-permute-start(bf16[1152,128]{1,0:T(8,128)(2,1)} %shard_map.56.w0.rest_0_), channel_id=1, source_target_pairs={{0,4},{4,0},{8,12},{12,8},{16,20},{20,16},{24,28},{28,24},{32,36},... | collective-permute-start | bytes 884744 | tf_op jit(solution)/shard_map/ppermute | solution.py:23
  2.1 10.8 %collective-permute-start.1 = (bf16[1152,128]{1,0:T(8,128)(2,1)}, bf16[1152,128]{1,0:T(8,128)(2,1)S(1)}, u32[]{:S(2)}, u32[]{:S(2)}) collective-permute-start(bf16[1152,128]{1,0:T(8,128)(2,1)} %shard_map.56.w0.rest_0_), channel_id=1, source_target_pairs={{0,1},{1,2},{2,3},{3,0},{4,5},{5,6},{6,7},{7,4},{8,9},{9,10},{10,1... | collective-permute-start | bytes 884744 | tf_op jit(solution)/shard_map/ppermute | solution.py:18
  2.6 10.6 %collective-permute-start = (bf16[1152,128]{1,0:T(8,128)(2,1)}, bf16[1152,128]{1,0:T(8,128)(2,1)S(1)}, u32[]{:S(2)}, u32[]{:S(2)}) collective-permute-start(bf16[1152,128]{1,0:T(8,128)(2,1)} %shard_map.56.w0.rest_0_), channel_id=1, source_target_pairs={{0,3},{1,0},{2,1},{3,2},{4,7},{5,4},{6,5},{7,6},{8,11},{9,8},{10,9... | collective-permute-start | bytes 884744 | tf_op jit(solution)/shard_map/ppermute | solution.py:18
  4.2 17.4 %collective-permute-start.7 = (bf16[1152,128]{1,0:T(8,128)(2,1)}, bf16[1152,128]{1,0:T(8,128)(2,1)S(1)}, u32[]{:S(2)}, u32[]{:S(2)}) collective-permute-start(bf16[1152,128]{1,0:T(8,128)(2,1)} %shard_map.56.w0.rest_0_), channel_id=1, source_target_pairs={{4,8},{8,4},{12,16},{16,12},{20,24},{24,20},{28,32},{32,28},{36,40... | collective-permute-start | bytes 884744 | tf_op jit(solution)/shard_map/ppermute | solution.py:35
  6.9 24.1 %copy-start.5 = (s32[2]{0:T(128)S(1)}, s32[2]{0:T(128)}, u32[]{:S(2)}) copy-start(s32[2]{0:T(128)} %pad_add_fusion.where_ref) | copy-start | bytes 28
  11.5 10.1 %collective-permute-start.3 = (bf16[1152,128]{1,0:T(8,128)(2,1)S(1)}, bf16[1152,128]{1,0:T(8,128)(2,1)S(1)}, u32[]{:S(2)}, u32[]{:S(2)}) collective-permute-start(bf16[1152,128]{1,0:T(8,128)(2,1)S(1)} %copy-done), channel_id=1, source_target_pairs={{0,2},{1,3},{2,0},{3,1},{4,6},{5,7},{6,4},{7,5},{8,10},{9,11},{10,... | collective-permute-start | bytes 884744 | tf_op jit(solution)/shard_map/ppermute | solution.py:18
  13.2 10.0 %collective-permute-start.8 = (bf16[1152,128]{1,0:T(8,128)(2,1)S(1)}, bf16[1152,128]{1,0:T(8,128)(2,1)S(1)}, u32[]{:S(2)}, u32[]{:S(2)}) collective-permute-start(bf16[1152,128]{1,0:T(8,128)(2,1)S(1)} %collective-permute-done.w1.rest_1_), channel_id=1, source_target_pairs={{4,8},{8,4},{12,16},{16,12},{20,24},{24,20},{28,32},{32,28},{36,40... | collective-permute-start | bytes 884744 | tf_op jit(solution)/shard_map/ppermute | solution.py:35
  15.6 9.3 %collective-permute-start.4 = (bf16[1152,128]{1,0:T(8,128)(2,1)S(1)}, bf16[1152,128]{1,0:T(8,128)(2,1)S(1)}, u32[]{:S(2)}, u32[]{:S(2)}) collective-permute-start(bf16[1152,128]{1,0:T(8,128)(2,1)S(1)} %collective-permute-done.w1.rest_1_), channel_id=1, source_target_pairs={{0,4},{4,0},{8,12},{12,8},{16,20},{20,16},{24,28},{28,24},{32,36},... | collective-permute-start | bytes 884744 | tf_op jit(solution)/shard_map/ppermute | solution.py:23
  15.7 10.1 %collective-permute-start.10 = (bf16[1152,128]{1,0:T(8,128)(2,1)S(1)}, bf16[1152,128]{1,0:T(8,128)(2,1)S(1)}, u32[]{:S(2)}, u32[]{:S(2)}) collective-permute-start(bf16[1152,128]{1,0:T(8,128)(2,1)S(1)} %collective-permute-done.1.w3.rest_3_), channel_id=1, source_target_pairs={{4,8},{8,4},{12,16},{16,12},{20,24},{24,20},{28,32},{32,28},{36,40... | collective-permute-start | bytes 884744 | tf_op jit(solution)/shard_map/ppermute | solution.py:35
  21.6 4.2 %collective-permute-start.6 = (bf16[1152,128]{1,0:T(8,128)(2,1)S(1)}, bf16[1152,128]{1,0:T(8,128)(2,1)S(1)}, u32[]{:S(2)}, u32[]{:S(2)}) collective-permute-start(bf16[1152,128]{1,0:T(8,128)(2,1)S(1)} %collective-permute-done.1.w3.rest_3_), channel_id=1, source_target_pairs={{0,4},{4,0},{8,12},{12,8},{16,20},{20,16},{24,28},{28,24},{32,36},... | collective-permute-start | bytes 884744 | tf_op jit(solution)/shard_map/ppermute | solution.py:23
  21.6 9.5 %collective-permute-start.9 = (bf16[1152,128]{1,0:T(8,128)(2,1)S(1)}, bf16[1152,128]{1,0:T(8,128)(2,1)S(1)}, u32[]{:S(2)}, u32[]{:S(2)}) collective-permute-start(bf16[1152,128]{1,0:T(8,128)(2,1)S(1)} %collective-permute-done.3.w2.rest_2_), channel_id=1, source_target_pairs={{4,8},{8,4},{12,16},{16,12},{20,24},{24,20},{28,32},{32,28},{36,40... | collective-permute-start | bytes 884744 | tf_op jit(solution)/shard_map/ppermute | solution.py:35
  23.1 7.9 %collective-permute-start.5 = (bf16[1152,128]{1,0:T(8,128)(2,1)S(1)}, bf16[1152,128]{1,0:T(8,128)(2,1)S(1)}, u32[]{:S(2)}, u32[]{:S(2)}) collective-permute-start(bf16[1152,128]{1,0:T(8,128)(2,1)S(1)} %collective-permute-done.3.w2.rest_2_), channel_id=1, source_target_pairs={{0,4},{4,0},{8,12},{12,8},{16,20},{20,16},{24,28},{28,24},{32,36},... | collective-permute-start | bytes 884744 | tf_op jit(solution)/shard_map/ppermute | solution.py:23
  23.1 0.7 %copy-start.2 = (s32[16,192]{1,0:T(8,128)S(1)}, s32[16,192]{1,0:T(8,128)}, u32[]{:S(2)}) copy-start(s32[16,192]{1,0:T(8,128)} %get-tuple-element.25.aggl_ref) | copy-start | bytes 36868
  31.1 0.7 %copy-start.3 = (s32[16,128]{1,0:T(8,128)S(1)}, s32[16,128]{1,0:T(8,128)}, u32[]{:S(2)}) copy-start(s32[16,128]{1,0:T(8,128)} %get-tuple-element.23.aggr_ref) | copy-start | bytes 24580
  43.2 0.7 %copy-start.1 = (f32[480,96]{1,0:T(8,128)}, f32[480,96]{1,0:T(8,128)S(1)}, u32[]{:S(2)}) copy-start(f32[480,96]{1,0:T(8,128)S(1)} %get-tuple-element.34.mid_ref) | copy-start | bytes 552964
  43.9 1.5 %collective-permute-start.11 = (f32[480,96]{1,0:T(8,128)S(1)}, f32[480,96]{1,0:T(8,128)S(1)}, u32[]{:S(2)}, u32[]{:S(2)}) collective-permute-start(f32[480,96]{1,0:T(8,128)S(1)} %get-tuple-element.35), channel_id=1, source_target_pairs={{0,4},{4,0},{8,12},{12,8},{16,20},{20,16},{24,28},{28,24},{32,36},... | collective-permute-start | bytes 552968 | tf_op jit(solution)/shard_map/ppermute | solution.py:23
  43.9 8.9 %collective-permute-start.12 = (f32[480,96]{1,0:T(8,128)S(1)}, f32[480,96]{1,0:T(8,128)S(1)}, u32[]{:S(2)}, u32[]{:S(2)}) collective-permute-start(f32[480,96]{1,0:T(8,128)S(1)} %get-tuple-element.36), channel_id=1, source_target_pairs={{4,8},{8,4},{12,16},{16,12},{20,24},{24,20},{28,32},{32,28},{36,40... | collective-permute-start | bytes 552968 | tf_op jit(solution)/shard_map/ppermute | solution.py:35
  45.4 7.4 %copy-start.7 = (f32[480,96]{1,0:T(8,128)}, f32[480,96]{1,0:T(8,128)S(1)}, u32[]{:S(2)}) copy-start(f32[480,96]{1,0:T(8,128)S(1)} %collective-permute-done.11.chip_ref) | copy-start | bytes 552964
  55.5 4.7 %collective-permute-start.13 = (f32[168,96]{1,0:T(8,128)}, f32[168,96]{1,0:T(8,128)S(1)}, u32[]{:S(2)}, u32[]{:S(2)}) collective-permute-start(f32[168,96]{1,0:T(8,128)} %get-tuple-element.38), channel_id=1, source_target_pairs={{0,1},{1,2},{2,3},{3,0},{4,5},{5,6},{6,7},{7,4},{8,9},{9,10},{10,1... | collective-permute-start | bytes 193544 | tf_op jit(solution)/shard_map/ppermute | solution.py:18
  57.2 6.2 %collective-permute-start.14 = (f32[168,96]{1,0:T(8,128)}, f32[168,96]{1,0:T(8,128)S(1)}, u32[]{:S(2)}, u32[]{:S(2)}) collective-permute-start(f32[168,96]{1,0:T(8,128)} %get-tuple-element.39), channel_id=1, source_target_pairs={{0,2},{1,3},{2,0},{3,1},{4,6},{5,7},{6,4},{7,5},{8,10},{9,11},{10,... | collective-permute-start | bytes 193544 | tf_op jit(solution)/shard_map/ppermute | solution.py:18
  58.4 5.9 %collective-permute-start.15 = (f32[168,96]{1,0:T(8,128)}, f32[168,96]{1,0:T(8,128)S(1)}, u32[]{:S(2)}, u32[]{:S(2)}) collective-permute-start(f32[168,96]{1,0:T(8,128)} %get-tuple-element.40), channel_id=1, source_target_pairs={{0,3},{1,0},{2,1},{3,2},{4,7},{5,4},{6,5},{7,6},{8,11},{9,8},{10,9... | collective-permute-start | bytes 193544 | tf_op jit(solution)/shard_map/ppermute | solution.py:18
  (1 other events, 0.7 us)

commit v3 on v2

v3 whole, which is shorter than its diff:
```python
import jax
import jax.numpy as jnp
from jax import lax
from jax.experimental import pallas as pl
from jax.experimental.pallas import tpu as pltpu
from jax.sharding import PartitionSpec as P

MODES = 6
LANES = 128
PARTS = 4
BF = jnp.bfloat16
F32 = jnp.float32
I32 = jnp.int32


def around(x, by):
    length = lax.axis_size("cols")
    return lax.ppermute(x, "cols", [(i, (i + by) % length) for i in range(length)])


def swap_chip(x):
    length = lax.axis_size("rows")
    return lax.ppermute(x, "rows", [(i, i ^ 1) for i in range(length)])


def swap_cross(x):
    rows = lax.axis_size("rows")
    cols = lax.axis_size("cols")
    pairs = []
    for c in range(cols):
        for r in range(1, rows - 1, 2):
            pairs += [(r * cols + c, (r + 1) * cols + c), ((r + 1) * cols + c, r * cols + c)]
        for r in (0, rows - 1):
            pairs.append((r * cols + c, r * cols + (c ^ 1)))
    return lax.ppermute(x, ("rows", "cols"), pairs)


def dot(a, b, trans_b=False):
    return lax.dot_general(
        a, b, (((1,), (1 if trans_b else 0,)), ((), ())), preferred_element_type=F32
    )


def pack_kernel(q_ref, out_ref):
    blocks, rows, dofs = q_ref.shape
    half = blocks // 2
    groups = rows // MODES
    many = 4
    r = lax.broadcasted_iota(I32, (many * rows, many * rows), 0)
    c = lax.broadcasted_iota(I32, (many * rows, many * rows), 1)
    rl = r % rows
    perm = (r - rl) + (rl % groups) * MODES + rl // groups == c
    perm = jnp.where(perm, 1.0, 0.0).astype(BF)
    step = many * rows
    for n in range(half // many):
        a = dot(perm, q_ref[n * many : (n + 1) * many].reshape(step, dofs))
        b = dot(perm, q_ref[half + n * many : half + (n + 1) * many].reshape(step, dofs))
        lo = n * step
        out_ref[lo : lo + step, :] = a[:, :LANES].astype(BF)
        hi = half * rows + lo
        out_ref[hi : hi + step, :] = b[:, :LANES].astype(BF)
        mixed = jnp.concatenate([a[:, LANES:], b[:, LANES:]], axis=1)
        tail = blocks * rows + lo
        out_ref[tail : tail + step, :] = mixed.astype(BF)


def table_kernel(nbr_ref, aggs_ref, s_hbm, s_out, aggr_ref, aggl_ref, rel, ssem):
    slots, blocks = nbr_ref.shape
    copies = [pltpu.make_async_copy(s_hbm.at[i], s_out.at[i], ssem.at[i]) for i in range(blocks)]
    for cp in copies:
        cp.start()
    nagg, total = aggs_ref.shape
    groups = nagg // PARTS
    row = lax.axis_index("rows")
    col = lax.axis_index("cols")
    rel[...] = (aggs_ref[...] - (row - 2) * blocks).astype(F32)
    turned = []
    for d in range(PARTS):
        q = col + d
        q = jnp.where(q >= PARTS, q - PARTS, q)
        turned.append(rel[pl.ds(pl.multiple_of(q * groups, groups), groups), :])
    turned = jnp.concatenate(turned, axis=0).astype(BF)
    wanted = nbr_ref[...].T
    lane = lax.broadcasted_iota(I32, (blocks, total), 1)
    pieces = []
    for k in range(slots):
        hot = jnp.where(lane == wanted[:, k : k + 1], 1.0, 0.0).astype(BF)
        pieces.append(dot(hot, turned, True))
    aggr_ref[...] = jnp.concatenate(pieces, axis=1).astype(I32)
    sub = lax.broadcasted_iota(I32, (blocks, total), 0) + row * blocks
    own = dot(jnp.where(lane == sub, 1.0, 0.0).astype(BF), turned, True)
    src = lax.broadcasted_iota(I32, (nagg, MODES * nagg), 0)
    dst = lax.broadcasted_iota(I32, (nagg, MODES * nagg), 1)
    rows = MODES * groups
    spread = src == (dst // rows) * groups + dst % groups
    own = dot(own.astype(BF), jnp.where(spread, 1.0, 0.0).astype(BF)).astype(I32) - blocks
    mode = (lax.broadcasted_iota(I32, own.shape, 1) % rows) // groups
    aggl_ref[...] = (own // blocks) * LANES + (own % blocks) * MODES + mode
    for cp in copies:
        cp.wait()


def left_kernel(aggl_ref, w0, w1, w2, w3, lo_ref, hi_ref):
    blocks = aggl_ref.shape[0]
    half = blocks // 2
    rows = aggl_ref.shape[1] // PARTS
    first_half = lax.broadcasted_iota(I32, (3 * LANES, LANES), 1) < LANES // 2

    def placed(i):
        hot = lax.broadcasted_iota(I32, (3 * LANES, PARTS * rows), 0) == aggl_ref[i : i + 1, :]
        hot = jnp.where(hot, 1.0, 0.0).astype(BF)
        first = jnp.concatenate([w[i * rows : (i + 1) * rows] for w in (w0, w1, w2, w3)], axis=0)
        at = (blocks + i % half) * rows
        second = jnp.concatenate([w[at : at + rows] for w in (w0, w1, w2, w3)], axis=0)
        left = dot(hot, jnp.concatenate([first, second], axis=1))
        lo_ref[:, i * LANES : (i + 1) * LANES] = left[:, :LANES].astype(BF)
        return left[:, LANES:]

    for n in range(half):
        a = placed(n)
        b = placed(n + half)
        hi_ref[:, n * LANES : (n + 1) * LANES] = jnp.where(first_half, a, b).astype(BF)


def main_kernel(nbr_ref, live_ref, aggr_ref, lo_ref, hi_ref, s_ref, *rest):
    pieces = rest[: 3 * PARTS]
    chip_ref, mid_ref, cross_ref, wbuf, images, asm_lo, asm_hi, wsem = rest[3 * PARTS :]
    blocks, slots, dofs, _ = s_ref.shape
    half = blocks // 2
    quarter = pieces[0].shape[0]
    rows = quarter // (blocks + half)
    groups = rows // MODES
    reach = 5 * blocks
    chunk = slots * PARTS * groups
    row = lax.axis_index("rows")
    col = lax.axis_index("cols")
    copies = [
        pltpu.make_async_copy(p, wbuf.at[pl.ds(n * quarter, quarter)], wsem.at[n])
        for n, p in enumerate(pieces)
    ]
    for cp in copies:
        cp.start()
    zeros = jnp.zeros((dofs, 2 * LANES - dofs), BF)
    odd = row % 2
    for cp in copies:
        cp.wait()

    def image(i, k):
        j = nbr_ref[k, i] - (row - 1) * blocks
        w = j // blocks
        jl = j - w * blocks
        w = jnp.where(w == 1, 0, jnp.where((w == 2) == (odd == 0), 1, 2))
        place = w * PARTS * quarter
        jh = jnp.where(jl >= half, jl - half, jl)
        first = [
            wbuf[pl.ds(pl.multiple_of(place + d * quarter + jl * rows, 16), rows), :]
            for d in range(PARTS)
        ]
        second = [
            wbuf[pl.ds(pl.multiple_of(place + d * quarter + (blocks + jh) * rows, 16), rows), :]
            for d in range(PARTS)
        ]
        pj = jnp.concatenate(
            [jnp.concatenate(first, axis=0), jnp.concatenate(second, axis=0)], axis=1
        )
        s = s_ref[i, k]
        tail = s[:, LANES:]
        tail = jnp.where(
            jl < half,
            jnp.concatenate([tail, zeros], axis=1),
            jnp.concatenate([zeros, tail], axis=1),
        )
        return dot(pj, jnp.concatenate([s[:, :LANES], tail], axis=1), True)

    for i in range(blocks):
        parts = [image(i, k) for k in range(slots)]
        for m in range(MODES):
            images[i, m * chunk : (m + 1) * chunk] = jnp.concatenate(
                [
                    img[d * rows + m * groups : d * rows + (m + 1) * groups]
                    for img in parts
                    for d in range(PARTS)
                ],
                axis=0,
            ).astype(BF)

    lane = lax.broadcasted_iota(I32, (1, chunk), 1) // (PARTS * groups)

    def assemble(i):
        target = jnp.where(lane + col * slots < live_ref[i], aggr_ref[i : i + 1, :], -1)
        place_t = lax.broadcasted_iota(I32, (reach, chunk), 0) == target
        place_t = jnp.where(place_t, 1.0, 0.0).astype(BF)
        tails = []
        for m in range(MODES):
            asm = dot(place_t, images[i, m * chunk : (m + 1) * chunk])
            asm_lo[m * reach : (m + 1) * reach, i * LANES : (i + 1) * LANES] = asm[
                :, :LANES
            ].astype(BF)
            tails.append(asm[:, LANES:].astype(BF))
        return tails

    for n in range(half):
        a = assemble(n)
        b = assemble(n + half)
        for m in range(MODES):
            asm_hi[m * reach : (m + 1) * reach, n * LANES : (n + 1) * LANES] = jnp.concatenate(
                [a[m], b[m]], axis=1
            )
    acc = dot(asm_lo[...], lo_ref[...], True) + dot(asm_hi[...], hi_ref[...], True)
    width = mid_ref.shape[1]
    even = odd == 0
    low = acc[:, :width]
    up = acc[:, 2 * LANES : 2 * LANES + width]
    chip_ref[...] = jnp.where(even, up, low)
    mid_ref[...] = acc[:, LANES : LANES + width]
    cross_ref[...] = jnp.where(even, low, up).astype(BF)


def share_kernel(mid_ref, chip_ref, cross_ref, o0, o1, o2, o3, tot):
    reach = mid_ref.shape[0] // MODES
    band = 7 * reach // 5
    blocks = band // 7
    piece = o0.shape[0]
    padded = o1.shape[0]
    width = tot.shape[1]

    def zeros(n):
        return jnp.zeros((n * blocks, width), F32)

    even = lax.axis_index("rows") % 2 == 0
    for m in range(MODES):
        src = slice(m * reach, (m + 1) * reach)
        chip = chip_ref[src]
        cross = cross_ref[src].astype(F32)
        above = jnp.where(even, chip, cross)
        below = jnp.where(even, cross, chip)
        tot[m * band : (m + 1) * band] = (
            jnp.concatenate([zeros(1), mid_ref[src], zeros(1)], axis=0)
            + jnp.concatenate([zeros(2), above], axis=0)
            + jnp.concatenate([below, zeros(2)], axis=0)
        )
    tot[MODES * band :] = jnp.zeros((padded - piece, width), F32)
    for d, o in enumerate((o0, o1, o2, o3)):
        c = lax.axis_index("cols") + d
        c = jnp.where(c >= PARTS, c - PARTS, c)
        o[...] = tot[pl.ds(pl.multiple_of(c * piece, 8), o.shape[0]), :].astype(o.dtype)


def on_device(stiffness, neighbors, live_counts, prolong, prolong_aggs):
    blocks, slots, dofs, _ = stiffness.shape
    rows = prolong.shape[1]
    nagg = prolong_aggs.shape[1]
    quarter = (blocks + blocks // 2) * rows
    vmem = pl.BlockSpec(memory_space=pltpu.VMEM)
    smem = pl.BlockSpec(memory_space=pltpu.SMEM)
    any_ = pl.BlockSpec(memory_space=pl.ANY)
    hbm = pl.BlockSpec(memory_space=pltpu.HBM)
    nbr = neighbors.T

    w0 = pl.pallas_call(
        pack_kernel,
        out_shape=jax.ShapeDtypeStruct((quarter, LANES), BF),
        in_specs=[vmem],
        out_specs=vmem,
        compiler_params=pltpu.CompilerParams(vmem_limit_bytes=8 * 2**20),
    )(prolong)
    w1 = around(w0, -1)
    w3 = around(w0, 1)
    b0 = swap_cross(w0)
    a0 = swap_chip(w0)
    aggs, a0 = lax.optimization_barrier((prolong_aggs.T, a0))
    w2 = around(w0, 2)

    s_near, aggr, aggl = pl.pallas_call(
        table_kernel,
        out_shape=[
            pltpu.VMEM(stiffness.shape, BF),
            pltpu.VMEM((blocks, slots * nagg), I32),
            pltpu.VMEM((blocks, MODES * nagg), I32),
        ],
        in_specs=[vmem, vmem, hbm],
        out_specs=[vmem] * 3,
        scratch_shapes=[
            pltpu.VMEM((nagg, prolong_aggs.shape[0]), F32),
            pltpu.SemaphoreType.DMA((blocks,)),
        ],
        compiler_params=pltpu.CompilerParams(vmem_limit_bytes=50 * 2**20),
    )(nbr, aggs, stiffness)
    w1, w3, aggl = lax.optimization_barrier((w1, w3, aggl))

    b1 = around(b0, -1)
    b3 = around(b0, 1)
    a1 = swap_chip(w1)
    a3 = swap_chip(w3)
    b2 = swap_cross(w2)
    a2 = swap_chip(w2)

    left_lo, left_hi = pl.pallas_call(
        left_kernel,
        out_shape=[
            pltpu.VMEM((3 * LANES, blocks * LANES), BF),
            pltpu.VMEM((3 * LANES, blocks * LANES // 2), BF),
        ],
        in_specs=[vmem] * 5,
        out_specs=[vmem] * 2,
        compiler_params=pltpu.CompilerParams(vmem_limit_bytes=16 * 2**20),
    )(aggl, w0, w1, w2, w3)

    reach = 5 * blocks
    out = jax.ShapeDtypeStruct((MODES * reach, blocks * MODES), F32)
    to_chip, mid, to_cross = pl.pallas_call(
        main_kernel,
        out_shape=[out, out, jax.ShapeDtypeStruct(out.shape, BF)],
        in_specs=[smem, smem, vmem, vmem, vmem, vmem] + [any_] * 12,
        out_specs=[vmem] * 3,
        scratch_shapes=[
            pltpu.VMEM((3 * PARTS * quarter, LANES), BF),
            pltpu.VMEM((blocks, slots * MODES * nagg, dofs), BF),
            pltpu.VMEM((MODES * reach, blocks * LANES), BF),
            pltpu.VMEM((MODES * reach, blocks * LANES // 2), BF),
            pltpu.SemaphoreType.DMA((3 * PARTS,)),
        ],
        compiler_params=pltpu.CompilerParams(vmem_limit_bytes=24 * 2**20),
    )(nbr, live_counts, aggr, left_lo, left_hi, s_near, w0, w1, w2, w3, a0, a1, a2, a3, b0, b1, b2, b3)
    from_cross = swap_cross(to_cross)
    from_chip = swap_chip(to_chip)
    piece = MODES * 7 * blocks // PARTS
    padded = -(-piece // 16) * 16
    sh = jax.ShapeDtypeStruct((padded, blocks * MODES), BF)
    s0, s1, s2, s3 = pl.pallas_call(
        share_kernel,
        out_shape=[jax.ShapeDtypeStruct((piece, blocks * MODES), F32), sh, sh, sh],
        in_specs=[vmem] * 3,
        out_specs=[vmem] * 4,
        scratch_shapes=[pltpu.VMEM((PARTS * piece + padded - piece, blocks * MODES), F32)],
        compiler_params=pltpu.CompilerParams(vmem_limit_bytes=8 * 2**20),
    )(mid, from_chip, from_cross)
    t1 = around(s1, 1)
    t3 = around(s3, -1)
    t2 = around(s2, 2)
    t1, t2, t3 = (t[:piece].astype(F32) for t in (t1, t2, t3))
    return ((s0 + t1) + (t2 + t3)).T


def solution(mesh):
    in_specs = (
        P("rows", "cols", None, None),
        P("rows", "cols"),
        P("rows"),
        P("rows", "cols", None),
        P(),
    )
    out_specs = P("rows", "cols")
    return jax.shard_map(
        on_device, mesh=mesh, in_specs=in_specs, out_specs=out_specs, check_vma=False
    )
```

time: 66.2 us -> 54.5 us (0.82)
  Pallas kernels: 21.1 us -> 11.5 us
  waiting for transfers between devices: 23 us -> 25.3 us
  local copies, waits for them, and re-layouts: 2.8 us -> 1 us
  other arithmetic: 2.2 us -> 0.66 us
  starting transfers between devices: 16.7 us -> 15.3 us
    pallas_call x3, Pallas kernels: 14.4 us -> 7.18 us  [the longest x1 6.12 us: on_device(): pl.pallas_call(main_kernel, out_shape=[out, out, jax.ShapeDtypeStruct(out...]
    ppermute x6 -> x8, waiting for transfers between devices: 9.42 us -> 16.6 us  [around(): lax.ppermute(x, 'cols', [(i, (i + by) % length) for i in range(length)])]
    ppermute x5 -> x3, waiting for transfers between devices: 13.5 us -> 8.71 us  [swap_cross(): return lax.ppermute(x, ('rows', 'cols'), pairs)]
    ppermute x5 -> x3, starting transfers between devices: 10.3 us -> 8.19 us  [swap_cross(): return lax.ppermute(x, ('rows', 'cols'), pairs)]
    unnamed x18 -> x6, local copies, waits for them, and re-layouts: 2.8 us -> 1 us
    pallas_call x1, Pallas kernels: 2.11 us -> 0.38 us  [on_device(): pl.pallas_call(pack_kernel, out_shape=jax.ShapeDtypeStruct((quarter, LANE...]
    transpose x1, other arithmetic: 1.55 us -> 0.66 us  [on_device(): return (s0 + t1 + (t2 + t3)).T]
    ppermute x6 -> x8, starting transfers between devices: 6.42 us -> 7.02 us  [around(): lax.ppermute(x, 'cols', [(i, (i + by) % length) for i in range(length)])]
  transfers between devices with their start and end apart: 16 -> 16, of which waited for: 8 -> 8; matrix products, arithmetic and copies ran while one was open for 1% -> 0% of each run, Pallas kernels for 8% -> 9%
where the time goes in v3:
time: 54.5 us; the launch traced here: 53.9 us
  waiting for transfers between devices  25.3 us (46%)
  starting transfers between devices  15.3 us (28%)
  Pallas kernels  11.5 us (21%)
  local copies, waits for them, and re-layouts  1 us (2%)
  other arithmetic  0.66 us (1%)
    ppermute x8, waiting for transfers between devices, around(): lax.ppermute(x, 'cols', [(i, (i + by) % length) for i in range(length)])  16.6 us
    ppermute x3, waiting for transfers between devices, swap_cross(): return lax.ppermute(x, ('rows', 'cols'), pairs)  8.71 us
    ppermute x3, starting transfers between devices, swap_cross(): return lax.ppermute(x, ('rows', 'cols'), pairs)  8.19 us
    ppermute x8, starting transfers between devices, around(): lax.ppermute(x, 'cols', [(i, (i + by) % length) for i in range(length)])  7.02 us
    pallas_call x1, Pallas kernels, on_device(): pl.pallas_call(main_kernel, out_shape=[out, out, jax.ShapeDtypeStruct(out...  6.12 us
    pallas_call x1, Pallas kernels, on_device(): pl.pallas_call(table_kernel, out_shape=[pltpu.VMEM(stiffness.shape, BF),...  3.92 us
  transfers between devices with their start and end apart: 16, of which 8 were waited for; matrix products, arithmetic and copies ran while one was open for 0% of the time, Pallas kernels for 9%

profile of v3, /device:TPU:134, one launch (start us, length us, event | category | flops | bytes accessed | tf_op | source)
XLA Modules:
  0.0 53.9 jit_solution(2238954326291280939)
XLA Ops:
  0.0 1.0 %copy-done = bf16[16,48,192]{2,1,0:T(8,128)(2,1)S(1)} copy-done((bf16[16,48,192]{2,1,0:T(8,128)(2,1)S(1)}, bf16[16,48,192]{2,1,0:T(8,128)(2,1)}, u32[]{:S(2)}) %copy-start) | copy-done | bytes 294936
  1.0 0.4 shard_map.55.w0.rest_0_
  1.4 2.1 %collective-permute-start.7 = (bf16[1152,128]{1,0:T(8,128)(2,1)S(1)}, bf16[1152,128]{1,0:T(8,128)(2,1)S(1)}, u32[]{:S(2)}, u32[]{:S(2)}) collective-permute-start(bf16[1152,128]{1,0:T(8,128)(2,1)S(1)} %shard_map.55.w0.rest_0_), channel_id=1, source_target_pairs={{4,8},{8,4},{12,16},{16,12},{20,24},{24,20},{28,32},{32,28},{36,40... | collective-permute-start | bytes 884744 | tf_op jit(solution)/shard_map/ppermute | solution.py:35
  3.5 0.5 collective-permute-start.2
  4.0 1.5 %collective-permute-start.1 = (bf16[1152,128]{1,0:T(8,128)(2,1)S(1)}, bf16[1152,128]{1,0:T(8,128)(2,1)S(1)}, u32[]{:S(2)}, u32[]{:S(2)}) collective-permute-start(bf16[1152,128]{1,0:T(8,128)(2,1)S(1)} %shard_map.55.w0.rest_0_), channel_id=1, source_target_pairs={{0,3},{1,0},{2,1},{3,2},{4,7},{5,4},{6,5},{7,6},{8,11},{9,8},{10,9... | collective-permute-start | bytes 884744 | tf_op jit(solution)/shard_map/ppermute | solution.py:18
  5.5 1.4 %collective-permute-start.3 = (bf16[1152,128]{1,0:T(8,128)(2,1)S(1)}, bf16[1152,128]{1,0:T(8,128)(2,1)S(1)}, u32[]{:S(2)}, u32[]{:S(2)}) collective-permute-start(bf16[1152,128]{1,0:T(8,128)(2,1)S(1)} %shard_map.55.w0.rest_0_), channel_id=1, source_target_pairs={{0,2},{1,3},{2,0},{3,1},{4,6},{5,7},{6,4},{7,5},{8,10},{9,11},{10,... | collective-permute-start | bytes 884744 | tf_op jit(solution)/shard_map/ppermute | solution.py:18
  6.9 4.0 %collective-permute-done.7.rest_8_ = bf16[1152,128]{1,0:T(8,128)(2,1)S(1)} collective-permute-done((bf16[1152,128]{1,0:T(8,128)(2,1)S(1)}, bf16[1152,128]{1,0:T(8,128)(2,1)S(1)}, u32[]{:S(2)}, u32[]{:S(2)}) %collective-permute-start.7) | collective-permute-done | bytes 294944 | tf_op jit(solution)/shard_map/ppermute | solution.py:35
  10.9 0.5 collective-permute-start.10
  11.4 3.9 %shard_map.56 = (bf16[16,4,192,192]{3,2,1,0:T(8,128)(2,1)S(1)}, s32[16,128]{1,0:T(8,128)S(1)}, s32[16,192]{1,0:T(8,128)S(1)}) custom-call(s32[4,16]{1,0:T(4,128)} %bitcast.4, s32[32,1024]{1,0:T(8,128)} %bitcast.6, bf16[16,4,192,192]{3,2,1,0:T(8,128)(2,1)} %s_hbm.1), custom_call_target="tpu_custom_call" | custom-call | tf_op jit(solution)/shard_map/pallas_call | solution.py:274
  15.4 5.3 %collective-permute-done.1.w1.rest_1_ = bf16[1152,128]{1,0:T(8,128)(2,1)S(1)} collective-permute-done((bf16[1152,128]{1,0:T(8,128)(2,1)S(1)}, bf16[1152,128]{1,0:T(8,128)(2,1)S(1)}, u32[]{:S(2)}, u32[]{:S(2)}) %collective-permute-start.1) | collective-permute-done | bytes 294944 | tf_op jit(solution)/shard_map/ppermute | solution.py:18
  20.6 3.1 %collective-permute-start.9 = (bf16[1152,128]{1,0:T(8,128)(2,1)S(1)}, bf16[1152,128]{1,0:T(8,128)(2,1)S(1)}, u32[]{:S(2)}, u32[]{:S(2)}) collective-permute-start(bf16[1152,128]{1,0:T(8,128)(2,1)S(1)} %collective-permute-done.3.w2.rest_2_), channel_id=1, source_target_pairs={{4,8},{8,4},{12,16},{16,12},{20,24},{24,20},{28,32},{32,28},{36,40... | collective-permute-start | bytes 884744 | tf_op jit(solution)/shard_map/ppermute | solution.py:35
  23.7 1.9 %collective-permute-done.10.rest_11_ = bf16[1152,128]{1,0:T(8,128)(2,1)S(1)} collective-permute-done((bf16[1152,128]{1,0:T(8,128)(2,1)S(1)}, bf16[1152,128]{1,0:T(8,128)(2,1)S(1)}, u32[]{:S(2)}, u32[]{:S(2)}) %collective-permute-start.10) | collective-permute-done | bytes 294944 | tf_op jit(solution)/shard_map/ppermute | solution.py:18
  25.6 1.0 %shard_map.57 = (bf16[384,2048]{1,0:T(8,128)(2,1)S(1)}, bf16[384,1024]{1,0:T(8,128)(2,1)S(1)}) custom-call(s32[16,192]{1,0:T(8,128)S(1)} %get-tuple-element.25.aggl_ref, bf16[1152,128]{1,0:T(8,128)(2,1)S(1)} %shard_map.55.w0.rest_0_, bf16[1152,128]{1,0:T(8,128)(2,1)S(1)} %collective-permute-done.1.w1.rest_1_, ...), custom_call_target="tpu_custom_call" | custom-call | tf_op jit(solution)/shard_map/pallas_call | solution.py:298
  26.6 4.7 %collective-permute-done.8.rest_9_ = bf16[1152,128]{1,0:T(8,128)(2,1)S(1)} collective-permute-done((bf16[1152,128]{1,0:T(8,128)(2,1)S(1)}, bf16[1152,128]{1,0:T(8,128)(2,1)S(1)}, u32[]{:S(2)}, u32[]{:S(2)}) %collective-permute-start.8) | collective-permute-done | bytes 294944 | tf_op jit(solution)/shard_map/ppermute | solution.py:18
  31.3 6.1 %shard_map.58 = (f32[480,96]{1,0:T(8,128)S(1)}, f32[480,96]{1,0:T(8,128)S(1)}, bf16[480,96]{1,0:T(8,128)(2,1)S(1)}) custom-call(s32[4,16]{1,0:T(4,128)S(1)} %bitcast.5, s32[16]{0:T(128)S(1)} %copy-done.2, s32[16,128]{1,0:T(8,128)S(1)} %get-tuple-element.23.aggr_ref, bf16[384,2048]{1,0:T(8,128)(2,1)S(1)} %get-tuple-element.28.lo_ref, ...), custom_call_target="tpu_custom_call" | custom-call | tf_op jit(solution)/shard_map/pallas_call | solution.py:311
  37.4 0.1 collective-permute-start.11
  37.5 3.0 %collective-permute-start.12 = (bf16[480,96]{1,0:T(8,128)(2,1)S(1)}, bf16[480,96]{1,0:T(8,128)(2,1)S(1)}, u32[]{:S(2)}, u32[]{:S(2)}) collective-permute-start(bf16[480,96]{1,0:T(8,128)(2,1)S(1)} %get-tuple-element.34), channel_id=1, source_target_pairs={{4,8},{8,4},{12,16},{16,12},{20,24},{24,20},{28,32},{32,28},{36,40... | collective-permute-start | bytes 276488 | tf_op jit(solution)/shard_map/ppermute | solution.py:35
  40.6 4.7 %collective-permute-done.12.cross_ref = bf16[480,96]{1,0:T(8,128)(2,1)S(1)} collective-permute-done((bf16[480,96]{1,0:T(8,128)(2,1)S(1)}, bf16[480,96]{1,0:T(8,128)(2,1)S(1)}, u32[]{:S(2)}, u32[]{:S(2)}) %collective-permute-start.12) | collective-permute-done | bytes 92192 | tf_op jit(solution)/shard_map/ppermute | solution.py:35
  45.3 2.2 %collective-permute-start.13 = (bf16[176,96]{1,0:T(8,128)(2,1)S(1)}, bf16[176,96]{1,0:T(8,128)(2,1)S(1)}, u32[]{:S(2)}, u32[]{:S(2)}) collective-permute-start(bf16[176,96]{1,0:T(8,128)(2,1)S(1)} %get-tuple-element.36), channel_id=1, source_target_pairs={{0,1},{1,2},{2,3},{3,0},{4,5},{5,6},{6,7},{7,4},{8,9},{9,10},{10,1... | collective-permute-start | bytes 101384 | tf_op jit(solution)/shard_map/ppermute | solution.py:18
  47.5 1.0 %collective-permute-start.15 = (bf16[176,96]{1,0:T(8,128)(2,1)S(1)}, bf16[176,96]{1,0:T(8,128)(2,1)S(1)}, u32[]{:S(2)}, u32[]{:S(2)}) collective-permute-start(bf16[176,96]{1,0:T(8,128)(2,1)S(1)} %get-tuple-element.38), channel_id=1, source_target_pairs={{0,3},{1,0},{2,1},{3,2},{4,7},{5,4},{6,5},{7,6},{8,11},{9,8},{10,9... | collective-permute-start | bytes 101384 | tf_op jit(solution)/shard_map/ppermute | solution.py:18
  48.4 1.0 %collective-permute-done.13 = bf16[176,96]{1,0:T(8,128)(2,1)S(1)} collective-permute-done((bf16[176,96]{1,0:T(8,128)(2,1)S(1)}, bf16[176,96]{1,0:T(8,128)(2,1)S(1)}, u32[]{:S(2)}, u32[]{:S(2)}) %collective-permute-start.13) | collective-permute-done | bytes 33824 | tf_op jit(solution)/shard_map/ppermute | solution.py:18
  49.5 3.7 %collective-permute-done.14 = bf16[176,96]{1,0:T(8,128)(2,1)S(1)} collective-permute-done((bf16[176,96]{1,0:T(8,128)(2,1)S(1)}, bf16[176,96]{1,0:T(8,128)(2,1)S(1)}, u32[]{:S(2)}, u32[]{:S(2)}) %collective-permute-start.14) | collective-permute-done | bytes 33824 | tf_op jit(solution)/shard_map/ppermute | solution.py:18
  53.1 0.1 collective-permute-done.15
  53.2 0.7 %add_bitcast_fusion = f32[96,168]{0,1:T(8,128)} fusion(f32[168,96]{1,0:T(8,128)S(1)} %get-tuple-element.35, bf16[176,96]{1,0:T(8,128)(2,1)S(1)} %collective-permute-done.15, bf16[176,96]{1,0:T(8,128)(2,1)S(1)} %collective-permute-done.14, bf16[176,96]{1,0:T(8,128)(2,1)S(1)} %collective-permute-done.13), kind=kLoop, calls=%fused_computation | loop fusion | flops 96768 | bytes 225792 | tf_op jit(solution)/shard_map/transpose | solution.py:342
  (20 shorter events, 0.1 us)
Async XLA Ops:
  0.0 1.0 %copy-start = (bf16[16,48,192]{2,1,0:T(8,128)(2,1)S(1)}, bf16[16,48,192]{2,1,0:T(8,128)(2,1)}, u32[]{:S(2)}) copy-start(bf16[16,48,192]{2,1,0:T(8,128)(2,1)} %q_ref.1) | copy-start | bytes 884740
  1.0 30.3 %copy-start.1 = (s32[16,4]{0,1:T(4,128)S(1)}, s32[16,4]{0,1:T(4,128)}, u32[]{:S(2)}) copy-start(s32[16,4]{0,1:T(4,128)} %param.6) | copy-start | bytes 772
  1.0 30.3 %copy-start.2 = (s32[16]{0:T(128)S(1)}, s32[16]{0:T(128)}, u32[]{:S(2)}) copy-start(s32[16]{0:T(128)} %live_ref.1) | copy-start | bytes 196
  1.4 9.6 %collective-permute-start.7 = (bf16[1152,128]{1,0:T(8,128)(2,1)S(1)}, bf16[1152,128]{1,0:T(8,128)(2,1)S(1)}, u32[]{:S(2)}, u32[]{:S(2)}) collective-permute-start(bf16[1152,128]{1,0:T(8,128)(2,1)S(1)} %shard_map.55.w0.rest_0_), channel_id=1, source_target_pairs={{4,8},{8,4},{12,16},{16,12},{20,24},{24,20},{28,32},{32,28},{36,40... | collective-permute-start | bytes 884744 | tf_op jit(solution)/shard_map/ppermute | solution.py:35
  3.5 8.0 %collective-permute-start = (bf16[1152,128]{1,0:T(8,128)(2,1)S(1)}, bf16[1152,128]{1,0:T(8,128)(2,1)S(1)}, u32[]{:S(2)}, u32[]{:S(2)}) collective-permute-start(bf16[1152,128]{1,0:T(8,128)(2,1)S(1)} %shard_map.55.w0.rest_0_), channel_id=1, source_target_pairs={{0,4},{4,0},{8,12},{12,8},{16,20},{20,16},{24,28},{28,24},{32,36},... | collective-permute-start | bytes 884744 | tf_op jit(solution)/shard_map/ppermute | solution.py:23
  3.5 11.9 %collective-permute-start.2 = (bf16[1152,128]{1,0:T(8,128)(2,1)S(1)}, bf16[1152,128]{1,0:T(8,128)(2,1)S(1)}, u32[]{:S(2)}, u32[]{:S(2)}) collective-permute-start(bf16[1152,128]{1,0:T(8,128)(2,1)S(1)} %shard_map.55.w0.rest_0_), channel_id=1, source_target_pairs={{0,1},{1,2},{2,3},{3,0},{4,5},{5,6},{6,7},{7,4},{8,9},{9,10},{10,1... | collective-permute-start | bytes 884744 | tf_op jit(solution)/shard_map/ppermute | solution.py:18
  4.0 16.7 %collective-permute-start.1 = (bf16[1152,128]{1,0:T(8,128)(2,1)S(1)}, bf16[1152,128]{1,0:T(8,128)(2,1)S(1)}, u32[]{:S(2)}, u32[]{:S(2)}) collective-permute-start(bf16[1152,128]{1,0:T(8,128)(2,1)S(1)} %shard_map.55.w0.rest_0_), channel_id=1, source_target_pairs={{0,3},{1,0},{2,1},{3,2},{4,7},{5,4},{6,5},{7,6},{8,11},{9,8},{10,9... | collective-permute-start | bytes 884744 | tf_op jit(solution)/shard_map/ppermute | solution.py:18
  5.5 15.1 %collective-permute-start.3 = (bf16[1152,128]{1,0:T(8,128)(2,1)S(1)}, bf16[1152,128]{1,0:T(8,128)(2,1)S(1)}, u32[]{:S(2)}, u32[]{:S(2)}) collective-permute-start(bf16[1152,128]{1,0:T(8,128)(2,1)S(1)} %shard_map.55.w0.rest_0_), channel_id=1, source_target_pairs={{0,2},{1,3},{2,0},{3,1},{4,6},{5,7},{6,4},{7,5},{8,10},{9,11},{10,... | collective-permute-start | bytes 884744 | tf_op jit(solution)/shard_map/ppermute | solution.py:18
  10.9 14.6 %collective-permute-start.10 = (bf16[1152,128]{1,0:T(8,128)(2,1)S(1)}, bf16[1152,128]{1,0:T(8,128)(2,1)S(1)}, u32[]{:S(2)}, u32[]{:S(2)}) collective-permute-start(bf16[1152,128]{1,0:T(8,128)(2,1)S(1)} %collective-permute-done.7.rest_8_), channel_id=1, source_target_pairs={{0,1},{1,2},{2,3},{3,0},{4,5},{5,6},{6,7},{7,4},{8,9},{9,10},{10,1... | collective-permute-start | bytes 884744 | tf_op jit(solution)/shard_map/ppermute | solution.py:18
  20.6 10.6 %collective-permute-start.4 = (bf16[1152,128]{1,0:T(8,128)(2,1)S(1)}, bf16[1152,128]{1,0:T(8,128)(2,1)S(1)}, u32[]{:S(2)}, u32[]{:S(2)}) collective-permute-start(bf16[1152,128]{1,0:T(8,128)(2,1)S(1)} %collective-permute-done.1.w1.rest_1_), channel_id=1, source_target_pairs={{0,4},{4,0},{8,12},{12,8},{16,20},{20,16},{24,28},{28,24},{32,36},... | collective-permute-start | bytes 884744 | tf_op jit(solution)/shard_map/ppermute | solution.py:23
  20.6 10.6 %collective-permute-start.8 = (bf16[1152,128]{1,0:T(8,128)(2,1)S(1)}, bf16[1152,128]{1,0:T(8,128)(2,1)S(1)}, u32[]{:S(2)}, u32[]{:S(2)}) collective-permute-start(bf16[1152,128]{1,0:T(8,128)(2,1)S(1)} %collective-permute-done.7.rest_8_), channel_id=1, source_target_pairs={{0,3},{1,0},{2,1},{3,2},{4,7},{5,4},{6,5},{7,6},{8,11},{9,8},{10,9... | collective-permute-start | bytes 884744 | tf_op jit(solution)/shard_map/ppermute | solution.py:18
  20.6 10.6 %collective-permute-start.9 = (bf16[1152,128]{1,0:T(8,128)(2,1)S(1)}, bf16[1152,128]{1,0:T(8,128)(2,1)S(1)}, u32[]{:S(2)}, u32[]{:S(2)}) collective-permute-start(bf16[1152,128]{1,0:T(8,128)(2,1)S(1)} %collective-permute-done.3.w2.rest_2_), channel_id=1, source_target_pairs={{4,8},{8,4},{12,16},{16,12},{20,24},{24,20},{28,32},{32,28},{36,40... | collective-permute-start | bytes 884744 | tf_op jit(solution)/shard_map/ppermute | solution.py:35
  23.7 7.6 %collective-permute-start.5 = (bf16[1152,128]{1,0:T(8,128)(2,1)S(1)}, bf16[1152,128]{1,0:T(8,128)(2,1)S(1)}, u32[]{:S(2)}, u32[]{:S(2)}) collective-permute-start(bf16[1152,128]{1,0:T(8,128)(2,1)S(1)} %collective-permute-done.3.w2.rest_2_), channel_id=1, source_target_pairs={{0,4},{4,0},{8,12},{12,8},{16,20},{20,16},{24,28},{28,24},{32,36},... | collective-permute-start | bytes 884744 | tf_op jit(solution)/shard_map/ppermute | solution.py:23
  25.6 5.7 %collective-permute-start.6 = (bf16[1152,128]{1,0:T(8,128)(2,1)S(1)}, bf16[1152,128]{1,0:T(8,128)(2,1)S(1)}, u32[]{:S(2)}, u32[]{:S(2)}) collective-permute-start(bf16[1152,128]{1,0:T(8,128)(2,1)S(1)} %collective-permute-done.2.w3.rest_3_), channel_id=1, source_target_pairs={{0,4},{4,0},{8,12},{12,8},{16,20},{20,16},{24,28},{28,24},{32,36},... | collective-permute-start | bytes 884744 | tf_op jit(solution)/shard_map/ppermute | solution.py:23
  37.4 7.8 %collective-permute-start.11 = (f32[480,96]{1,0:T(8,128)S(1)}, f32[480,96]{1,0:T(8,128)S(1)}, u32[]{:S(2)}, u32[]{:S(2)}) collective-permute-start(f32[480,96]{1,0:T(8,128)S(1)} %get-tuple-element.33), channel_id=1, source_target_pairs={{0,4},{4,0},{8,12},{12,8},{16,20},{20,16},{24,28},{28,24},{32,36},... | collective-permute-start | bytes 552968 | tf_op jit(solution)/shard_map/ppermute | solution.py:23
  37.5 7.7 %collective-permute-start.12 = (bf16[480,96]{1,0:T(8,128)(2,1)S(1)}, bf16[480,96]{1,0:T(8,128)(2,1)S(1)}, u32[]{:S(2)}, u32[]{:S(2)}) collective-permute-start(bf16[480,96]{1,0:T(8,128)(2,1)S(1)} %get-tuple-element.34), channel_id=1, source_target_pairs={{4,8},{8,4},{12,16},{16,12},{20,24},{24,20},{28,32},{32,28},{36,40... | collective-permute-start | bytes 276488 | tf_op jit(solution)/shard_map/ppermute | solution.py:35
  45.3 4.1 %collective-permute-start.13 = (bf16[176,96]{1,0:T(8,128)(2,1)S(1)}, bf16[176,96]{1,0:T(8,128)(2,1)S(1)}, u32[]{:S(2)}, u32[]{:S(2)}) collective-permute-start(bf16[176,96]{1,0:T(8,128)(2,1)S(1)} %get-tuple-element.36), channel_id=1, source_target_pairs={{0,1},{1,2},{2,3},{3,0},{4,5},{5,6},{6,7},{7,4},{8,9},{9,10},{10,1... | collective-permute-start | bytes 101384 | tf_op jit(solution)/shard_map/ppermute | solution.py:18
  47.5 5.7 %collective-permute-start.14 = (bf16[176,96]{1,0:T(8,128)(2,1)S(1)}, bf16[176,96]{1,0:T(8,128)(2,1)S(1)}, u32[]{:S(2)}, u32[]{:S(2)}) collective-permute-start(bf16[176,96]{1,0:T(8,128)(2,1)S(1)} %get-tuple-element.37), channel_id=1, source_target_pairs={{0,2},{1,3},{2,0},{3,1},{4,6},{5,7},{6,4},{7,5},{8,10},{9,11},{10,... | collective-permute-start | bytes 101384 | tf_op jit(solution)/shard_map/ppermute | solution.py:18
  47.5 5.7 %collective-permute-start.15 = (bf16[176,96]{1,0:T(8,128)(2,1)S(1)}, bf16[176,96]{1,0:T(8,128)(2,1)S(1)}, u32[]{:S(2)}, u32[]{:S(2)}) collective-permute-start(bf16[176,96]{1,0:T(8,128)(2,1)S(1)} %get-tuple-element.38), channel_id=1, source_target_pairs={{0,3},{1,0},{2,1},{3,2},{4,7},{5,4},{6,5},{7,6},{8,11},{9,8},{10,9... | collective-permute-start | bytes 101384 | tf_op jit(solution)/shard_map/ppermute | solution.py:18

commit v4 on v3

--- a/solution.py
+++ b/solution.py
@@ -264,12 +264,11 @@
         out_specs=vmem,
         compiler_params=pltpu.CompilerParams(vmem_limit_bytes=8 * 2**20),
     )(prolong)
+    w2 = around(w0, 2)
     w1 = around(w0, -1)
     w3 = around(w0, 1)
     b0 = swap_cross(w0)
-    a0 = swap_chip(w0)
-    aggs, a0 = lax.optimization_barrier((prolong_aggs.T, a0))
-    w2 = around(w0, 2)
+    aggs, b0 = lax.optimization_barrier((prolong_aggs.T, b0))
 
     s_near, aggr, aggl = pl.pallas_call(
         table_kernel,
@@ -286,14 +285,13 @@
         ],
         compiler_params=pltpu.CompilerParams(vmem_limit_bytes=50 * 2**20),
     )(nbr, aggs, stiffness)
-    w1, w3, aggl = lax.optimization_barrier((w1, w3, aggl))
+    w2, aggl = lax.optimization_barrier((w2, aggl))
 
     b1 = around(b0, -1)
     b3 = around(b0, 1)
-    a1 = swap_chip(w1)
-    a3 = swap_chip(w3)
     b2 = swap_cross(w2)
-    a2 = swap_chip(w2)
+    q1, q3, b1 = lax.optimization_barrier((w1, w3, b1))
+    a0, a1, a2, a3 = (swap_chip(q) for q in (w0, q1, w2, q3))
 
     left_lo, left_hi = pl.pallas_call(
         left_kernel,

time: 54.5 us -> 52 us (0.954)
  waiting for transfers between devices: 25.3 us -> 21.2 us
  starting transfers between devices: 15.3 us -> 17.4 us
    ppermute x8, waiting for transfers between devices: 16.6 us -> 11.1 us  [around(): lax.ppermute(x, 'cols', [(i, (i + by) % length) for i in range(length)])]
    ppermute x8, starting transfers between devices: 7.02 us -> 11.2 us  [around(): lax.ppermute(x, 'cols', [(i, (i + by) % length) for i in range(length)])]
    ppermute x3, starting transfers between devices: 8.19 us -> 5.44 us  [swap_cross(): return lax.ppermute(x, ('rows', 'cols'), pairs)]
    ppermute x3, waiting for transfers between devices: 8.71 us -> 9.68 us  [swap_cross(): return lax.ppermute(x, ('rows', 'cols'), pairs)]
    ppermute x5, starting transfers between devices: 0.1 us -> 0.73 us  [swap_chip(): return lax.ppermute(x, 'rows', [(i, i ^ 1) for i in range(length)])]
where the time goes in v4:
time: 52 us; the launch traced here: 51.8 us
  waiting for transfers between devices  21.2 us (41%)
  starting transfers between devices  17.4 us (33%)
  Pallas kernels  11.5 us (22%)
  local copies, waits for them, and re-layouts  1 us (2%)
  other arithmetic  0.66 us (1%)
    ppermute x8, starting transfers between devices, around(): lax.ppermute(x, 'cols', [(i, (i + by) % length) for i in range(length)])  11.2 us
    ppermute x8, waiting for transfers between devices, around(): lax.ppermute(x, 'cols', [(i, (i + by) % length) for i in range(length)])  11.1 us
    ppermute x3, waiting for transfers between devices, swap_cross(): return lax.ppermute(x, ('rows', 'cols'), pairs)  9.68 us
    pallas_call x1, Pallas kernels, on_device(): pl.pallas_call(main_kernel, out_shape=[out, out, jax.ShapeDtypeStruct(out...  6.1 us
    ppermute x3, starting transfers between devices, swap_cross(): return lax.ppermute(x, ('rows', 'cols'), pairs)  5.44 us
    pallas_call x1, Pallas kernels, on_device(): pl.pallas_call(table_kernel, out_shape=[pltpu.VMEM(stiffness.shape, BF),...  3.92 us
  transfers between devices with their start and end apart: 16, of which 8 were waited for; matrix products, arithmetic and copies ran while one was open for 0% of the time, Pallas kernels for 9%

profile of v4, /device:TPU:134, one launch (start us, length us, event | category | flops | bytes accessed | tf_op | source)
XLA Modules:
  0.0 51.8 jit_solution(6504116460531748692)
XLA Ops:
  0.0 1.0 %copy-done = bf16[16,48,192]{2,1,0:T(8,128)(2,1)S(1)} copy-done((bf16[16,48,192]{2,1,0:T(8,128)(2,1)S(1)}, bf16[16,48,192]{2,1,0:T(8,128)(2,1)}, u32[]{:S(2)}) %copy-start) | copy-done | bytes 294936
  1.0 0.4 shard_map.55.w0.rest_0_
  1.4 2.1 %collective-permute-start = (bf16[1152,128]{1,0:T(8,128)(2,1)S(1)}, bf16[1152,128]{1,0:T(8,128)(2,1)S(1)}, u32[]{:S(2)}, u32[]{:S(2)}) collective-permute-start(bf16[1152,128]{1,0:T(8,128)(2,1)S(1)} %shard_map.55.w0.rest_0_), channel_id=1, source_target_pairs={{4,8},{8,4},{12,16},{16,12},{20,24},{24,20},{28,32},{32,28},{36,40... | collective-permute-start | bytes 884744 | tf_op jit(solution)/shard_map/ppermute | solution.py:35
  3.5 1.4 %collective-permute-start.1 = (bf16[1152,128]{1,0:T(8,128)(2,1)S(1)}, bf16[1152,128]{1,0:T(8,128)(2,1)S(1)}, u32[]{:S(2)}, u32[]{:S(2)}) collective-permute-start(bf16[1152,128]{1,0:T(8,128)(2,1)S(1)} %shard_map.55.w0.rest_0_), channel_id=1, source_target_pairs={{0,2},{1,3},{2,0},{3,1},{4,6},{5,7},{6,4},{7,5},{8,10},{9,11},{10,... | collective-permute-start | bytes 884744 | tf_op jit(solution)/shard_map/ppermute | solution.py:18
  4.9 2.1 %collective-permute-start.3 = (bf16[1152,128]{1,0:T(8,128)(2,1)S(1)}, bf16[1152,128]{1,0:T(8,128)(2,1)S(1)}, u32[]{:S(2)}, u32[]{:S(2)}) collective-permute-start(bf16[1152,128]{1,0:T(8,128)(2,1)S(1)} %shard_map.55.w0.rest_0_), channel_id=1, source_target_pairs={{0,1},{1,2},{2,3},{3,0},{4,5},{5,6},{6,7},{7,4},{8,9},{9,10},{10,1... | collective-permute-start | bytes 884744 | tf_op jit(solution)/shard_map/ppermute | solution.py:18
  7.0 4.0 %collective-permute-done.rest_8_ = bf16[1152,128]{1,0:T(8,128)(2,1)S(1)} collective-permute-done((bf16[1152,128]{1,0:T(8,128)(2,1)S(1)}, bf16[1152,128]{1,0:T(8,128)(2,1)S(1)}, u32[]{:S(2)}, u32[]{:S(2)}) %collective-permute-start) | collective-permute-done | bytes 294944 | tf_op jit(solution)/shard_map/ppermute | solution.py:35
  10.9 0.8 %collective-permute-start.5 = (bf16[1152,128]{1,0:T(8,128)(2,1)S(1)}, bf16[1152,128]{1,0:T(8,128)(2,1)S(1)}, u32[]{:S(2)}, u32[]{:S(2)}) collective-permute-start(bf16[1152,128]{1,0:T(8,128)(2,1)S(1)} %collective-permute-done.rest_8_), channel_id=1, source_target_pairs={{0,3},{1,0},{2,1},{3,2},{4,7},{5,4},{6,5},{7,6},{8,11},{9,8},{10,9... | collective-permute-start | bytes 884744 | tf_op jit(solution)/shard_map/ppermute | solution.py:18
  11.8 3.9 %shard_map.56 = (bf16[16,4,192,192]{3,2,1,0:T(8,128)(2,1)S(1)}, s32[16,128]{1,0:T(8,128)S(1)}, s32[16,192]{1,0:T(8,128)S(1)}) custom-call(s32[4,16]{1,0:T(4,128)} %bitcast.4, s32[32,1024]{1,0:T(8,128)} %bitcast.6, bf16[16,4,192,192]{3,2,1,0:T(8,128)(2,1)} %s_hbm.1), custom_call_target="tpu_custom_call" | custom-call | tf_op jit(solution)/shard_map/pallas_call | solution.py:273
  15.7 2.5 %collective-permute-start.10 = (bf16[1152,128]{1,0:T(8,128)(2,1)S(1)}, bf16[1152,128]{1,0:T(8,128)(2,1)S(1)}, u32[]{:S(2)}, u32[]{:S(2)}) collective-permute-start(bf16[1152,128]{1,0:T(8,128)(2,1)S(1)} %collective-permute-done.rest_8_), channel_id=1, source_target_pairs={{0,1},{1,2},{2,3},{3,0},{4,5},{5,6},{6,7},{7,4},{8,9},{9,10},{10,1... | collective-permute-start | bytes 884744 | tf_op jit(solution)/shard_map/ppermute | solution.py:18
  18.2 1.4 %collective-permute-start.9 = (bf16[1152,128]{1,0:T(8,128)(2,1)S(1)}, bf16[1152,128]{1,0:T(8,128)(2,1)S(1)}, u32[]{:S(2)}, u32[]{:S(2)}) collective-permute-start(bf16[1152,128]{1,0:T(8,128)(2,1)S(1)} %collective-permute-done.1.w2.rest_2_), channel_id=1, source_target_pairs={{4,8},{8,4},{12,16},{16,12},{20,24},{24,20},{28,32},{32,28},{36,40... | collective-permute-start | bytes 884744 | tf_op jit(solution)/shard_map/ppermute | solution.py:35
  19.6 0.4 collective-permute-done.2.w1.rest_1_
  20.0 6.2 %collective-permute-done.5.rest_9_ = bf16[1152,128]{1,0:T(8,128)(2,1)S(1)} collective-permute-done((bf16[1152,128]{1,0:T(8,128)(2,1)S(1)}, bf16[1152,128]{1,0:T(8,128)(2,1)S(1)}, u32[]{:S(2)}, u32[]{:S(2)}) %collective-permute-start.5) | collective-permute-done | bytes 294944 | tf_op jit(solution)/shard_map/ppermute | solution.py:18
  26.2 0.5 collective-permute-start.8
  26.7 1.0 %shard_map.57 = (bf16[384,2048]{1,0:T(8,128)(2,1)S(1)}, bf16[384,1024]{1,0:T(8,128)(2,1)S(1)}) custom-call(s32[16,192]{1,0:T(8,128)S(1)} %get-tuple-element.27.aggl_ref, bf16[1152,128]{1,0:T(8,128)(2,1)S(1)} %shard_map.55.w0.rest_0_, bf16[1152,128]{1,0:T(8,128)(2,1)S(1)} %collective-permute-done.2.w1.rest_1_, ...), custom_call_target="tpu_custom_call" | custom-call | tf_op jit(solution)/shard_map/pallas_call | solution.py:296
  27.8 0.4 collective-permute-done.8.rest_7_
  28.2 6.1 %shard_map.58 = (f32[480,96]{1,0:T(8,128)S(1)}, f32[480,96]{1,0:T(8,128)S(1)}, bf16[480,96]{1,0:T(8,128)(2,1)S(1)}) custom-call(s32[4,16]{1,0:T(4,128)S(1)} %bitcast.5, s32[16]{0:T(128)S(1)} %copy-done.2, s32[16,128]{1,0:T(8,128)S(1)} %get-tuple-element.25.aggr_ref, bf16[384,2048]{1,0:T(8,128)(2,1)S(1)} %get-tuple-element.29.lo_ref, ...), custom_call_target="tpu_custom_call" | custom-call | tf_op jit(solution)/shard_map/pallas_call | solution.py:309
  34.5 1.9 %collective-permute-start.12 = (bf16[480,96]{1,0:T(8,128)(2,1)S(1)}, bf16[480,96]{1,0:T(8,128)(2,1)S(1)}, u32[]{:S(2)}, u32[]{:S(2)}) collective-permute-start(bf16[480,96]{1,0:T(8,128)(2,1)S(1)} %get-tuple-element.38), channel_id=1, source_target_pairs={{4,8},{8,4},{12,16},{16,12},{20,24},{24,20},{28,32},{32,28},{36,40... | collective-permute-start | bytes 276488 | tf_op jit(solution)/shard_map/ppermute | solution.py:35
  36.5 5.7 %collective-permute-done.12.cross_ref = bf16[480,96]{1,0:T(8,128)(2,1)S(1)} collective-permute-done((bf16[480,96]{1,0:T(8,128)(2,1)S(1)}, bf16[480,96]{1,0:T(8,128)(2,1)S(1)}, u32[]{:S(2)}, u32[]{:S(2)}) %collective-permute-start.12) | collective-permute-done | bytes 92192 | tf_op jit(solution)/shard_map/ppermute | solution.py:35
  42.3 1.7 %collective-permute-start.13 = (bf16[176,96]{1,0:T(8,128)(2,1)S(1)}, bf16[176,96]{1,0:T(8,128)(2,1)S(1)}, u32[]{:S(2)}, u32[]{:S(2)}) collective-permute-start(bf16[176,96]{1,0:T(8,128)(2,1)S(1)} %get-tuple-element.40), channel_id=1, source_target_pairs={{0,1},{1,2},{2,3},{3,0},{4,5},{5,6},{6,7},{7,4},{8,9},{9,10},{10,1... | collective-permute-start | bytes 101384 | tf_op jit(solution)/shard_map/ppermute | solution.py:18
  44.0 1.9 %collective-permute-start.14 = (bf16[176,96]{1,0:T(8,128)(2,1)S(1)}, bf16[176,96]{1,0:T(8,128)(2,1)S(1)}, u32[]{:S(2)}, u32[]{:S(2)}) collective-permute-start(bf16[176,96]{1,0:T(8,128)(2,1)S(1)} %get-tuple-element.41), channel_id=1, source_target_pairs={{0,2},{1,3},{2,0},{3,1},{4,6},{5,7},{6,4},{7,5},{8,10},{9,11},{10,... | collective-permute-start | bytes 101384 | tf_op jit(solution)/shard_map/ppermute | solution.py:18
  45.9 0.8 %collective-permute-start.15 = (bf16[176,96]{1,0:T(8,128)(2,1)S(1)}, bf16[176,96]{1,0:T(8,128)(2,1)S(1)}, u32[]{:S(2)}, u32[]{:S(2)}) collective-permute-start(bf16[176,96]{1,0:T(8,128)(2,1)S(1)} %get-tuple-element.42), channel_id=1, source_target_pairs={{0,3},{1,0},{2,1},{3,2},{4,7},{5,4},{6,5},{7,6},{8,11},{9,8},{10,9... | collective-permute-start | bytes 101384 | tf_op jit(solution)/shard_map/ppermute | solution.py:18
  46.7 2.9 %collective-permute-done.14 = bf16[176,96]{1,0:T(8,128)(2,1)S(1)} collective-permute-done((bf16[176,96]{1,0:T(8,128)(2,1)S(1)}, bf16[176,96]{1,0:T(8,128)(2,1)S(1)}, u32[]{:S(2)}, u32[]{:S(2)}) %collective-permute-start.14) | collective-permute-done | bytes 33824 | tf_op jit(solution)/shard_map/ppermute | solution.py:18
  49.5 1.6 %collective-permute-done.15 = bf16[176,96]{1,0:T(8,128)(2,1)S(1)} collective-permute-done((bf16[176,96]{1,0:T(8,128)(2,1)S(1)}, bf16[176,96]{1,0:T(8,128)(2,1)S(1)}, u32[]{:S(2)}, u32[]{:S(2)}) %collective-permute-start.15) | collective-permute-done | bytes 33824 | tf_op jit(solution)/shard_map/ppermute | solution.py:18
  51.2 0.7 %add_bitcast_fusion = f32[96,168]{0,1:T(8,128)} fusion(f32[168,96]{1,0:T(8,128)S(1)} %get-tuple-element.39, bf16[176,96]{1,0:T(8,128)(2,1)S(1)} %collective-permute-done.15, bf16[176,96]{1,0:T(8,128)(2,1)S(1)} %collective-permute-done.14, bf16[176,96]{1,0:T(8,128)(2,1)S(1)} %collective-permute-done.13), kind=kLoop, calls=%fused_computation | loop fusion | flops 96768 | bytes 225792 | tf_op jit(solution)/shard_map/transpose | solution.py:340
  (20 shorter events, 0.4 us)
Async XLA Ops:
  0.0 1.0 %copy-start = (bf16[16,48,192]{2,1,0:T(8,128)(2,1)S(1)}, bf16[16,48,192]{2,1,0:T(8,128)(2,1)}, u32[]{:S(2)}) copy-start(bf16[16,48,192]{2,1,0:T(8,128)(2,1)} %q_ref.1) | copy-start | bytes 884740
  1.0 27.2 %copy-start.1 = (s32[16,4]{0,1:T(4,128)S(1)}, s32[16,4]{0,1:T(4,128)}, u32[]{:S(2)}) copy-start(s32[16,4]{0,1:T(4,128)} %param.6) | copy-start | bytes 772
  1.0 27.2 %copy-start.2 = (s32[16]{0:T(128)S(1)}, s32[16]{0:T(128)}, u32[]{:S(2)}) copy-start(s32[16]{0:T(128)} %live_ref.1) | copy-start | bytes 196
  1.4 9.6 %collective-permute-start = (bf16[1152,128]{1,0:T(8,128)(2,1)S(1)}, bf16[1152,128]{1,0:T(8,128)(2,1)S(1)}, u32[]{:S(2)}, u32[]{:S(2)}) collective-permute-start(bf16[1152,128]{1,0:T(8,128)(2,1)S(1)} %shard_map.55.w0.rest_0_), channel_id=1, source_target_pairs={{4,8},{8,4},{12,16},{16,12},{20,24},{24,20},{28,32},{32,28},{36,40... | collective-permute-start | bytes 884744 | tf_op jit(solution)/shard_map/ppermute | solution.py:35
  3.5 12.2 %collective-permute-start.1 = (bf16[1152,128]{1,0:T(8,128)(2,1)S(1)}, bf16[1152,128]{1,0:T(8,128)(2,1)S(1)}, u32[]{:S(2)}, u32[]{:S(2)}) collective-permute-start(bf16[1152,128]{1,0:T(8,128)(2,1)S(1)} %shard_map.55.w0.rest_0_), channel_id=1, source_target_pairs={{0,2},{1,3},{2,0},{3,1},{4,6},{5,7},{6,4},{7,5},{8,10},{9,11},{10,... | collective-permute-start | bytes 884744 | tf_op jit(solution)/shard_map/ppermute | solution.py:18
  4.9 13.3 %collective-permute-start.3 = (bf16[1152,128]{1,0:T(8,128)(2,1)S(1)}, bf16[1152,128]{1,0:T(8,128)(2,1)S(1)}, u32[]{:S(2)}, u32[]{:S(2)}) collective-permute-start(bf16[1152,128]{1,0:T(8,128)(2,1)S(1)} %shard_map.55.w0.rest_0_), channel_id=1, source_target_pairs={{0,1},{1,2},{2,3},{3,0},{4,5},{5,6},{6,7},{7,4},{8,9},{9,10},{10,1... | collective-permute-start | bytes 884744 | tf_op jit(solution)/shard_map/ppermute | solution.py:18
  7.0 13.0 %collective-permute-start.2 = (bf16[1152,128]{1,0:T(8,128)(2,1)S(1)}, bf16[1152,128]{1,0:T(8,128)(2,1)S(1)}, u32[]{:S(2)}, u32[]{:S(2)}) collective-permute-start(bf16[1152,128]{1,0:T(8,128)(2,1)S(1)} %shard_map.55.w0.rest_0_), channel_id=1, source_target_pairs={{0,3},{1,0},{2,1},{3,2},{4,7},{5,4},{6,5},{7,6},{8,11},{9,8},{10,9... | collective-permute-start | bytes 884744 | tf_op jit(solution)/shard_map/ppermute | solution.py:18
  10.9 15.3 %collective-permute-start.5 = (bf16[1152,128]{1,0:T(8,128)(2,1)S(1)}, bf16[1152,128]{1,0:T(8,128)(2,1)S(1)}, u32[]{:S(2)}, u32[]{:S(2)}) collective-permute-start(bf16[1152,128]{1,0:T(8,128)(2,1)S(1)} %collective-permute-done.rest_8_), channel_id=1, source_target_pairs={{0,3},{1,0},{2,1},{3,2},{4,7},{5,4},{6,5},{7,6},{8,11},{9,8},{10,9... | collective-permute-start | bytes 884744 | tf_op jit(solution)/shard_map/ppermute | solution.py:18
  11.8 14.5 %collective-permute-start.4 = (bf16[1152,128]{1,0:T(8,128)(2,1)S(1)}, bf16[1152,128]{1,0:T(8,128)(2,1)S(1)}, u32[]{:S(2)}, u32[]{:S(2)}) collective-permute-start(bf16[1152,128]{1,0:T(8,128)(2,1)S(1)} %shard_map.55.w0.rest_0_), channel_id=1, source_target_pairs={{0,4},{4,0},{8,12},{12,8},{16,20},{20,16},{24,28},{28,24},{32,36},... | collective-permute-start | bytes 884744 | tf_op jit(solution)/shard_map/ppermute | solution.py:23
  15.7 12.0 %collective-permute-start.10 = (bf16[1152,128]{1,0:T(8,128)(2,1)S(1)}, bf16[1152,128]{1,0:T(8,128)(2,1)S(1)}, u32[]{:S(2)}, u32[]{:S(2)}) collective-permute-start(bf16[1152,128]{1,0:T(8,128)(2,1)S(1)} %collective-permute-done.rest_8_), channel_id=1, source_target_pairs={{0,1},{1,2},{2,3},{3,0},{4,5},{5,6},{6,7},{7,4},{8,9},{9,10},{10,1... | collective-permute-start | bytes 884744 | tf_op jit(solution)/shard_map/ppermute | solution.py:18
  18.2 9.5 %collective-permute-start.9 = (bf16[1152,128]{1,0:T(8,128)(2,1)S(1)}, bf16[1152,128]{1,0:T(8,128)(2,1)S(1)}, u32[]{:S(2)}, u32[]{:S(2)}) collective-permute-start(bf16[1152,128]{1,0:T(8,128)(2,1)S(1)} %collective-permute-done.1.w2.rest_2_), channel_id=1, source_target_pairs={{4,8},{8,4},{12,16},{16,12},{20,24},{24,20},{28,32},{32,28},{36,40... | collective-permute-start | bytes 884744 | tf_op jit(solution)/shard_map/ppermute | solution.py:35
  20.0 7.7 %collective-permute-start.7 = (bf16[1152,128]{1,0:T(8,128)(2,1)S(1)}, bf16[1152,128]{1,0:T(8,128)(2,1)S(1)}, u32[]{:S(2)}, u32[]{:S(2)}) collective-permute-start(bf16[1152,128]{1,0:T(8,128)(2,1)S(1)} %collective-permute-done.1.w2.rest_2_), channel_id=1, source_target_pairs={{0,4},{4,0},{8,12},{12,8},{16,20},{20,16},{24,28},{28,24},{32,36},... | collective-permute-start | bytes 884744 | tf_op jit(solution)/shard_map/ppermute | solution.py:23
  26.2 1.6 %collective-permute-start.6 = (bf16[1152,128]{1,0:T(8,128)(2,1)S(1)}, bf16[1152,128]{1,0:T(8,128)(2,1)S(1)}, u32[]{:S(2)}, u32[]{:S(2)}) collective-permute-start(bf16[1152,128]{1,0:T(8,128)(2,1)S(1)} %collective-permute-done.2.w1.rest_1_), channel_id=1, source_target_pairs={{0,4},{4,0},{8,12},{12,8},{16,20},{20,16},{24,28},{28,24},{32,36},... | collective-permute-start | bytes 884744 | tf_op jit(solution)/shard_map/ppermute | solution.py:23
  26.2 2.0 %collective-permute-start.8 = (bf16[1152,128]{1,0:T(8,128)(2,1)S(1)}, bf16[1152,128]{1,0:T(8,128)(2,1)S(1)}, u32[]{:S(2)}, u32[]{:S(2)}) collective-permute-start(bf16[1152,128]{1,0:T(8,128)(2,1)S(1)} %collective-permute-done.3.w3.rest_3_), channel_id=1, source_target_pairs={{0,4},{4,0},{8,12},{12,8},{16,20},{20,16},{24,28},{28,24},{32,36},... | collective-permute-start | bytes 884744 | tf_op jit(solution)/shard_map/ppermute | solution.py:23
  34.3 7.8 %collective-permute-start.11 = (f32[480,96]{1,0:T(8,128)S(1)}, f32[480,96]{1,0:T(8,128)S(1)}, u32[]{:S(2)}, u32[]{:S(2)}) collective-permute-start(f32[480,96]{1,0:T(8,128)S(1)} %get-tuple-element.37), channel_id=1, source_target_pairs={{0,4},{4,0},{8,12},{12,8},{16,20},{20,16},{24,28},{28,24},{32,36},... | collective-permute-start | bytes 552968 | tf_op jit(solution)/shard_map/ppermute | solution.py:23
  34.5 7.6 %collective-permute-start.12 = (bf16[480,96]{1,0:T(8,128)(2,1)S(1)}, bf16[480,96]{1,0:T(8,128)(2,1)S(1)}, u32[]{:S(2)}, u32[]{:S(2)}) collective-permute-start(bf16[480,96]{1,0:T(8,128)(2,1)S(1)} %get-tuple-element.38), channel_id=1, source_target_pairs={{4,8},{8,4},{12,16},{16,12},{20,24},{24,20},{28,32},{32,28},{36,40... | collective-permute-start | bytes 276488 | tf_op jit(solution)/shard_map/ppermute | solution.py:35
  42.3 4.4 %collective-permute-start.13 = (bf16[176,96]{1,0:T(8,128)(2,1)S(1)}, bf16[176,96]{1,0:T(8,128)(2,1)S(1)}, u32[]{:S(2)}, u32[]{:S(2)}) collective-permute-start(bf16[176,96]{1,0:T(8,128)(2,1)S(1)} %get-tuple-element.40), channel_id=1, source_target_pairs={{0,1},{1,2},{2,3},{3,0},{4,5},{5,6},{6,7},{7,4},{8,9},{9,10},{10,1... | collective-permute-start | bytes 101384 | tf_op jit(solution)/shard_map/ppermute | solution.py:18
  44.0 5.6 %collective-permute-start.14 = (bf16[176,96]{1,0:T(8,128)(2,1)S(1)}, bf16[176,96]{1,0:T(8,128)(2,1)S(1)}, u32[]{:S(2)}, u32[]{:S(2)}) collective-permute-start(bf16[176,96]{1,0:T(8,128)(2,1)S(1)} %get-tuple-element.41), channel_id=1, source_target_pairs={{0,2},{1,3},{2,0},{3,1},{4,6},{5,7},{6,4},{7,5},{8,10},{9,11},{10,... | collective-permute-start | bytes 101384 | tf_op jit(solution)/shard_map/ppermute | solution.py:18
  45.9 5.3 %collective-permute-start.15 = (bf16[176,96]{1,0:T(8,128)(2,1)S(1)}, bf16[176,96]{1,0:T(8,128)(2,1)S(1)}, u32[]{:S(2)}, u32[]{:S(2)}) collective-permute-start(bf16[176,96]{1,0:T(8,128)(2,1)S(1)} %get-tuple-element.42), channel_id=1, source_target_pairs={{0,3},{1,0},{2,1},{3,2},{4,7},{5,4},{6,5},{7,6},{8,11},{9,8},{10,9... | collective-permute-start | bytes 101384 | tf_op jit(solution)/shard_map/ppermute | solution.py:18

commit v5 on v4

--- a/solution.py
+++ b/solution.py
@@ -23,7 +23,7 @@
     return lax.ppermute(x, "rows", [(i, i ^ 1) for i in range(length)])
 
 
-def swap_cross(x):
+def swap_cross(x, turn=1):
     rows = lax.axis_size("rows")
     cols = lax.axis_size("cols")
     pairs = []
@@ -31,7 +31,7 @@
         for r in range(1, rows - 1, 2):
             pairs += [(r * cols + c, (r + 1) * cols + c), ((r + 1) * cols + c, r * cols + c)]
         for r in (0, rows - 1):
-            pairs.append((r * cols + c, r * cols + (c ^ 1)))
+            pairs.append((r * cols + c, r * cols + (c ^ turn)))
     return lax.ppermute(x, ("rows", "cols"), pairs)
 
 
@@ -268,7 +268,7 @@
     w1 = around(w0, -1)
     w3 = around(w0, 1)
     b0 = swap_cross(w0)
-    aggs, b0 = lax.optimization_barrier((prolong_aggs.T, b0))
+    aggs = prolong_aggs.T
 
     s_near, aggr, aggl = pl.pallas_call(
         table_kernel,
@@ -289,9 +289,9 @@
 
     b1 = around(b0, -1)
     b3 = around(b0, 1)
-    b2 = swap_cross(w2)
-    q1, q3, b1 = lax.optimization_barrier((w1, w3, b1))
-    a0, a1, a2, a3 = (swap_chip(q) for q in (w0, q1, w2, q3))
+    b2 = swap_cross(w2, 3)
+    q0, q1, q2, q3, b2 = lax.optimization_barrier((w0, w1, w2, w3, b2))
+    a0, a1, a2, a3 = (swap_chip(q) for q in (q0, q1, q2, q3))
 
     left_lo, left_hi = pl.pallas_call(
         left_kernel,

time: 52 us -> 49.4 us (0.950)
  starting transfers between devices: 17.4 us -> 15 us
    ppermute x3, starting transfers between devices: 5.44 us -> 3.94 us  [swap_cross(): return lax.ppermute(x, ('rows', 'cols'), pairs)]
    ppermute x8, waiting for transfers between devices: 11.1 us -> 9.82 us  [around(): lax.ppermute(x, 'cols', [(i, (i + by) % length) for i in range(length)])]
    ppermute x8, starting transfers between devices: 11.2 us -> 10.3 us  [around(): lax.ppermute(x, 'cols', [(i, (i + by) % length) for i in range(length)])]
    ppermute x3, waiting for transfers between devices: 9.68 us -> 10.6 us  [swap_cross(): return lax.ppermute(x, ('rows', 'cols'), pairs)]
  transfers between devices with their start and end apart: 16 -> 16, of which waited for: 8 -> 10; matrix products, arithmetic and copies ran while one was open for 0% -> 0% of each run, Pallas kernels for 9% -> 10%
where the time goes in v5:
time: 49.4 us; the launch traced here: 48.9 us
  waiting for transfers between devices  20.7 us (42%)
  starting transfers between devices  15 us (30%)
  Pallas kernels  11.4 us (23%)
  local copies, waits for them, and re-layouts  1 us (2%)
  other arithmetic  0.66 us (1%)
    ppermute x3, waiting for transfers between devices, swap_cross(): return lax.ppermute(x, ('rows', 'cols'), pairs)  10.6 us
    ppermute x8, starting transfers between devices, around(): lax.ppermute(x, 'cols', [(i, (i + by) % length) for i in range(length)])  10.3 us
    ppermute x8, waiting for transfers between devices, around(): lax.ppermute(x, 'cols', [(i, (i + by) % length) for i in range(length)])  9.82 us
    pallas_call x1, Pallas kernels, on_device(): pl.pallas_call(main_kernel, out_shape=[out, out, jax.ShapeDtypeStruct(out...  6.06 us
    ppermute x3, starting transfers between devices, swap_cross(): return lax.ppermute(x, ('rows', 'cols'), pairs)  3.94 us
    pallas_call x1, Pallas kernels, on_device(): pl.pallas_call(table_kernel, out_shape=[pltpu.VMEM(stiffness.shape, BF),...  3.92 us
    unnamed x6, local copies, waits for them, and re-layouts  1 us
  transfers between devices with their start and end apart: 16, of which 10 were waited for; matrix products, arithmetic and copies ran while one was open for 0% of the time, Pallas kernels for 10%

profile of v5, /device:TPU:134, one launch (start us, length us, event | category | flops | bytes accessed | tf_op | source)
XLA Modules:
  0.0 48.9 jit_solution(12515720628425555011)
XLA Ops:
  0.0 1.0 %copy-done = bf16[16,48,192]{2,1,0:T(8,128)(2,1)S(1)} copy-done((bf16[16,48,192]{2,1,0:T(8,128)(2,1)S(1)}, bf16[16,48,192]{2,1,0:T(8,128)(2,1)}, u32[]{:S(2)}) %copy-start) | copy-done | bytes 294936
  1.0 0.4 shard_map.56.w0.rest_0_
  1.4 1.5 %collective-permute-start = (bf16[1152,128]{1,0:T(8,128)(2,1)S(1)}, bf16[1152,128]{1,0:T(8,128)(2,1)S(1)}, u32[]{:S(2)}, u32[]{:S(2)}) collective-permute-start(bf16[1152,128]{1,0:T(8,128)(2,1)S(1)} %shard_map.56.w0.rest_0_), channel_id=1, source_target_pairs={{0,2},{1,3},{2,0},{3,1},{4,6},{5,7},{6,4},{7,5},{8,10},{9,11},{10,... | collective-permute-start | bytes 884744 | tf_op jit(solution)/shard_map/ppermute | solution.py:18
  2.9 1.7 %collective-permute-start.8 = (bf16[1152,128]{1,0:T(8,128)(2,1)S(1)}, bf16[1152,128]{1,0:T(8,128)(2,1)S(1)}, u32[]{:S(2)}, u32[]{:S(2)}) collective-permute-start(bf16[1152,128]{1,0:T(8,128)(2,1)S(1)} %shard_map.56.w0.rest_0_), channel_id=1, source_target_pairs={{4,8},{8,4},{12,16},{16,12},{20,24},{24,20},{28,32},{32,28},{36,40... | collective-permute-start | bytes 884744 | tf_op jit(solution)/shard_map/ppermute | solution.py:35
  4.6 2.1 %collective-permute-start.2 = (bf16[1152,128]{1,0:T(8,128)(2,1)S(1)}, bf16[1152,128]{1,0:T(8,128)(2,1)S(1)}, u32[]{:S(2)}, u32[]{:S(2)}) collective-permute-start(bf16[1152,128]{1,0:T(8,128)(2,1)S(1)} %shard_map.56.w0.rest_0_), channel_id=1, source_target_pairs={{0,1},{1,2},{2,3},{3,0},{4,5},{5,6},{6,7},{7,4},{8,9},{9,10},{10,1... | collective-permute-start | bytes 884744 | tf_op jit(solution)/shard_map/ppermute | solution.py:18
  6.7 3.9 %shard_map.55 = (bf16[16,4,192,192]{3,2,1,0:T(8,128)(2,1)S(1)}, s32[16,128]{1,0:T(8,128)S(1)}, s32[16,192]{1,0:T(8,128)S(1)}) custom-call(s32[4,16]{1,0:T(4,128)} %bitcast.4, s32[32,1024]{1,0:T(8,128)} %bitcast.6, bf16[16,4,192,192]{3,2,1,0:T(8,128)(2,1)} %s_hbm.1), custom_call_target="tpu_custom_call" | custom-call | tf_op jit(solution)/shard_map/pallas_call | solution.py:273
  10.6 2.3 %collective-permute-done.w2.rest_2_ = bf16[1152,128]{1,0:T(8,128)(2,1)S(1)} collective-permute-done((bf16[1152,128]{1,0:T(8,128)(2,1)S(1)}, bf16[1152,128]{1,0:T(8,128)(2,1)S(1)}, u32[]{:S(2)}, u32[]{:S(2)}) %collective-permute-start) | collective-permute-done | bytes 294944 | tf_op jit(solution)/shard_map/ppermute | solution.py:18
  12.9 0.9 %collective-permute-start.3 = (bf16[1152,128]{1,0:T(8,128)(2,1)S(1)}, bf16[1152,128]{1,0:T(8,128)(2,1)S(1)}, u32[]{:S(2)}, u32[]{:S(2)}) collective-permute-start(bf16[1152,128]{1,0:T(8,128)(2,1)S(1)} %collective-permute-done.w2.rest_2_), channel_id=1, source_target_pairs={{4,8},{8,4},{12,16},{16,12},{20,24},{24,20},{28,32},{32,28},{36,40... | collective-permute-start | bytes 884744 | tf_op jit(solution)/shard_map/ppermute | solution.py:35
  13.8 3.0 %collective-permute-start.10 = (bf16[1152,128]{1,0:T(8,128)(2,1)S(1)}, bf16[1152,128]{1,0:T(8,128)(2,1)S(1)}, u32[]{:S(2)}, u32[]{:S(2)}) collective-permute-start(bf16[1152,128]{1,0:T(8,128)(2,1)S(1)} %collective-permute-done.8.rest_8_), channel_id=1, source_target_pairs={{0,1},{1,2},{2,3},{3,0},{4,5},{5,6},{6,7},{7,4},{8,9},{9,10},{10,1... | collective-permute-start | bytes 884744 | tf_op jit(solution)/shard_map/ppermute | solution.py:18
  16.7 1.3 %collective-permute-done.1.w1.rest_1_ = bf16[1152,128]{1,0:T(8,128)(2,1)S(1)} collective-permute-done((bf16[1152,128]{1,0:T(8,128)(2,1)S(1)}, bf16[1152,128]{1,0:T(8,128)(2,1)S(1)}, u32[]{:S(2)}, u32[]{:S(2)}) %collective-permute-start.1) | collective-permute-done | bytes 294944 | tf_op jit(solution)/shard_map/ppermute | solution.py:18
  18.0 4.3 %collective-permute-done.3.rest_10_ = bf16[1152,128]{1,0:T(8,128)(2,1)S(1)} collective-permute-done((bf16[1152,128]{1,0:T(8,128)(2,1)S(1)}, bf16[1152,128]{1,0:T(8,128)(2,1)S(1)}, u32[]{:S(2)}, u32[]{:S(2)}) %collective-permute-start.3) | collective-permute-done | bytes 294944 | tf_op jit(solution)/shard_map/ppermute | solution.py:35
  22.3 0.5 %collective-permute-start.5 = (bf16[1152,128]{1,0:T(8,128)(2,1)S(1)}, bf16[1152,128]{1,0:T(8,128)(2,1)S(1)}, u32[]{:S(2)}, u32[]{:S(2)}) collective-permute-start(bf16[1152,128]{1,0:T(8,128)(2,1)S(1)} %collective-permute-done.1.w1.rest_1_), channel_id=1, source_target_pairs={{0,4},{4,0},{8,12},{12,8},{16,20},{20,16},{24,28},{28,24},{32,36},... | collective-permute-start | bytes 884744 | tf_op jit(solution)/shard_map/ppermute | solution.py:23
  22.9 0.6 %collective-permute-done.10.rest_11_ = bf16[1152,128]{1,0:T(8,128)(2,1)S(1)} collective-permute-done((bf16[1152,128]{1,0:T(8,128)(2,1)S(1)}, bf16[1152,128]{1,0:T(8,128)(2,1)S(1)}, u32[]{:S(2)}, u32[]{:S(2)}) %collective-permute-start.10) | collective-permute-done | bytes 294944 | tf_op jit(solution)/shard_map/ppermute | solution.py:18
  23.5 1.0 %shard_map.57 = (bf16[384,2048]{1,0:T(8,128)(2,1)S(1)}, bf16[384,1024]{1,0:T(8,128)(2,1)S(1)}) custom-call(s32[16,192]{1,0:T(8,128)S(1)} %get-tuple-element.26.aggl_ref, bf16[1152,128]{1,0:T(8,128)(2,1)S(1)} %shard_map.56.w0.rest_0_, bf16[1152,128]{1,0:T(8,128)(2,1)S(1)} %collective-permute-done.1.w1.rest_1_, ...), custom_call_target="tpu_custom_call" | custom-call | tf_op jit(solution)/shard_map/pallas_call | solution.py:296
  24.5 0.4 collective-permute-done.9.rest_9_
  25.2 6.1 %shard_map.58 = (f32[480,96]{1,0:T(8,128)S(1)}, f32[480,96]{1,0:T(8,128)S(1)}, bf16[480,96]{1,0:T(8,128)(2,1)S(1)}) custom-call(s32[4,16]{1,0:T(4,128)S(1)} %bitcast.5, s32[16]{0:T(128)S(1)} %copy-done.2, s32[16,128]{1,0:T(8,128)S(1)} %get-tuple-element.24.aggr_ref, bf16[384,2048]{1,0:T(8,128)(2,1)S(1)} %get-tuple-element.28.lo_ref, ...), custom_call_target="tpu_custom_call" | custom-call | tf_op jit(solution)/shard_map/pallas_call | solution.py:309
  31.5 1.3 %collective-permute-start.12 = (bf16[480,96]{1,0:T(8,128)(2,1)S(1)}, bf16[480,96]{1,0:T(8,128)(2,1)S(1)}, u32[]{:S(2)}, u32[]{:S(2)}) collective-permute-start(bf16[480,96]{1,0:T(8,128)(2,1)S(1)} %get-tuple-element.38), channel_id=1, source_target_pairs={{4,8},{8,4},{12,16},{16,12},{20,24},{24,20},{28,32},{32,28},{36,40... | collective-permute-start | bytes 276488 | tf_op jit(solution)/shard_map/ppermute | solution.py:35
  32.8 6.3 %collective-permute-done.12.cross_ref = bf16[480,96]{1,0:T(8,128)(2,1)S(1)} collective-permute-done((bf16[480,96]{1,0:T(8,128)(2,1)S(1)}, bf16[480,96]{1,0:T(8,128)(2,1)S(1)}, u32[]{:S(2)}, u32[]{:S(2)}) %collective-permute-start.12) | collective-permute-done | bytes 92192 | tf_op jit(solution)/shard_map/ppermute | solution.py:35
  39.2 1.6 %collective-permute-start.13 = (bf16[176,96]{1,0:T(8,128)(2,1)S(1)}, bf16[176,96]{1,0:T(8,128)(2,1)S(1)}, u32[]{:S(2)}, u32[]{:S(2)}) collective-permute-start(bf16[176,96]{1,0:T(8,128)(2,1)S(1)} %get-tuple-element.40), channel_id=1, source_target_pairs={{0,1},{1,2},{2,3},{3,0},{4,5},{5,6},{6,7},{7,4},{8,9},{9,10},{10,1... | collective-permute-start | bytes 101384 | tf_op jit(solution)/shard_map/ppermute | solution.py:18
  40.8 2.1 %collective-permute-start.14 = (bf16[176,96]{1,0:T(8,128)(2,1)S(1)}, bf16[176,96]{1,0:T(8,128)(2,1)S(1)}, u32[]{:S(2)}, u32[]{:S(2)}) collective-permute-start(bf16[176,96]{1,0:T(8,128)(2,1)S(1)} %get-tuple-element.41), channel_id=1, source_target_pairs={{0,2},{1,3},{2,0},{3,1},{4,6},{5,7},{6,4},{7,5},{8,10},{9,11},{10,... | collective-permute-start | bytes 101384 | tf_op jit(solution)/shard_map/ppermute | solution.py:18
  43.0 0.4 collective-permute-done.13
  43.4 3.0 %collective-permute-done.14 = bf16[176,96]{1,0:T(8,128)(2,1)S(1)} collective-permute-done((bf16[176,96]{1,0:T(8,128)(2,1)S(1)}, bf16[176,96]{1,0:T(8,128)(2,1)S(1)}, u32[]{:S(2)}, u32[]{:S(2)}) %collective-permute-start.14) | collective-permute-done | bytes 33824 | tf_op jit(solution)/shard_map/ppermute | solution.py:18
  46.4 1.8 %collective-permute-done.15 = bf16[176,96]{1,0:T(8,128)(2,1)S(1)} collective-permute-done((bf16[176,96]{1,0:T(8,128)(2,1)S(1)}, bf16[176,96]{1,0:T(8,128)(2,1)S(1)}, u32[]{:S(2)}, u32[]{:S(2)}) %collective-permute-start.15) | collective-permute-done | bytes 33824 | tf_op jit(solution)/shard_map/ppermute | solution.py:18
  48.2 0.7 %add_bitcast_fusion = f32[96,168]{0,1:T(8,128)} fusion(f32[168,96]{1,0:T(8,128)S(1)} %get-tuple-element.39, bf16[176,96]{1,0:T(8,128)(2,1)S(1)} %collective-permute-done.15, bf16[176,96]{1,0:T(8,128)(2,1)S(1)} %collective-permute-done.14, bf16[176,96]{1,0:T(8,128)(2,1)S(1)} %collective-permute-done.13), kind=kLoop, calls=%fused_computation | loop fusion | flops 96768 | bytes 225792 | tf_op jit(solution)/shard_map/transpose | solution.py:340
  (20 shorter events, 0.7 us)
Async XLA Ops:
  0.0 1.0 %copy-start = (bf16[16,48,192]{2,1,0:T(8,128)(2,1)S(1)}, bf16[16,48,192]{2,1,0:T(8,128)(2,1)}, u32[]{:S(2)}) copy-start(bf16[16,48,192]{2,1,0:T(8,128)(2,1)} %q_ref.1) | copy-start | bytes 884740
  1.0 24.2 %copy-start.1 = (s32[16,4]{0,1:T(4,128)S(1)}, s32[16,4]{0,1:T(4,128)}, u32[]{:S(2)}) copy-start(s32[16,4]{0,1:T(4,128)} %param.6) | copy-start | bytes 772
  1.0 24.2 %copy-start.2 = (s32[16]{0:T(128)S(1)}, s32[16]{0:T(128)}, u32[]{:S(2)}) copy-start(s32[16]{0:T(128)} %live_ref.1) | copy-start | bytes 196
  1.4 11.5 %collective-permute-start = (bf16[1152,128]{1,0:T(8,128)(2,1)S(1)}, bf16[1152,128]{1,0:T(8,128)(2,1)S(1)}, u32[]{:S(2)}, u32[]{:S(2)}) collective-permute-start(bf16[1152,128]{1,0:T(8,128)(2,1)S(1)} %shard_map.56.w0.rest_0_), channel_id=1, source_target_pairs={{0,2},{1,3},{2,0},{3,1},{4,6},{5,7},{6,4},{7,5},{8,10},{9,11},{10,... | collective-permute-start | bytes 884744 | tf_op jit(solution)/shard_map/ppermute | solution.py:18
  2.9 10.9 %collective-permute-start.8 = (bf16[1152,128]{1,0:T(8,128)(2,1)S(1)}, bf16[1152,128]{1,0:T(8,128)(2,1)S(1)}, u32[]{:S(2)}, u32[]{:S(2)}) collective-permute-start(bf16[1152,128]{1,0:T(8,128)(2,1)S(1)} %shard_map.56.w0.rest_0_), channel_id=1, source_target_pairs={{4,8},{8,4},{12,16},{16,12},{20,24},{24,20},{28,32},{32,28},{36,40... | collective-permute-start | bytes 884744 | tf_op jit(solution)/shard_map/ppermute | solution.py:35
  4.6 12.2 %collective-permute-start.2 = (bf16[1152,128]{1,0:T(8,128)(2,1)S(1)}, bf16[1152,128]{1,0:T(8,128)(2,1)S(1)}, u32[]{:S(2)}, u32[]{:S(2)}) collective-permute-start(bf16[1152,128]{1,0:T(8,128)(2,1)S(1)} %shard_map.56.w0.rest_0_), channel_id=1, source_target_pairs={{0,1},{1,2},{2,3},{3,0},{4,5},{5,6},{6,7},{7,4},{8,9},{9,10},{10,1... | collective-permute-start | bytes 884744 | tf_op jit(solution)/shard_map/ppermute | solution.py:18
  6.7 11.4 %collective-permute-start.1 = (bf16[1152,128]{1,0:T(8,128)(2,1)S(1)}, bf16[1152,128]{1,0:T(8,128)(2,1)S(1)}, u32[]{:S(2)}, u32[]{:S(2)}) collective-permute-start(bf16[1152,128]{1,0:T(8,128)(2,1)S(1)} %shard_map.56.w0.rest_0_), channel_id=1, source_target_pairs={{0,3},{1,0},{2,1},{3,2},{4,7},{5,4},{6,5},{7,6},{8,11},{9,8},{10,9... | collective-permute-start | bytes 884744 | tf_op jit(solution)/shard_map/ppermute | solution.py:18
  12.9 9.5 %collective-permute-start.3 = (bf16[1152,128]{1,0:T(8,128)(2,1)S(1)}, bf16[1152,128]{1,0:T(8,128)(2,1)S(1)}, u32[]{:S(2)}, u32[]{:S(2)}) collective-permute-start(bf16[1152,128]{1,0:T(8,128)(2,1)S(1)} %collective-permute-done.w2.rest_2_), channel_id=1, source_target_pairs={{4,8},{8,4},{12,16},{16,12},{20,24},{24,20},{28,32},{32,28},{36,40... | collective-permute-start | bytes 884744 | tf_op jit(solution)/shard_map/ppermute | solution.py:35
  13.8 9.7 %collective-permute-start.10 = (bf16[1152,128]{1,0:T(8,128)(2,1)S(1)}, bf16[1152,128]{1,0:T(8,128)(2,1)S(1)}, u32[]{:S(2)}, u32[]{:S(2)}) collective-permute-start(bf16[1152,128]{1,0:T(8,128)(2,1)S(1)} %collective-permute-done.8.rest_8_), channel_id=1, source_target_pairs={{0,1},{1,2},{2,3},{3,0},{4,5},{5,6},{6,7},{7,4},{8,9},{9,10},{10,1... | collective-permute-start | bytes 884744 | tf_op jit(solution)/shard_map/ppermute | solution.py:18
  16.7 8.1 %collective-permute-start.9 = (bf16[1152,128]{1,0:T(8,128)(2,1)S(1)}, bf16[1152,128]{1,0:T(8,128)(2,1)S(1)}, u32[]{:S(2)}, u32[]{:S(2)}) collective-permute-start(bf16[1152,128]{1,0:T(8,128)(2,1)S(1)} %collective-permute-done.8.rest_8_), channel_id=1, source_target_pairs={{0,3},{1,0},{2,1},{3,2},{4,7},{5,4},{6,5},{7,6},{8,11},{9,8},{10,9... | collective-permute-start | bytes 884744 | tf_op jit(solution)/shard_map/ppermute | solution.py:18
  22.3 2.6 %collective-permute-start.4 = (bf16[1152,128]{1,0:T(8,128)(2,1)S(1)}, bf16[1152,128]{1,0:T(8,128)(2,1)S(1)}, u32[]{:S(2)}, u32[]{:S(2)}) collective-permute-start(bf16[1152,128]{1,0:T(8,128)(2,1)S(1)} %shard_map.56.w0.rest_0_), channel_id=1, source_target_pairs={{0,4},{4,0},{8,12},{12,8},{16,20},{20,16},{24,28},{28,24},{32,36},... | collective-permute-start | bytes 884744 | tf_op jit(solution)/shard_map/ppermute | solution.py:23
  22.3 2.6 %collective-permute-start.5 = (bf16[1152,128]{1,0:T(8,128)(2,1)S(1)}, bf16[1152,128]{1,0:T(8,128)(2,1)S(1)}, u32[]{:S(2)}, u32[]{:S(2)}) collective-permute-start(bf16[1152,128]{1,0:T(8,128)(2,1)S(1)} %collective-permute-done.1.w1.rest_1_), channel_id=1, source_target_pairs={{0,4},{4,0},{8,12},{12,8},{16,20},{20,16},{24,28},{28,24},{32,36},... | collective-permute-start | bytes 884744 | tf_op jit(solution)/shard_map/ppermute | solution.py:23
  22.8 2.0 %collective-permute-start.6 = (bf16[1152,128]{1,0:T(8,128)(2,1)S(1)}, bf16[1152,128]{1,0:T(8,128)(2,1)S(1)}, u32[]{:S(2)}, u32[]{:S(2)}) collective-permute-start(bf16[1152,128]{1,0:T(8,128)(2,1)S(1)} %collective-permute-done.w2.rest_2_), channel_id=1, source_target_pairs={{0,4},{4,0},{8,12},{12,8},{16,20},{20,16},{24,28},{28,24},{32,36},... | collective-permute-start | bytes 884744 | tf_op jit(solution)/shard_map/ppermute | solution.py:23
  23.5 1.7 %collective-permute-start.7 = (bf16[1152,128]{1,0:T(8,128)(2,1)S(1)}, bf16[1152,128]{1,0:T(8,128)(2,1)S(1)}, u32[]{:S(2)}, u32[]{:S(2)}) collective-permute-start(bf16[1152,128]{1,0:T(8,128)(2,1)S(1)} %collective-permute-done.2.w3.rest_3_), channel_id=1, source_target_pairs={{0,4},{4,0},{8,12},{12,8},{16,20},{20,16},{24,28},{28,24},{32,36},... | collective-permute-start | bytes 884744 | tf_op jit(solution)/shard_map/ppermute | solution.py:23
  31.3 7.9 %collective-permute-start.11 = (f32[480,96]{1,0:T(8,128)S(1)}, f32[480,96]{1,0:T(8,128)S(1)}, u32[]{:S(2)}, u32[]{:S(2)}) collective-permute-start(f32[480,96]{1,0:T(8,128)S(1)} %get-tuple-element.37), channel_id=1, source_target_pairs={{0,4},{4,0},{8,12},{12,8},{16,20},{20,16},{24,28},{28,24},{32,36},... | collective-permute-start | bytes 552968 | tf_op jit(solution)/shard_map/ppermute | solution.py:23
  31.5 7.6 %collective-permute-start.12 = (bf16[480,96]{1,0:T(8,128)(2,1)S(1)}, bf16[480,96]{1,0:T(8,128)(2,1)S(1)}, u32[]{:S(2)}, u32[]{:S(2)}) collective-permute-start(bf16[480,96]{1,0:T(8,128)(2,1)S(1)} %get-tuple-element.38), channel_id=1, source_target_pairs={{4,8},{8,4},{12,16},{16,12},{20,24},{24,20},{28,32},{32,28},{36,40... | collective-permute-start | bytes 276488 | tf_op jit(solution)/shard_map/ppermute | solution.py:35
  39.2 4.1 %collective-permute-start.13 = (bf16[176,96]{1,0:T(8,128)(2,1)S(1)}, bf16[176,96]{1,0:T(8,128)(2,1)S(1)}, u32[]{:S(2)}, u32[]{:S(2)}) collective-permute-start(bf16[176,96]{1,0:T(8,128)(2,1)S(1)} %get-tuple-element.40), channel_id=1, source_target_pairs={{0,1},{1,2},{2,3},{3,0},{4,5},{5,6},{6,7},{7,4},{8,9},{9,10},{10,1... | collective-permute-start | bytes 101384 | tf_op jit(solution)/shard_map/ppermute | solution.py:18
  40.8 5.6 %collective-permute-start.14 = (bf16[176,96]{1,0:T(8,128)(2,1)S(1)}, bf16[176,96]{1,0:T(8,128)(2,1)S(1)}, u32[]{:S(2)}, u32[]{:S(2)}) collective-permute-start(bf16[176,96]{1,0:T(8,128)(2,1)S(1)} %get-tuple-element.41), channel_id=1, source_target_pairs={{0,2},{1,3},{2,0},{3,1},{4,6},{5,7},{6,4},{7,5},{8,10},{9,11},{10,... | collective-permute-start | bytes 101384 | tf_op jit(solution)/shard_map/ppermute | solution.py:18
  43.0 5.3 %collective-permute-start.15 = (bf16[176,96]{1,0:T(8,128)(2,1)S(1)}, bf16[176,96]{1,0:T(8,128)(2,1)S(1)}, u32[]{:S(2)}, u32[]{:S(2)}) collective-permute-start(bf16[176,96]{1,0:T(8,128)(2,1)S(1)} %get-tuple-element.42), channel_id=1, source_target_pairs={{0,3},{1,0},{2,1},{3,2},{4,7},{5,4},{6,5},{7,6},{8,11},{9,8},{10,9... | collective-permute-start | bytes 101384 | tf_op jit(solution)/shard_map/ppermute | solution.py:18

commit v6 on v5

--- a/solution.py
+++ b/solution.py
@@ -140,7 +140,7 @@
     ]
     for cp in copies:
         cp.start()
-    zeros = jnp.zeros((dofs, 2 * LANES - dofs), BF)
+    low_lanes = (lax.broadcasted_iota(I32, (1, LANES), 1) < LANES // 2).astype(I32)
     odd = row % 2
     for cp in copies:
         cp.wait()
@@ -160,17 +160,13 @@
             wbuf[pl.ds(pl.multiple_of(place + d * quarter + (blocks + jh) * rows, 16), rows), :]
             for d in range(PARTS)
         ]
+        keep = jnp.where((low_lanes == 1) == (jl < half), 1.0, 0.0).astype(BF)
         pj = jnp.concatenate(
-            [jnp.concatenate(first, axis=0), jnp.concatenate(second, axis=0)], axis=1
+            [jnp.concatenate(first, axis=0), jnp.concatenate(second, axis=0) * keep], axis=1
         )
         s = s_ref[i, k]
         tail = s[:, LANES:]
-        tail = jnp.where(
-            jl < half,
-            jnp.concatenate([tail, zeros], axis=1),
-            jnp.concatenate([zeros, tail], axis=1),
-        )
-        return dot(pj, jnp.concatenate([s[:, :LANES], tail], axis=1), True)
+        return dot(pj, jnp.concatenate([s[:, :LANES], tail, tail], axis=1), True)
 
     for i in range(blocks):
         parts = [image(i, k) for k in range(slots)]

time: 49.4 us -> 49.5 us (level)
  no operation moved by 1% of the time
where the time goes in v6:
time: 49.5 us; the launch traced here: 49 us
  waiting for transfers between devices  20.8 us (42%)
  starting transfers between devices  15 us (30%)
  Pallas kernels  11.5 us (23%)
  local copies, waits for them, and re-layouts  1 us (2%)
  other arithmetic  0.66 us (1%)
    ppermute x3, waiting for transfers between devices, swap_cross(): return lax.ppermute(x, ('rows', 'cols'), pairs)  10.6 us
    ppermute x8, starting transfers between devices, around(): lax.ppermute(x, 'cols', [(i, (i + by) % length) for i in range(length)])  10.3 us
    ppermute x8, waiting for transfers between devices, around(): lax.ppermute(x, 'cols', [(i, (i + by) % length) for i in range(length)])  9.85 us
    pallas_call x1, Pallas kernels, on_device(): pl.pallas_call(main_kernel, out_shape=[out, out, jax.ShapeDtypeStruct(out...  6.16 us
    ppermute x3, starting transfers between devices, swap_cross(): return lax.ppermute(x, ('rows', 'cols'), pairs)  3.94 us
    pallas_call x1, Pallas kernels, on_device(): pl.pallas_call(table_kernel, out_shape=[pltpu.VMEM(stiffness.shape, BF),...  3.92 us
    unnamed x6, local copies, waits for them, and re-layouts  1 us
  transfers between devices with their start and end apart: 16, of which 10 were waited for; matrix products, arithmetic and copies ran while one was open for 0% of the time, Pallas kernels for 10%

profile of v6, /device:TPU:134, one launch (start us, length us, event | category | flops | bytes accessed | tf_op | source)
XLA Modules:
  0.0 49.0 jit_solution(18348993922327901504)
XLA Ops:
  0.0 1.0 %copy-done = bf16[16,48,192]{2,1,0:T(8,128)(2,1)S(1)} copy-done((bf16[16,48,192]{2,1,0:T(8,128)(2,1)S(1)}, bf16[16,48,192]{2,1,0:T(8,128)(2,1)}, u32[]{:S(2)}) %copy-start) | copy-done | bytes 294936
  1.0 0.4 shard_map.56.w0.rest_0_
  1.4 1.5 %collective-permute-start = (bf16[1152,128]{1,0:T(8,128)(2,1)S(1)}, bf16[1152,128]{1,0:T(8,128)(2,1)S(1)}, u32[]{:S(2)}, u32[]{:S(2)}) collective-permute-start(bf16[1152,128]{1,0:T(8,128)(2,1)S(1)} %shard_map.56.w0.rest_0_), channel_id=1, source_target_pairs={{0,2},{1,3},{2,0},{3,1},{4,6},{5,7},{6,4},{7,5},{8,10},{9,11},{10,... | collective-permute-start | bytes 884744 | tf_op jit(solution)/shard_map/ppermute | solution.py:18
  2.9 1.7 %collective-permute-start.8 = (bf16[1152,128]{1,0:T(8,128)(2,1)S(1)}, bf16[1152,128]{1,0:T(8,128)(2,1)S(1)}, u32[]{:S(2)}, u32[]{:S(2)}) collective-permute-start(bf16[1152,128]{1,0:T(8,128)(2,1)S(1)} %shard_map.56.w0.rest_0_), channel_id=1, source_target_pairs={{4,8},{8,4},{12,16},{16,12},{20,24},{24,20},{28,32},{32,28},{36,40... | collective-permute-start | bytes 884744 | tf_op jit(solution)/shard_map/ppermute | solution.py:35
  4.6 2.1 %collective-permute-start.2 = (bf16[1152,128]{1,0:T(8,128)(2,1)S(1)}, bf16[1152,128]{1,0:T(8,128)(2,1)S(1)}, u32[]{:S(2)}, u32[]{:S(2)}) collective-permute-start(bf16[1152,128]{1,0:T(8,128)(2,1)S(1)} %shard_map.56.w0.rest_0_), channel_id=1, source_target_pairs={{0,1},{1,2},{2,3},{3,0},{4,5},{5,6},{6,7},{7,4},{8,9},{9,10},{10,1... | collective-permute-start | bytes 884744 | tf_op jit(solution)/shard_map/ppermute | solution.py:18
  6.7 3.9 %shard_map.55 = (bf16[16,4,192,192]{3,2,1,0:T(8,128)(2,1)S(1)}, s32[16,128]{1,0:T(8,128)S(1)}, s32[16,192]{1,0:T(8,128)S(1)}) custom-call(s32[4,16]{1,0:T(4,128)} %bitcast.4, s32[32,1024]{1,0:T(8,128)} %bitcast.6, bf16[16,4,192,192]{3,2,1,0:T(8,128)(2,1)} %s_hbm.1), custom_call_target="tpu_custom_call" | custom-call | tf_op jit(solution)/shard_map/pallas_call | solution.py:269
  10.6 2.3 %collective-permute-done.w2.rest_2_ = bf16[1152,128]{1,0:T(8,128)(2,1)S(1)} collective-permute-done((bf16[1152,128]{1,0:T(8,128)(2,1)S(1)}, bf16[1152,128]{1,0:T(8,128)(2,1)S(1)}, u32[]{:S(2)}, u32[]{:S(2)}) %collective-permute-start) | collective-permute-done | bytes 294944 | tf_op jit(solution)/shard_map/ppermute | solution.py:18
  12.9 0.9 %collective-permute-start.3 = (bf16[1152,128]{1,0:T(8,128)(2,1)S(1)}, bf16[1152,128]{1,0:T(8,128)(2,1)S(1)}, u32[]{:S(2)}, u32[]{:S(2)}) collective-permute-start(bf16[1152,128]{1,0:T(8,128)(2,1)S(1)} %collective-permute-done.w2.rest_2_), channel_id=1, source_target_pairs={{4,8},{8,4},{12,16},{16,12},{20,24},{24,20},{28,32},{32,28},{36,40... | collective-permute-start | bytes 884744 | tf_op jit(solution)/shard_map/ppermute | solution.py:35
  13.8 3.0 %collective-permute-start.10 = (bf16[1152,128]{1,0:T(8,128)(2,1)S(1)}, bf16[1152,128]{1,0:T(8,128)(2,1)S(1)}, u32[]{:S(2)}, u32[]{:S(2)}) collective-permute-start(bf16[1152,128]{1,0:T(8,128)(2,1)S(1)} %collective-permute-done.8.rest_8_), channel_id=1, source_target_pairs={{0,1},{1,2},{2,3},{3,0},{4,5},{5,6},{6,7},{7,4},{8,9},{9,10},{10,1... | collective-permute-start | bytes 884744 | tf_op jit(solution)/shard_map/ppermute | solution.py:18
  16.7 1.3 %collective-permute-done.1.w1.rest_1_ = bf16[1152,128]{1,0:T(8,128)(2,1)S(1)} collective-permute-done((bf16[1152,128]{1,0:T(8,128)(2,1)S(1)}, bf16[1152,128]{1,0:T(8,128)(2,1)S(1)}, u32[]{:S(2)}, u32[]{:S(2)}) %collective-permute-start.1) | collective-permute-done | bytes 294944 | tf_op jit(solution)/shard_map/ppermute | solution.py:18
  18.0 4.3 %collective-permute-done.3.rest_10_ = bf16[1152,128]{1,0:T(8,128)(2,1)S(1)} collective-permute-done((bf16[1152,128]{1,0:T(8,128)(2,1)S(1)}, bf16[1152,128]{1,0:T(8,128)(2,1)S(1)}, u32[]{:S(2)}, u32[]{:S(2)}) %collective-permute-start.3) | collective-permute-done | bytes 294944 | tf_op jit(solution)/shard_map/ppermute | solution.py:35
  22.3 0.5 %collective-permute-start.5 = (bf16[1152,128]{1,0:T(8,128)(2,1)S(1)}, bf16[1152,128]{1,0:T(8,128)(2,1)S(1)}, u32[]{:S(2)}, u32[]{:S(2)}) collective-permute-start(bf16[1152,128]{1,0:T(8,128)(2,1)S(1)} %collective-permute-done.1.w1.rest_1_), channel_id=1, source_target_pairs={{0,4},{4,0},{8,12},{12,8},{16,20},{20,16},{24,28},{28,24},{32,36},... | collective-permute-start | bytes 884744 | tf_op jit(solution)/shard_map/ppermute | solution.py:23
  22.9 0.6 %collective-permute-done.10.rest_11_ = bf16[1152,128]{1,0:T(8,128)(2,1)S(1)} collective-permute-done((bf16[1152,128]{1,0:T(8,128)(2,1)S(1)}, bf16[1152,128]{1,0:T(8,128)(2,1)S(1)}, u32[]{:S(2)}, u32[]{:S(2)}) %collective-permute-start.10) | collective-permute-done | bytes 294944 | tf_op jit(solution)/shard_map/ppermute | solution.py:18
  23.5 1.0 %shard_map.57 = (bf16[384,2048]{1,0:T(8,128)(2,1)S(1)}, bf16[384,1024]{1,0:T(8,128)(2,1)S(1)}) custom-call(s32[16,192]{1,0:T(8,128)S(1)} %get-tuple-element.26.aggl_ref, bf16[1152,128]{1,0:T(8,128)(2,1)S(1)} %shard_map.56.w0.rest_0_, bf16[1152,128]{1,0:T(8,128)(2,1)S(1)} %collective-permute-done.1.w1.rest_1_, ...), custom_call_target="tpu_custom_call" | custom-call | tf_op jit(solution)/shard_map/pallas_call | solution.py:292
  24.5 0.4 collective-permute-done.9.rest_9_
  25.2 6.2 %shard_map.58 = (f32[480,96]{1,0:T(8,128)S(1)}, f32[480,96]{1,0:T(8,128)S(1)}, bf16[480,96]{1,0:T(8,128)(2,1)S(1)}) custom-call(s32[4,16]{1,0:T(4,128)S(1)} %bitcast.5, s32[16]{0:T(128)S(1)} %copy-done.2, s32[16,128]{1,0:T(8,128)S(1)} %get-tuple-element.24.aggr_ref, bf16[384,2048]{1,0:T(8,128)(2,1)S(1)} %get-tuple-element.28.lo_ref, ...), custom_call_target="tpu_custom_call" | custom-call | tf_op jit(solution)/shard_map/pallas_call | solution.py:305
  31.6 1.3 %collective-permute-start.12 = (bf16[480,96]{1,0:T(8,128)(2,1)S(1)}, bf16[480,96]{1,0:T(8,128)(2,1)S(1)}, u32[]{:S(2)}, u32[]{:S(2)}) collective-permute-start(bf16[480,96]{1,0:T(8,128)(2,1)S(1)} %get-tuple-element.38), channel_id=1, source_target_pairs={{4,8},{8,4},{12,16},{16,12},{20,24},{24,20},{28,32},{32,28},{36,40... | collective-permute-start | bytes 276488 | tf_op jit(solution)/shard_map/ppermute | solution.py:35
  32.9 6.3 %collective-permute-done.12.cross_ref = bf16[480,96]{1,0:T(8,128)(2,1)S(1)} collective-permute-done((bf16[480,96]{1,0:T(8,128)(2,1)S(1)}, bf16[480,96]{1,0:T(8,128)(2,1)S(1)}, u32[]{:S(2)}, u32[]{:S(2)}) %collective-permute-start.12) | collective-permute-done | bytes 92192 | tf_op jit(solution)/shard_map/ppermute | solution.py:35
  39.3 1.6 %collective-permute-start.13 = (bf16[176,96]{1,0:T(8,128)(2,1)S(1)}, bf16[176,96]{1,0:T(8,128)(2,1)S(1)}, u32[]{:S(2)}, u32[]{:S(2)}) collective-permute-start(bf16[176,96]{1,0:T(8,128)(2,1)S(1)} %get-tuple-element.40), channel_id=1, source_target_pairs={{0,1},{1,2},{2,3},{3,0},{4,5},{5,6},{6,7},{7,4},{8,9},{9,10},{10,1... | collective-permute-start | bytes 101384 | tf_op jit(solution)/shard_map/ppermute | solution.py:18
  41.0 2.1 %collective-permute-start.14 = (bf16[176,96]{1,0:T(8,128)(2,1)S(1)}, bf16[176,96]{1,0:T(8,128)(2,1)S(1)}, u32[]{:S(2)}, u32[]{:S(2)}) collective-permute-start(bf16[176,96]{1,0:T(8,128)(2,1)S(1)} %get-tuple-element.41), channel_id=1, source_target_pairs={{0,2},{1,3},{2,0},{3,1},{4,6},{5,7},{6,4},{7,5},{8,10},{9,11},{10,... | collective-permute-start | bytes 101384 | tf_op jit(solution)/shard_map/ppermute | solution.py:18
  43.0 0.4 collective-permute-done.13
  43.4 3.1 %collective-permute-done.14 = bf16[176,96]{1,0:T(8,128)(2,1)S(1)} collective-permute-done((bf16[176,96]{1,0:T(8,128)(2,1)S(1)}, bf16[176,96]{1,0:T(8,128)(2,1)S(1)}, u32[]{:S(2)}, u32[]{:S(2)}) %collective-permute-start.14) | collective-permute-done | bytes 33824 | tf_op jit(solution)/shard_map/ppermute | solution.py:18
  46.5 1.8 %collective-permute-done.15 = bf16[176,96]{1,0:T(8,128)(2,1)S(1)} collective-permute-done((bf16[176,96]{1,0:T(8,128)(2,1)S(1)}, bf16[176,96]{1,0:T(8,128)(2,1)S(1)}, u32[]{:S(2)}, u32[]{:S(2)}) %collective-permute-start.15) | collective-permute-done | bytes 33824 | tf_op jit(solution)/shard_map/ppermute | solution.py:18
  48.3 0.7 %add_bitcast_fusion = f32[96,168]{0,1:T(8,128)} fusion(f32[168,96]{1,0:T(8,128)S(1)} %get-tuple-element.39, bf16[176,96]{1,0:T(8,128)(2,1)S(1)} %collective-permute-done.15, bf16[176,96]{1,0:T(8,128)(2,1)S(1)} %collective-permute-done.14, bf16[176,96]{1,0:T(8,128)(2,1)S(1)} %collective-permute-done.13), kind=kLoop, calls=%fused_computation | loop fusion | flops 96768 | bytes 225792 | tf_op jit(solution)/shard_map/transpose | solution.py:336
  (20 shorter events, 0.6 us)
Async XLA Ops:
  0.0 1.0 %copy-start = (bf16[16,48,192]{2,1,0:T(8,128)(2,1)S(1)}, bf16[16,48,192]{2,1,0:T(8,128)(2,1)}, u32[]{:S(2)}) copy-start(bf16[16,48,192]{2,1,0:T(8,128)(2,1)} %q_ref.1) | copy-start | bytes 884740
  1.0 24.2 %copy-start.1 = (s32[16,4]{0,1:T(4,128)S(1)}, s32[16,4]{0,1:T(4,128)}, u32[]{:S(2)}) copy-start(s32[16,4]{0,1:T(4,128)} %param.6) | copy-start | bytes 772
  1.0 24.2 %copy-start.2 = (s32[16]{0:T(128)S(1)}, s32[16]{0:T(128)}, u32[]{:S(2)}) copy-start(s32[16]{0:T(128)} %live_ref.1) | copy-start | bytes 196
  1.4 11.5 %collective-permute-start = (bf16[1152,128]{1,0:T(8,128)(2,1)S(1)}, bf16[1152,128]{1,0:T(8,128)(2,1)S(1)}, u32[]{:S(2)}, u32[]{:S(2)}) collective-permute-start(bf16[1152,128]{1,0:T(8,128)(2,1)S(1)} %shard_map.56.w0.rest_0_), channel_id=1, source_target_pairs={{0,2},{1,3},{2,0},{3,1},{4,6},{5,7},{6,4},{7,5},{8,10},{9,11},{10,... | collective-permute-start | bytes 884744 | tf_op jit(solution)/shard_map/ppermute | solution.py:18
  2.9 10.9 %collective-permute-start.8 = (bf16[1152,128]{1,0:T(8,128)(2,1)S(1)}, bf16[1152,128]{1,0:T(8,128)(2,1)S(1)}, u32[]{:S(2)}, u32[]{:S(2)}) collective-permute-start(bf16[1152,128]{1,0:T(8,128)(2,1)S(1)} %shard_map.56.w0.rest_0_), channel_id=1, source_target_pairs={{4,8},{8,4},{12,16},{16,12},{20,24},{24,20},{28,32},{32,28},{36,40... | collective-permute-start | bytes 884744 | tf_op jit(solution)/shard_map/ppermute | solution.py:35
  4.6 12.2 %collective-permute-start.2 = (bf16[1152,128]{1,0:T(8,128)(2,1)S(1)}, bf16[1152,128]{1,0:T(8,128)(2,1)S(1)}, u32[]{:S(2)}, u32[]{:S(2)}) collective-permute-start(bf16[1152,128]{1,0:T(8,128)(2,1)S(1)} %shard_map.56.w0.rest_0_), channel_id=1, source_target_pairs={{0,1},{1,2},{2,3},{3,0},{4,5},{5,6},{6,7},{7,4},{8,9},{9,10},{10,1... | collective-permute-start | bytes 884744 | tf_op jit(solution)/shard_map/ppermute | solution.py:18
  6.7 11.4 %collective-permute-start.1 = (bf16[1152,128]{1,0:T(8,128)(2,1)S(1)}, bf16[1152,128]{1,0:T(8,128)(2,1)S(1)}, u32[]{:S(2)}, u32[]{:S(2)}) collective-permute-start(bf16[1152,128]{1,0:T(8,128)(2,1)S(1)} %shard_map.56.w0.rest_0_), channel_id=1, source_target_pairs={{0,3},{1,0},{2,1},{3,2},{4,7},{5,4},{6,5},{7,6},{8,11},{9,8},{10,9... | collective-permute-start | bytes 884744 | tf_op jit(solution)/shard_map/ppermute | solution.py:18
  12.9 9.5 %collective-permute-start.3 = (bf16[1152,128]{1,0:T(8,128)(2,1)S(1)}, bf16[1152,128]{1,0:T(8,128)(2,1)S(1)}, u32[]{:S(2)}, u32[]{:S(2)}) collective-permute-start(bf16[1152,128]{1,0:T(8,128)(2,1)S(1)} %collective-permute-done.w2.rest_2_), channel_id=1, source_target_pairs={{4,8},{8,4},{12,16},{16,12},{20,24},{24,20},{28,32},{32,28},{36,40... | collective-permute-start | bytes 884744 | tf_op jit(solution)/shard_map/ppermute | solution.py:35
  13.8 9.7 %collective-permute-start.10 = (bf16[1152,128]{1,0:T(8,128)(2,1)S(1)}, bf16[1152,128]{1,0:T(8,128)(2,1)S(1)}, u32[]{:S(2)}, u32[]{:S(2)}) collective-permute-start(bf16[1152,128]{1,0:T(8,128)(2,1)S(1)} %collective-permute-done.8.rest_8_), channel_id=1, source_target_pairs={{0,1},{1,2},{2,3},{3,0},{4,5},{5,6},{6,7},{7,4},{8,9},{9,10},{10,1... | collective-permute-start | bytes 884744 | tf_op jit(solution)/shard_map/ppermute | solution.py:18
  16.7 8.1 %collective-permute-start.9 = (bf16[1152,128]{1,0:T(8,128)(2,1)S(1)}, bf16[1152,128]{1,0:T(8,128)(2,1)S(1)}, u32[]{:S(2)}, u32[]{:S(2)}) collective-permute-start(bf16[1152,128]{1,0:T(8,128)(2,1)S(1)} %collective-permute-done.8.rest_8_), channel_id=1, source_target_pairs={{0,3},{1,0},{2,1},{3,2},{4,7},{5,4},{6,5},{7,6},{8,11},{9,8},{10,9... | collective-permute-start | bytes 884744 | tf_op jit(solution)/shard_map/ppermute | solution.py:18
  22.3 2.6 %collective-permute-start.4 = (bf16[1152,128]{1,0:T(8,128)(2,1)S(1)}, bf16[1152,128]{1,0:T(8,128)(2,1)S(1)}, u32[]{:S(2)}, u32[]{:S(2)}) collective-permute-start(bf16[1152,128]{1,0:T(8,128)(2,1)S(1)} %shard_map.56.w0.rest_0_), channel_id=1, source_target_pairs={{0,4},{4,0},{8,12},{12,8},{16,20},{20,16},{24,28},{28,24},{32,36},... | collective-permute-start | bytes 884744 | tf_op jit(solution)/shard_map/ppermute | solution.py:23
  22.3 2.6 %collective-permute-start.5 = (bf16[1152,128]{1,0:T(8,128)(2,1)S(1)}, bf16[1152,128]{1,0:T(8,128)(2,1)S(1)}, u32[]{:S(2)}, u32[]{:S(2)}) collective-permute-start(bf16[1152,128]{1,0:T(8,128)(2,1)S(1)} %collective-permute-done.1.w1.rest_1_), channel_id=1, source_target_pairs={{0,4},{4,0},{8,12},{12,8},{16,20},{20,16},{24,28},{28,24},{32,36},... | collective-permute-start | bytes 884744 | tf_op jit(solution)/shard_map/ppermute | solution.py:23
  22.8 2.0 %collective-permute-start.6 = (bf16[1152,128]{1,0:T(8,128)(2,1)S(1)}, bf16[1152,128]{1,0:T(8,128)(2,1)S(1)}, u32[]{:S(2)}, u32[]{:S(2)}) collective-permute-start(bf16[1152,128]{1,0:T(8,128)(2,1)S(1)} %collective-permute-done.w2.rest_2_), channel_id=1, source_target_pairs={{0,4},{4,0},{8,12},{12,8},{16,20},{20,16},{24,28},{28,24},{32,36},... | collective-permute-start | bytes 884744 | tf_op jit(solution)/shard_map/ppermute | solution.py:23
  23.5 1.7 %collective-permute-start.7 = (bf16[1152,128]{1,0:T(8,128)(2,1)S(1)}, bf16[1152,128]{1,0:T(8,128)(2,1)S(1)}, u32[]{:S(2)}, u32[]{:S(2)}) collective-permute-start(bf16[1152,128]{1,0:T(8,128)(2,1)S(1)} %collective-permute-done.2.w3.rest_3_), channel_id=1, source_target_pairs={{0,4},{4,0},{8,12},{12,8},{16,20},{20,16},{24,28},{28,24},{32,36},... | collective-permute-start | bytes 884744 | tf_op jit(solution)/shard_map/ppermute | solution.py:23
  31.4 7.9 %collective-permute-start.11 = (f32[480,96]{1,0:T(8,128)S(1)}, f32[480,96]{1,0:T(8,128)S(1)}, u32[]{:S(2)}, u32[]{:S(2)}) collective-permute-start(f32[480,96]{1,0:T(8,128)S(1)} %get-tuple-element.37), channel_id=1, source_target_pairs={{0,4},{4,0},{8,12},{12,8},{16,20},{20,16},{24,28},{28,24},{32,36},... | collective-permute-start | bytes 552968 | tf_op jit(solution)/shard_map/ppermute | solution.py:23
  31.6 7.6 %collective-permute-start.12 = (bf16[480,96]{1,0:T(8,128)(2,1)S(1)}, bf16[480,96]{1,0:T(8,128)(2,1)S(1)}, u32[]{:S(2)}, u32[]{:S(2)}) collective-permute-start(bf16[480,96]{1,0:T(8,128)(2,1)S(1)} %get-tuple-element.38), channel_id=1, source_target_pairs={{4,8},{8,4},{12,16},{16,12},{20,24},{24,20},{28,32},{32,28},{36,40... | collective-permute-start | bytes 276488 | tf_op jit(solution)/shard_map/ppermute | solution.py:35
  39.3 4.1 %collective-permute-start.13 = (bf16[176,96]{1,0:T(8,128)(2,1)S(1)}, bf16[176,96]{1,0:T(8,128)(2,1)S(1)}, u32[]{:S(2)}, u32[]{:S(2)}) collective-permute-start(bf16[176,96]{1,0:T(8,128)(2,1)S(1)} %get-tuple-element.40), channel_id=1, source_target_pairs={{0,1},{1,2},{2,3},{3,0},{4,5},{5,6},{6,7},{7,4},{8,9},{9,10},{10,1... | collective-permute-start | bytes 101384 | tf_op jit(solution)/shard_map/ppermute | solution.py:18
  41.0 5.6 %collective-permute-start.14 = (bf16[176,96]{1,0:T(8,128)(2,1)S(1)}, bf16[176,96]{1,0:T(8,128)(2,1)S(1)}, u32[]{:S(2)}, u32[]{:S(2)}) collective-permute-start(bf16[176,96]{1,0:T(8,128)(2,1)S(1)} %get-tuple-element.41), channel_id=1, source_target_pairs={{0,2},{1,3},{2,0},{3,1},{4,6},{5,7},{6,4},{7,5},{8,10},{9,11},{10,... | collective-permute-start | bytes 101384 | tf_op jit(solution)/shard_map/ppermute | solution.py:18
  43.0 5.3 %collective-permute-start.15 = (bf16[176,96]{1,0:T(8,128)(2,1)S(1)}, bf16[176,96]{1,0:T(8,128)(2,1)S(1)}, u32[]{:S(2)}, u32[]{:S(2)}) collective-permute-start(bf16[176,96]{1,0:T(8,128)(2,1)S(1)} %get-tuple-element.42), channel_id=1, source_target_pairs={{0,3},{1,0},{2,1},{3,2},{4,7},{5,4},{6,5},{7,6},{8,11},{9,8},{10,9... | collective-permute-start | bytes 101384 | tf_op jit(solution)/shard_map/ppermute | solution.py:18
